TPU v7x, 32 devices: a whole 2x2x4 slice. The times are simulated.
32 devices in a mesh: section: 2 (over core), dp: 4 (over y, x), tensor: 4 (over z).
Axes of the slice: x: 2, y: 2, z: 4, core: 2. Of those that a mesh axis runs over, the one named last changes fastest.
Arguments:
- tokens_in: bfloat16 [2, 1536, 2048], P(None, ('dp', 'tensor')), may hold values from -6 to 6
- cotangent: bfloat16 [2, 1536, 2048], P(None, ('dp', 'tensor')), may hold values from -6 to 6
- lengths: int32 [2, 4, 2], P(None, 'dp'), may hold values from 1 to 288, 384 in all within a row
- attn_gain: bfloat16 [2, 2048], P('section', 'dp'), may hold values from 0.5 to 1.5
- w_query: bfloat16 [2, 2048, 2048], P('section', 'dp', 'tensor'), may hold values from -0.125 to 0.125
- w_key: bfloat16 [2, 2048, 256], P('section', 'dp', 'tensor'), may hold values from -0.125 to 0.125
- w_value: bfloat16 [2, 2048, 256], P('section', 'dp', 'tensor'), may hold values from -0.125 to 0.125
- w_out: bfloat16 [2, 2048, 2048], P('section', 'tensor', 'dp'), may hold values from -1 to 1
- ffn_gain: bfloat16 [2, 2048], P('section', 'dp'), may hold values from 0.5 to 1.5
- w_gate: bfloat16 [2, 2048, 5632], P('section', 'dp', 'tensor'), may hold values from -0.125 to 0.125
- w_up: bfloat16 [2, 2048, 5632], P('section', 'dp', 'tensor'), may hold values from -0.125 to 0.125
- w_down: bfloat16 [2, 5632, 2048], P('section', 'tensor', 'dp'), may hold values from -0.078125 to 0.078125
Outputs:
- section_out: bfloat16 [2, 2, 1536, 2048], P('section', None, ('dp', 'tensor'))
- input_grad: bfloat16 [2, 2, 1536, 2048], P('section', None, ('dp', 'tensor'))
- grad_attn_gain: float32 [2, 2048], P('section', ('dp', 'tensor'))
- grad_query: float32 [2, 2048, 2048], P('section', 'dp', 'tensor')
- grad_key: float32 [2, 2048, 256], P('section', 'dp', 'tensor')
- grad_value: float32 [2, 2048, 256], P('section', 'dp', 'tensor')
- grad_out: float32 [2, 2048, 2048], P('section', 'tensor', 'dp')
- grad_ffn_gain: float32 [2, 2048], P('section', ('dp', 'tensor'))
- grad_gate: float32 [2, 2048, 5632], P('section', 'dp', 'tensor')
- grad_up: float32 [2, 2048, 5632], P('section', 'dp', 'tensor')
- grad_down: float32 [2, 5632, 2048], P('section', 'tensor', 'dp')
Inputs may be any that keep to these rules, and one draw needn't show every extreme that they name: lengths[m, g, :] are the lengths of the sequences that fill the 384 rows of group g in micro-batch m, in order, summing to 384; each such row of lengths holds two sequences of 96 to 288 rows each.
All inputs are finite; a program needn't handle non-finite values.
Results may differ from a plain program's by a relative error of at most 0.03.
Values may be sent and summed in bfloat16 or wider, within the bound.
No kernel may reach another device: no remote copies, remote signals or barrier semaphores. Data moves between devices by JAX's collectives and lax.ppermute only.
A program may use at most 192 MiB of HBM per device.

v0:
```python
import jax
import jax.numpy as jnp
from jax import lax
from jax.sharding import PartitionSpec as P

HEAD = 64


EPSILON = 1e-05
MASK_FILL = -1e30


def from_behind(value, axis, steps):
    count = lax.axis_size(axis)
    leading, last = (max(0, -steps), min(count, count - steps))
    return lax.ppermute(value, axis, [(source, source + steps) for source in range(leading, last)])


def contract(left, right, left_dim, right_dim):
    return lax.dot_general(
        left, right, (((left_dim,), (right_dim,)), ((), ())), preferred_element_type=jnp.float32
    )


def sequence_layout(seq_lens, group):
    row_ids = jnp.arange(group, dtype=jnp.int32)
    ends = jnp.cumsum(seq_lens)
    starts = ends - seq_lens
    member = jnp.sum((row_ids[:, None] >= ends[None, :]).astype(jnp.int32), axis=1)
    slots = jnp.arange(seq_lens.shape[0], dtype=jnp.int32)
    begins = jnp.sum(jnp.where(member[:, None] == slots[None, :], starts[None, :], 0), axis=1)
    return (member, row_ids - begins)


def rotary_tables(position, head_size):
    half_dim = head_size // 2
    frequency = 10000.0 ** (-jnp.arange(half_dim, dtype=jnp.float32) / half_dim)
    angle_table = position.astype(jnp.float32)[:, None] * frequency[None, :]
    return (jnp.cos(angle_table), jnp.sin(angle_table))


def rotate(tensor, cosine, sine_part):
    half_dim = tensor.shape[-1] // 2
    front = tensor[..., :half_dim]
    back_half = tensor[..., half_dim:]
    return jnp.concatenate(
        [front * cosine - back_half * sine_part, back_half * cosine + front * sine_part], axis=-1
    )


def unrotate(tensor, cosine, sine_part):
    half_dim = tensor.shape[-1] // 2
    front = tensor[..., :half_dim]
    back_half = tensor[..., half_dim:]
    return jnp.concatenate(
        [front * cosine + back_half * sine_part, back_half * cosine - front * sine_part], axis=-1
    )


def geometry(seq_lens, group):
    member, position = sequence_layout(seq_lens, group)
    cosine, sine_part = rotary_tables(position, HEAD)
    row_ids = jnp.arange(group, dtype=jnp.int32)
    allowed = (member[:, None] == member[None, :]) & (row_ids[:, None] >= row_ids[None, :])
    return (cosine, sine_part, allowed)


def spread(local_block):
    return lax.all_gather(local_block, "tensor", axis=0, tiled=True)


def collect(term_fn, local_rows):
    return lax.psum_scatter(
        term_fn(jnp.int32(0), local_rows * lax.axis_size("tensor")).astype(jnp.bfloat16),
        "tensor",
        scatter_dimension=0,
        tiled=True,
    ).astype(jnp.float32)


def spread_grad(local_block):
    return lax.all_gather(local_block, "tensor", axis=0, tiled=True)


def collect_grad(term_fn, local_rows):
    return lax.psum_scatter(
        term_fn(jnp.int32(0), local_rows * lax.axis_size("tensor")).astype(jnp.bfloat16),
        "tensor",
        scatter_dimension=0,
        tiled=True,
    ).astype(jnp.float32)


def gather_weights(local_params):
    return (
        lax.all_gather(local_params[0], "dp", axis=0, tiled=True),
        lax.all_gather(local_params[1], "dp", axis=0, tiled=True),
        lax.all_gather(local_params[2], "dp", axis=0, tiled=True),
        lax.all_gather(local_params[3], "dp", axis=0, tiled=True),
        lax.all_gather(local_params[4], "dp", axis=1, tiled=True),
        lax.all_gather(local_params[5], "dp", axis=0, tiled=True),
        lax.all_gather(local_params[6], "dp", axis=0, tiled=True),
        lax.all_gather(local_params[7], "dp", axis=0, tiled=True),
        lax.all_gather(local_params[8], "dp", axis=1, tiled=True),
    )


def gather_weights_again(local_params):
    return (
        lax.all_gather(local_params[0], "dp", axis=0, tiled=True),
        lax.all_gather(local_params[1], "dp", axis=0, tiled=True),
        lax.all_gather(local_params[2], "dp", axis=0, tiled=True),
        lax.all_gather(local_params[3], "dp", axis=0, tiled=True),
        lax.all_gather(local_params[4], "dp", axis=1, tiled=True),
        lax.all_gather(local_params[5], "dp", axis=0, tiled=True),
        lax.all_gather(local_params[6], "dp", axis=0, tiled=True),
        lax.all_gather(local_params[7], "dp", axis=0, tiled=True),
        lax.all_gather(local_params[8], "dp", axis=1, tiled=True),
    )


def forward(layer_in, seq_lens, weights):
    norm_gain, w_query, w_key, w_value, w_out, ffn_gain, w_gate, w_up, w_down = weights
    local_rows = layer_in.shape[0]
    group = local_rows * lax.axis_size("tensor")
    inverse_one = lax.rsqrt(jnp.mean(layer_in * layer_in, axis=1, keepdims=True) + EPSILON)
    normed_one = spread(
        (layer_in * inverse_one * norm_gain.astype(jnp.float32)).astype(jnp.bfloat16)
    )
    cosine, sine_part, allowed = geometry(seq_lens, group)
    kv_count = w_key.shape[1] // HEAD
    repeats = w_query.shape[1] // w_key.shape[1]
    queries = jnp.dot(normed_one, w_query, preferred_element_type=jnp.float32).reshape(
        group, kv_count, repeats, HEAD
    )
    queries = rotate(queries, cosine[:, None, None, :], sine_part[:, None, None, :]).astype(
        jnp.bfloat16
    )
    key_rot = jnp.dot(normed_one, w_key, preferred_element_type=jnp.float32).reshape(
        group, kv_count, HEAD
    )
    key_rot = rotate(key_rot, cosine[:, None, :], sine_part[:, None, :]).astype(jnp.bfloat16)
    values = (
        jnp.dot(normed_one, w_value, preferred_element_type=jnp.float32)
        .reshape(group, kv_count, HEAD)
        .astype(jnp.bfloat16)
    )
    scores = jnp.einsum(
        "qgrd,kgd->grqk", queries, key_rot, preferred_element_type=jnp.float32
    ) * HEAD ** (-0.5)
    scores = jnp.where(allowed, scores, MASK_FILL)
    row_max = jnp.max(scores, axis=-1, keepdims=True)
    exponent = jnp.exp(scores - row_max)
    totals = jnp.sum(exponent, axis=-1, keepdims=True)
    log_total = row_max + jnp.log(totals)
    softmax_probs = (exponent / totals).astype(jnp.bfloat16)
    mixed = (
        jnp.einsum("grqk,kgd->qgrd", softmax_probs, values, preferred_element_type=jnp.float32)
        .reshape(group, -1)
        .astype(jnp.bfloat16)
    )

    def attention_term(first_row, row_count):
        return jnp.dot(mixed, w_out, preferred_element_type=jnp.float32)

    middle = layer_in + collect(attention_term, local_rows)
    inverse_two = lax.rsqrt(jnp.mean(middle * middle, axis=1, keepdims=True) + EPSILON)
    normed_two = spread((middle * inverse_two * ffn_gain.astype(jnp.float32)).astype(jnp.bfloat16))
    gate_proj = jnp.dot(normed_two, w_gate, preferred_element_type=jnp.float32)
    up_proj = jnp.dot(normed_two, w_up, preferred_element_type=jnp.float32)
    hidden = (jax.nn.silu(gate_proj) * up_proj).astype(jnp.bfloat16)

    def feed_term(first_row, row_count):
        return jnp.dot(hidden, w_down, preferred_element_type=jnp.float32)

    result = (middle + collect(feed_term, local_rows)).astype(jnp.bfloat16)
    kept = (
        layer_in,
        inverse_one,
        normed_one,
        queries,
        key_rot,
        values,
        log_total,
        mixed,
        middle,
        inverse_two,
        normed_two,
        gate_proj,
        up_proj,
        hidden,
        seq_lens,
    )
    return (result, kept)


def backward(kept, grad_result, weights):
    (
        layer_in,
        inverse_one,
        normed_one,
        queries,
        key_rot,
        values,
        log_total,
        mixed,
        middle,
        inverse_two,
        normed_two,
        gate_proj,
        up_proj,
        hidden,
        seq_lens,
    ) = kept
    norm_gain, w_query, w_key, w_value, w_out, ffn_gain, w_gate, w_up, w_down = weights
    local_rows = layer_in.shape[0]
    group = normed_one.shape[0]
    grad_feed = spread_grad(grad_result.astype(jnp.bfloat16))
    d_hidden = contract(grad_feed, w_down, 1, 1)
    g_down = contract(hidden, grad_feed, 0, 0)
    sigmoid_gate = jax.nn.sigmoid(gate_proj)
    d_up = (d_hidden * gate_proj * sigmoid_gate).astype(jnp.bfloat16)
    d_gate = (d_hidden * up_proj * sigmoid_gate * (1.0 + gate_proj * (1.0 - sigmoid_gate))).astype(
        jnp.bfloat16
    )
    g_gate = contract(normed_two, d_gate, 0, 0)
    g_up = contract(normed_two, d_up, 0, 0)

    def feed_back(first_row, row_count):
        return contract(d_gate, w_gate, 1, 1) + contract(d_up, w_up, 1, 1)

    d_norm_two = collect_grad(feed_back, local_rows)
    unit_two = middle * inverse_two
    scaled_two = d_norm_two * ffn_gain.astype(jnp.float32)
    g_ffn_gain = jnp.sum(d_norm_two * unit_two, axis=0)
    d_middle = grad_result + inverse_two * (
        scaled_two - unit_two * jnp.mean(scaled_two * unit_two, axis=1, keepdims=True)
    )
    grad_attn = spread_grad(d_middle.astype(jnp.bfloat16))
    g_out = contract(mixed, grad_attn, 0, 0)
    kv_count = key_rot.shape[1]
    repeats = queries.shape[2]
    d_mixed = (
        contract(grad_attn, w_out, 1, 1)
        .astype(jnp.bfloat16)
        .reshape(group, kv_count, repeats, HEAD)
    )
    cosine, sine_part, allowed = geometry(seq_lens, group)
    scores = jnp.einsum(
        "qgrd,kgd->grqk", queries, key_rot, preferred_element_type=jnp.float32
    ) * HEAD ** (-0.5)
    softmax_probs = jnp.where(allowed, jnp.exp(scores - log_total), 0.0)
    d_probs = jnp.einsum("qgrd,kgd->grqk", d_mixed, values, preferred_element_type=jnp.float32)
    d_values = jnp.einsum(
        "grqk,qgrd->kgd",
        softmax_probs.astype(jnp.bfloat16),
        d_mixed,
        preferred_element_type=jnp.float32,
    )
    d_scores = (
        softmax_probs * (d_probs - jnp.sum(d_probs * softmax_probs, axis=-1, keepdims=True))
    ).astype(jnp.bfloat16)
    d_queries = jnp.einsum(
        "grqk,kgd->qgrd", d_scores, key_rot, preferred_element_type=jnp.float32
    ) * HEAD ** (-0.5)
    d_keys = jnp.einsum(
        "grqk,qgrd->kgd", d_scores, queries, preferred_element_type=jnp.float32
    ) * HEAD ** (-0.5)
    d_queries = (
        unrotate(d_queries, cosine[:, None, None, :], sine_part[:, None, None, :])
        .astype(jnp.bfloat16)
        .reshape(group, -1)
    )
    d_keys = (
        unrotate(d_keys, cosine[:, None, :], sine_part[:, None, :])
        .astype(jnp.bfloat16)
        .reshape(group, -1)
    )
    d_values = d_values.astype(jnp.bfloat16).reshape(group, -1)
    g_query = contract(normed_one, d_queries, 0, 0)
    g_key = contract(normed_one, d_keys, 0, 0)
    g_value = contract(normed_one, d_values, 0, 0)

    def attention_back(first_row, row_count):
        return (
            contract(d_queries, w_query, 1, 1)
            + contract(d_keys, w_key, 1, 1)
            + contract(d_values, w_value, 1, 1)
        )

    d_norm_one = collect_grad(attention_back, local_rows)
    unit_one = layer_in * inverse_one
    scaled_one = d_norm_one * norm_gain.astype(jnp.float32)
    g_attn_gain = jnp.sum(d_norm_one * unit_one, axis=0)
    d_input = d_middle + inverse_one * (
        scaled_one - unit_one * jnp.mean(scaled_one * unit_one, axis=1, keepdims=True)
    )
    matrices = (g_query, g_key, g_value, g_out, g_gate, g_up, g_down)
    return (d_input.astype(jnp.bfloat16), matrices, (g_attn_gain, g_ffn_gain))


def local(
    tokens_in,
    cotangent,
    lengths,
    attn_gain,
    w_query,
    w_key,
    w_value,
    w_out,
    ffn_gain,
    w_gate,
    w_up,
    w_down,
):
    micro = tokens_in.shape[0]
    section_id = lax.axis_index("section")
    at_first = section_id == 0
    local_params = (
        attn_gain[0],
        w_query[0],
        w_key[0],
        w_value[0],
        w_out[0],
        ffn_gain[0],
        w_gate[0],
        w_up[0],
        w_down[0],
    )
    weights = gather_weights(local_params)
    passed = jnp.zeros(tokens_in.shape[1:], jnp.bfloat16)
    kept_all = []
    results = []
    for tick_index in range(micro + 1):
        own_micro = min(tick_index, micro - 1)
        late_micro = max(tick_index - 1, 0)
        layer_in = jnp.where(at_first, tokens_in[own_micro], passed)
        seq_lens = jnp.where(at_first, lengths[own_micro, 0], lengths[late_micro, 0])
        result, kept = forward(layer_in.astype(jnp.float32), seq_lens, weights)
        kept_all.append(kept)
        results.append(result)
        if tick_index < micro:
            passed = from_behind(result, "section", 1)
    weights_back = gather_weights_again(local_params)
    received = jnp.zeros(tokens_in.shape[1:], jnp.bfloat16)
    zero_rows = jnp.zeros(tokens_in.shape[1:], jnp.bfloat16)
    input_grads = []
    matrix_totals = None
    gain_totals = None
    for back_step in range(micro + 1):
        tick_index = micro - back_step
        late_micro = micro - 1 - back_step
        upstream = cotangent[late_micro] if late_micro >= 0 else zero_rows
        grad_result = jnp.where(at_first, received, upstream)
        d_input, matrices, gains = backward(
            kept_all[tick_index], grad_result.astype(jnp.float32), weights_back
        )
        input_grads.append(d_input)
        if back_step < micro:
            received = from_behind(d_input, "section", -1)
        if matrix_totals is None:
            matrix_totals = matrices
            gain_totals = gains
        else:
            matrix_totals = tuple((total + extra for total, extra in zip(matrix_totals, matrices)))
            gain_totals = tuple((total + extra for total, extra in zip(gain_totals, gains)))
    shares = (
        lax.psum_scatter(
            matrix_totals[0].astype(jnp.bfloat16), "dp", scatter_dimension=0, tiled=True
        ).astype(jnp.float32),
        lax.psum_scatter(
            matrix_totals[1].astype(jnp.bfloat16), "dp", scatter_dimension=0, tiled=True
        ).astype(jnp.float32),
        lax.psum_scatter(
            matrix_totals[2].astype(jnp.bfloat16), "dp", scatter_dimension=0, tiled=True
        ).astype(jnp.float32),
        lax.psum_scatter(
            matrix_totals[3].astype(jnp.bfloat16), "dp", scatter_dimension=1, tiled=True
        ).astype(jnp.float32),
        lax.psum_scatter(
            matrix_totals[4].astype(jnp.bfloat16), "dp", scatter_dimension=0, tiled=True
        ).astype(jnp.float32),
        lax.psum_scatter(
            matrix_totals[5].astype(jnp.bfloat16), "dp", scatter_dimension=0, tiled=True
        ).astype(jnp.float32),
        lax.psum_scatter(
            matrix_totals[6].astype(jnp.bfloat16), "dp", scatter_dimension=1, tiled=True
        ).astype(jnp.float32),
    )
    gain_shares = (
        lax.psum_scatter(gain_totals[0], ("dp", "tensor"), scatter_dimension=0, tiled=True),
        lax.psum_scatter(gain_totals[1], ("dp", "tensor"), scatter_dimension=0, tiled=True),
    )
    section_out = jnp.stack(
        [jnp.where(at_first, results[which], results[which + 1]) for which in range(micro)]
    )
    input_grad = jnp.stack(
        [
            jnp.where(at_first, input_grads[micro - which], input_grads[micro - 1 - which])
            for which in range(micro)
        ]
    )
    return (
        section_out[None],
        input_grad[None],
        gain_shares[0][None],
        shares[0][None],
        shares[1][None],
        shares[2][None],
        shares[3][None],
        gain_shares[1][None],
        shares[4][None],
        shares[5][None],
        shares[6][None],
    )


def solution(mesh):
    return jax.shard_map(
        local,
        mesh=mesh,
        in_specs=(
            P(None, ("dp", "tensor"), None),
            P(None, ("dp", "tensor"), None),
            P(None, "dp", None),
            P("section", "dp"),
            P("section", "dp", "tensor"),
            P("section", "dp", "tensor"),
            P("section", "dp", "tensor"),
            P("section", "tensor", "dp"),
            P("section", "dp"),
            P("section", "dp", "tensor"),
            P("section", "dp", "tensor"),
            P("section", "tensor", "dp"),
        ),
        out_specs=(
            P("section", None, ("dp", "tensor"), None),
            P("section", None, ("dp", "tensor"), None),
            P("section", ("dp", "tensor")),
            P("section", "dp", "tensor"),
            P("section", "dp", "tensor"),
            P("section", "dp", "tensor"),
            P("section", "tensor", "dp"),
            P("section", ("dp", "tensor")),
            P("section", "dp", "tensor"),
            P("section", "dp", "tensor"),
            P("section", "tensor", "dp"),
        ),
        check_vma=False,
    )
```

profile of v0, /device:TPU:0, one launch (start us, length us, event | category | flops | bytes accessed | tf_op | source)
XLA Modules:
  0.0 1712.3 jit_solution(2365654597355986699)
XLA Ops:
  175.8 33.6 %all-gather.30.cloned.1.call-done = bf16[384,2048]{1,0:T(8,128)(2,1)} async-done(((bf16[96,2048]{1,0:T(8,128)(2,1)}), bf16[384,2048]{1,0:T(8,128)(2,1)}) %all-gather.30.cloned.1.call-update) | async-done | bytes 1572880 | tf_op jit(solution)/shard_map/all_gather | solution.py:69
  209.4 66.4 %all-gather.54.cloned.1.call-done = bf16[1,2048,1408]{2,1,0:T(8,128)(2,1)} async-done(((bf16[1,512,1408]{2,1,0:T(8,128)(2,1)}), bf16[1,2048,1408]{2,1,0:T(8,128)(2,1)}) %all-gather.54.cloned.1.call-update) | async-done | bytes 5767184 | tf_op jit(solution)/shard_map/all_gather | solution.py:102
  282.8 60.6 %all-gather.56.cloned.1.call-done = bf16[1,2048,1408]{2,1,0:T(8,128)(2,1)} async-done(((bf16[1,512,1408]{2,1,0:T(8,128)(2,1)}), bf16[1,2048,1408]{2,1,0:T(8,128)(2,1)}) %all-gather.56.cloned.1.call-update) | async-done | bytes 5767184 | tf_op jit(solution)/shard_map/all_gather | solution.py:103
  350.4 60.5 %all-gather.58.cloned.1.call-done = bf16[1,1408,2048]{2,1,0:T(8,128)(2,1)} async-done(((bf16[1,1408,512]{2,1,0:T(8,128)(2,1)}), bf16[1,1408,2048]{2,1,0:T(8,128)(2,1)}) %all-gather.58.cloned.1.call-update) | async-done | bytes 5767184 | tf_op jit(solution)/shard_map/all_gather | solution.py:104
  417.8 35.4 %reduce-scatter.22.cloned.1.call-done = bf16[96,2048]{1,0:T(8,128)(2,1)} async-done(((bf16[384,2048]{1,0:T(8,128)(2,1)}), bf16[96,2048]{1,0:T(8,128)(2,1)}) %reduce-scatter.22.cloned.1.call-update) | async-done | bytes 393232 | tf_op jit(solution)/shard_map/reduce_scatter | solution.py:73
  458.7 36.3 %all-gather.32.cloned.1.call-done = bf16[384,2048]{1,0:T(8,128)(2,1)} async-done(((bf16[96,2048]{1,0:T(8,128)(2,1)}), bf16[384,2048]{1,0:T(8,128)(2,1)}) %all-gather.32.cloned.1.call-update) | async-done | bytes 1572880 | tf_op jit(solution)/shard_map/all_gather | solution.py:69
  509.1 34.1 %reduce-scatter.24.cloned.1.call-done = bf16[96,2048]{1,0:T(8,128)(2,1)} async-done(((bf16[384,2048]{1,0:T(8,128)(2,1)}), bf16[96,2048]{1,0:T(8,128)(2,1)}) %reduce-scatter.24.cloned.1.call-update) | async-done | bytes 393232 | tf_op jit(solution)/shard_map/reduce_scatter | solution.py:73
  546.4 36.2 %all-gather.34.cloned.1.call-done = bf16[384,2048]{1,0:T(8,128)(2,1)} async-done(((bf16[96,2048]{1,0:T(8,128)(2,1)}), bf16[384,2048]{1,0:T(8,128)(2,1)}) %all-gather.34.cloned.1.call-update) | async-done | bytes 1572880 | tf_op jit(solution)/shard_map/all_gather | solution.py:69
  600.8 34.3 %reduce-scatter.26.cloned.1.call-done = bf16[96,2048]{1,0:T(8,128)(2,1)} async-done(((bf16[384,2048]{1,0:T(8,128)(2,1)}), bf16[96,2048]{1,0:T(8,128)(2,1)}) %reduce-scatter.26.cloned.1.call-update) | async-done | bytes 393232 | tf_op jit(solution)/shard_map/reduce_scatter | solution.py:73
  641.5 36.3 %all-gather.36.cloned.1.call-done = bf16[384,2048]{1,0:T(8,128)(2,1)} async-done(((bf16[96,2048]{1,0:T(8,128)(2,1)}), bf16[384,2048]{1,0:T(8,128)(2,1)}) %all-gather.36.cloned.1.call-update) | async-done | bytes 1572880 | tf_op jit(solution)/shard_map/all_gather | solution.py:69
  730.9 34.4 %all-gather.60.cloned.1.call-done = bf16[1,384,2048]{2,1,0:T(8,128)(2,1)} async-done(((bf16[1,96,2048]{2,1,0:T(8,128)(2,1)}), bf16[1,384,2048]{2,1,0:T(8,128)(2,1)}) %all-gather.60.cloned.1.call-update) | async-done | bytes 1572880 | tf_op jit(solution)/shard_map/all_gather | solution.py:82
  822.9 34.2 %reduce-scatter.32.cloned.1.call-done = bf16[96,2048]{1,0:T(8,128)(2,1)} async-done(((bf16[384,2048]{1,0:T(8,128)(2,1)}), bf16[96,2048]{1,0:T(8,128)(2,1)}) %reduce-scatter.32.cloned.1.call-update) | async-done | bytes 393232 | tf_op jit(solution)/shard_map/reduce_scatter | solution.py:86
  863.7 34.7 %all-gather.40.cloned.1.call-done = bf16[384,2048]{1,0:T(8,128)(2,1)} async-done(((bf16[96,2048]{1,0:T(8,128)(2,1)}), bf16[384,2048]{1,0:T(8,128)(2,1)}) %all-gather.40.cloned.1.call-update) | async-done | bytes 1572880 | tf_op jit(solution)/shard_map/all_gather | solution.py:82
  919.8 34.2 %reduce-scatter.34.cloned.1.call-done = bf16[96,2048]{1,0:T(8,128)(2,1)} async-done(((bf16[384,2048]{1,0:T(8,128)(2,1)}), bf16[96,2048]{1,0:T(8,128)(2,1)}) %reduce-scatter.34.cloned.1.call-update) | async-done | bytes 393232 | tf_op jit(solution)/shard_map/reduce_scatter | solution.py:86
  963.2 36.2 %all-gather.42.cloned.1.call-done = bf16[384,2048]{1,0:T(8,128)(2,1)} async-done(((bf16[96,2048]{1,0:T(8,128)(2,1)}), bf16[384,2048]{1,0:T(8,128)(2,1)}) %all-gather.42.cloned.1.call-update) | async-done | bytes 1572880 | tf_op jit(solution)/shard_map/all_gather | solution.py:82
  1020.1 34.3 %reduce-scatter.36.cloned.1.call-done = bf16[96,2048]{1,0:T(8,128)(2,1)} async-done(((bf16[384,2048]{1,0:T(8,128)(2,1)}), bf16[96,2048]{1,0:T(8,128)(2,1)}) %reduce-scatter.36.cloned.1.call-update) | async-done | bytes 393232 | tf_op jit(solution)/shard_map/reduce_scatter | solution.py:86
  1059.9 35.2 %all-gather.44.cloned.1.call-done = bf16[384,2048]{1,0:T(8,128)(2,1)} async-done(((bf16[96,2048]{1,0:T(8,128)(2,1)}), bf16[384,2048]{1,0:T(8,128)(2,1)}) %all-gather.44.cloned.1.call-update) | async-done | bytes 1572880 | tf_op jit(solution)/shard_map/all_gather | solution.py:82
  1116.5 34.3 %reduce-scatter.38.cloned.1.call-done = bf16[96,2048]{1,0:T(8,128)(2,1)} async-done(((bf16[384,2048]{1,0:T(8,128)(2,1)}), bf16[96,2048]{1,0:T(8,128)(2,1)}) %reduce-scatter.38.cloned.1.call-update) | async-done | bytes 393232 | tf_op jit(solution)/shard_map/reduce_scatter | solution.py:86
  1160.1 35.7 %all-gather.46.cloned.1.call-done = bf16[384,2048]{1,0:T(8,128)(2,1)} async-done(((bf16[96,2048]{1,0:T(8,128)(2,1)}), bf16[384,2048]{1,0:T(8,128)(2,1)}) %all-gather.46.cloned.1.call-update) | async-done | bytes 1572880 | tf_op jit(solution)/shard_map/all_gather | solution.py:82
  1216.6 34.3 %reduce-scatter.40.cloned.1.call-done = bf16[96,2048]{1,0:T(8,128)(2,1)} async-done(((bf16[384,2048]{1,0:T(8,128)(2,1)}), bf16[96,2048]{1,0:T(8,128)(2,1)}) %reduce-scatter.40.cloned.1.call-update) | async-done | bytes 393232 | tf_op jit(solution)/shard_map/reduce_scatter | solution.py:86
  1421.4 75.7 %all-reduce.2 = (f32[2048]{0:T(1024)S(1)}, f32[2048]{0:T(1024)S(1)}) all-reduce(f32[2048]{0:T(1024)S(1)} %add_add_fusion.1, f32[2048]{0:T(1024)S(1)} %add_add_fusion), channel_id=24, replica_groups=mesh['section'=2,'dp'=4,'tensor'=4] {'dp','tensor'}, use_global_device_ids=true, to_apply=%region_45.46.clone | all-reduce | flops 4096 | bytes 32768
  1505.1 59.6 %reduce-scatter.52.cloned.1.call-done = bf16[512,1408]{1,0:T(8,128)(2,1)} async-done(((bf16[2048,1408]{1,0:T(8,128)(2,1)}), bf16[512,1408]{1,0:T(8,128)(2,1)}) %reduce-scatter.52.cloned.1.call-update) | async-done | bytes 1441808 | tf_op jit(solution)/shard_map/reduce_scatter | solution.py:380
  1567.8 65.7 %reduce-scatter.54.cloned.1.call-done = bf16[512,1408]{1,0:T(8,128)(2,1)} async-done(((bf16[2048,1408]{1,0:T(8,128)(2,1)}), bf16[512,1408]{1,0:T(8,128)(2,1)}) %reduce-scatter.54.cloned.1.call-update) | async-done | bytes 1441808 | tf_op jit(solution)/shard_map/reduce_scatter | solution.py:383
  1636.7 65.5 %reduce-scatter.56.cloned.1.call-done = bf16[1408,512]{1,0:T(8,128)(2,1)} async-done(((bf16[1408,2048]{1,0:T(8,128)(2,1)}), bf16[1408,512]{1,0:T(8,128)(2,1)}) %reduce-scatter.56.cloned.1.call-update) | async-done | bytes 1441808 | tf_op jit(solution)/shard_map/reduce_scatter | solution.py:386
  (696 shorter events, 646.9 us)
Async XLA Ops:
  20.8 109.8 %all-gather.52.cloned.1.call-start = ((), (), s32[]{:S(2)}) async-start(), calls=%async_computation.50 | async-start | bytes 2621440 | tf_op jit(solution)/shard_map/all_gather | solution.py:100
  21.5 148.4 %reduce-scatter.20.cloned.1.call-start = ((), (), s32[]{:S(2)}) async-start(), calls=%async_computation.20 | async-start | bytes 1966080 | tf_op jit(solution)/shard_map/reduce_scatter | solution.py:73
  173.2 102.6 %all-gather.54.cloned.1.call-start = ((), (), s32[]{:S(2)}) async-start(), calls=%async_computation.51 | async-start | bytes 7208960 | tf_op jit(solution)/shard_map/all_gather | solution.py:102
  173.7 169.7 %all-gather.56.cloned.1.call-start = ((), (), s32[]{:S(2)}) async-start(), calls=%async_computation.52 | async-start | bytes 7208960 | tf_op jit(solution)/shard_map/all_gather | solution.py:103
  174.5 236.5 %all-gather.58.cloned.1.call-start = ((), (), s32[]{:S(2)}) async-start(), calls=%async_computation.53 | async-start | bytes 7208960 | tf_op jit(solution)/shard_map/all_gather | solution.py:104
  175.2 277.9 %reduce-scatter.22.cloned.1.call-start = ((), (), s32[]{:S(2)}) async-start(), calls=%async_computation.22 | async-start | bytes 1966080 | tf_op jit(solution)/shard_map/reduce_scatter | solution.py:73
  458.5 84.7 %reduce-scatter.24.cloned.1.call-start = ((), (), s32[]{:S(2)}) async-start(), calls=%async_computation.24 | async-start | bytes 1966080 | tf_op jit(solution)/shard_map/reduce_scatter | solution.py:73
  546.3 88.7 %reduce-scatter.26.cloned.1.call-start = ((), (), s32[]{:S(2)}) async-start(), calls=%async_computation.26 | async-start | bytes 1966080 | tf_op jit(solution)/shard_map/reduce_scatter | solution.py:73
  641.3 85.9 %reduce-scatter.28.cloned.1.call-start = ((), (), s32[]{:S(2)}) async-start(), calls=%async_computation.28 | async-start | bytes 1966080 | tf_op jit(solution)/shard_map/reduce_scatter | solution.py:73
  695.1 108.1 %all-gather.38.cloned.1.call-start = ((), (), s32[]{:S(2)}) async-start(), calls=%async_computation.29 | async-start | bytes 1966080 | tf_op jit(solution)/shard_map/all_gather | solution.py:69
  730.8 126.3 %reduce-scatter.32.cloned.1.call-start = ((), (), s32[]{:S(2)}) async-start(), calls=%async_computation.31 | async-start | bytes 1966080 | tf_op jit(solution)/shard_map/reduce_scatter | solution.py:86
  862.1 91.9 %reduce-scatter.34.cloned.1.call-start = ((), (), s32[]{:S(2)}) async-start(), calls=%async_computation.33 | async-start | bytes 1966080 | tf_op jit(solution)/shard_map/reduce_scatter | solution.py:86
  963.1 91.3 %reduce-scatter.36.cloned.1.call-start = ((), (), s32[]{:S(2)}) async-start(), calls=%async_computation.35 | async-start | bytes 1966080 | tf_op jit(solution)/shard_map/reduce_scatter | solution.py:86
  1058.9 91.9 %reduce-scatter.38.cloned.1.call-start = ((), (), s32[]{:S(2)}) async-start(), calls=%async_computation.37 | async-start | bytes 1966080 | tf_op jit(solution)/shard_map/reduce_scatter | solution.py:86
  1159.7 91.2 %reduce-scatter.40.cloned.1.call-start = ((), (), s32[]{:S(2)}) async-start(), calls=%async_computation.39 | async-start | bytes 1966080 | tf_op jit(solution)/shard_map/reduce_scatter | solution.py:86
  1254.9 159.5 %reduce-scatter.30.cloned.1.call-start = ((), (), s32[]{:S(2)}) async-start(), calls=%async_computation.30 | async-start | bytes 1966080 | tf_op jit(solution)/shard_map/reduce_scatter | solution.py:73
  1262.4 154.5 %reduce-scatter.46.cloned.1.call-start = ((), (), s32[]{:S(2)}) async-start(), calls=%async_computation.43 | async-start | bytes 327680 | tf_op jit(solution)/shard_map/reduce_scatter | solution.py:371
  1313.8 104.6 %reduce-scatter.48.cloned.1.call-start = ((), (), s32[]{:S(2)}) async-start(), calls=%async_computation.44 | async-start | bytes 327680 | tf_op jit(solution)/shard_map/reduce_scatter | solution.py:374
  1321.8 98.2 %reduce-scatter.42.cloned.1.call-start = ((), (), s32[]{:S(2)}) async-start(), calls=%async_computation.41 | async-start | bytes 1966080 | tf_op jit(solution)/shard_map/reduce_scatter | solution.py:86
  1329.4 171.4 %reduce-scatter.44.cloned.1.call-start = ((), (), s32[]{:S(2)}) async-start(), calls=%async_computation.42 | async-start | bytes 2621440 | tf_op jit(solution)/shard_map/reduce_scatter | solution.py:368
  1336.2 166.8 %reduce-scatter.50.cloned.1.call-start = ((), (), s32[]{:S(2)}) async-start(), calls=%async_computation.45 | async-start | bytes 2621440 | tf_op jit(solution)/shard_map/reduce_scatter | solution.py:377
  1344.0 220.7 %reduce-scatter.52.cloned.1.call-start = ((), (), s32[]{:S(2)}) async-start(), calls=%async_computation.46 | async-start | bytes 7208960 | tf_op jit(solution)/shard_map/reduce_scatter | solution.py:380
  1367.0 266.6 %reduce-scatter.54.cloned.1.call-start = ((), (), s32[]{:S(2)}) async-start(), calls=%async_computation.47 | async-start | bytes 7208960 | tf_op jit(solution)/shard_map/reduce_scatter | solution.py:383
  1390.1 312.1 %reduce-scatter.56.cloned.1.call-start = ((), (), s32[]{:S(2)}) async-start(), calls=%async_computation.48 | async-start | bytes 7208960 | tf_op jit(solution)/shard_map/reduce_scatter | solution.py:386
  (220 other events, 5398.8 us)
Sparse Core Ops, SparseCore 0:
  20.2 37.3 all-gather.27
  95.4 35.1 all-gather.51
  134.6 35.2 reduce-scatter.19
  173.3 36.0 all-gather.29
  211.1 64.6 all-gather.53
  277.6 65.7 all-gather.55
  345.3 65.6 all-gather.57
  417.9 35.2 reduce-scatter.21
  458.6 36.3 all-gather.31
  546.5 36.0 all-gather.33
  641.4 36.2 all-gather.35
  729.2 36.0 all-gather.59
  767.3 35.9 all-gather.37
  862.3 36.0 all-gather.39
  963.2 36.0 all-gather.41
  1059.0 36.0 all-gather.43
  1159.8 36.0 all-gather.45
  1255.1 36.0 all-gather.47
  1383.3 35.2 reduce-scatter.41
  1422.2 34.5 reduce-scatter.43
  1460.4 35.3 reduce-scatter.49
  1498.8 65.8 reduce-scatter.51
  1567.7 65.8 reduce-scatter.53
  1636.4 65.8 reduce-scatter.55
  (12 shorter events, 387.9 us)
where the time goes:
time: 1720 us; the launch traced here: 1710 us
  waiting for transfers between devices  1170 us (68%)
  matrix products  292 us (17%)
  blocking collectives  110 us (6%)
  other arithmetic  83.7 us (5%)
  local copies, waits for them, and re-layouts  23.2 us (1%)
  between operations  17.9 us (1%)
    all_gather x6, waiting for transfers between devices, spread_grad(): return lax.all_gather(local_block, 'tensor', axis=0, tiled=True)  201 us
    all_gather x6, waiting for transfers between devices, spread(): return lax.all_gather(local_block, 'tensor', axis=0, tiled=True)  190 us
    dot_general x42, matrix products, contract(): lax.dot_general(left, right, (((left_dim,), (right_dim,)), ((), ())), pre...  171 us
    reduce_scatter x6, waiting for transfers between devices, collect_grad(): lax.psum_scatter(term_fn(jnp.int32(0), local_rows * lax.axis_size('tensor...  171 us
    reduce_scatter x6, waiting for transfers between devices, collect(): lax.psum_scatter(term_fn(jnp.int32(0), local_rows * lax.axis_size('tensor...  163 us
    unnamed x1, blocking collectives  75.7 us
    all_gather x1, waiting for transfers between devices, gather_weights(): lax.all_gather(local_params[6], 'dp', axis=0, tiled=True)  66.4 us
    reduce_scatter x1, waiting for transfers between devices, local(): lax.psum_scatter(matrix_totals[5].astype(jnp.bfloat16), 'dp', scatter_dim...  65.7 us
  transfers between devices with their start and end apart: 40, of which 34 were waited for; matrix products, arithmetic and copies ran while one was open for 11% of the time, Pallas kernels for 0%

commit v1 on v0

v1 whole, which is shorter than its diff:
```python
import jax
import jax.numpy as jnp
from jax import lax
from jax.experimental import pallas as pl
from jax.experimental.pallas import tpu as pltpu
from jax.sharding import PartitionSpec as P

HEAD = 64


EPSILON = 1e-05
MASK_FILL = -1e30
BF16 = jnp.bfloat16
F32 = jnp.float32
LANES = 128
SCALE = HEAD ** (-0.5)
VMEM_BYTES = 24 * 2**20


def turn(value, axis, steps):
    count = lax.axis_size(axis)
    return lax.ppermute(value, axis, [(i, (i + steps) % count) for i in range(count)])


def swap(value):
    return lax.ppermute(value, "section", [(0, 1), (1, 0)])


def contract(left, right, left_dim, right_dim):
    return lax.dot_general(
        left, right, (((left_dim,), (right_dim,)), ((), ())), preferred_element_type=F32
    )


def geometry(seq_lens, rows):
    count = lax.axis_size("tensor")
    place = (lax.axis_index("tensor") - jnp.arange(count, dtype=jnp.int32)) % count
    row_ids = (place[:, None] * rows + jnp.arange(rows, dtype=jnp.int32)[None, :]).reshape(-1)
    ends = jnp.cumsum(seq_lens)
    starts = ends - seq_lens
    member = jnp.sum((row_ids[:, None] >= ends[None, :]).astype(jnp.int32), axis=1)
    slots = jnp.arange(seq_lens.shape[0], dtype=jnp.int32)
    begins = jnp.sum(jnp.where(member[:, None] == slots[None, :], starts[None, :], 0), axis=1)
    position = row_ids - begins
    half_dim = HEAD // 2
    frequency = 10000.0 ** (-jnp.arange(half_dim, dtype=F32) / half_dim)
    angle = position.astype(F32)[:, None] * frequency[None, :]
    allowed = (member[:, None] == member[None, :]) & (row_ids[:, None] >= row_ids[None, :])
    cosine, sine_part = (jnp.cos(angle), jnp.sin(angle))
    cosine = jnp.concatenate([cosine] * (LANES // half_dim), axis=1)
    sine_part = jnp.concatenate([-sine_part, sine_part] * (LANES // HEAD), axis=1)
    turned = jnp.arange(LANES) < HEAD
    tables = jnp.stack(
        [cosine, sine_part, jnp.where(turned, cosine, 1.0), jnp.where(turned, sine_part, 0.0)]
    )
    return (tables, jnp.where(allowed, 0.0, MASK_FILL))


def barrier(*values):
    return lax.optimization_barrier(values)


class Job:
    def __init__(self, fn, *inputs):
        self.fn, self.inputs, self.results = (fn, inputs, None)

    def __getitem__(self, which):
        return self.results[which]


def step(value, job):
    if job is None:
        return turn(value, "tensor", 1)
    inputs = job.inputs() if callable(job.inputs) else job.inputs
    value, *inputs = barrier(value, *inputs)
    recv = turn(value, "tensor", 1)
    recv, *results = barrier(recv, *job.fn(*inputs))
    job.results = results
    return recv


def spread(block, jobs=()):
    pieces = [block]
    for k in range(lax.axis_size("tensor") - 1):
        pieces.append(step(pieces[-1], jobs[k] if k < len(jobs) else None))
    return jnp.concatenate(pieces, axis=0)


def collect(partial, jobs=()):
    count = lax.axis_size("tensor")
    rows = partial.shape[0] // count
    blocks = partial.reshape(count, rows, partial.shape[1])
    total = blocks[1 % count]
    for k in range(count - 1):
        recv = step(total.astype(BF16), jobs[k] if k < len(jobs) else None)
        total = recv.astype(F32) + blocks[(k + 2) % count]
    return total


class Ring:
    def __init__(self, first):
        self.count, self.taken, self.value = (lax.axis_size("tensor"), 0, first)

    def run(self, fn, *inputs):
        if self.taken == self.count - 1:
            return fn(*inputs)
        job = Job(fn, *inputs)
        self.accept(step(self.value, job))
        self.taken += 1
        return tuple(job.results)

    def finish(self):
        while self.taken < self.count - 1:
            self.run(lambda: ())
        return self.result()


class SpreadRing(Ring):
    def __init__(self, block):
        super().__init__(block)
        self.pieces = [block]

    def accept(self, recv):
        self.pieces.append(recv)
        self.value = recv

    def result(self):
        return jnp.concatenate(self.pieces, axis=0)


class CollectRing(Ring):
    def __init__(self, partial):
        count = lax.axis_size("tensor")
        self.blocks = partial.reshape(count, partial.shape[0] // count, partial.shape[1])
        self.total = self.blocks[1 % count].astype(F32)
        super().__init__(self.total.astype(BF16))

    def accept(self, recv):
        self.total = recv.astype(F32) + self.blocks[(self.taken + 2) % self.count]
        self.value = self.total.astype(BF16)

    def result(self):
        return self.total


def gather_direct(piece):
    count, me = (lax.axis_size("dp"), lax.axis_index("dp"))
    whole = jnp.zeros((count,) + piece.shape, piece.dtype)
    for k in range(count):
        part = turn(piece, "dp", k) if k else piece
        whole = lax.dynamic_update_index_in_dim(whole, part, (me - k) % count, 0)
    return whole


def normalizer(rows):
    return lax.rsqrt(jnp.mean(rows * rows, axis=1, keepdims=True) + EPSILON)


def half_swap(x):
    lane = lax.broadcasted_iota(jnp.int32, x.shape, 1)
    first = (lane % HEAD) < HEAD // 2
    return jnp.where(
        first, pltpu.roll(x, LANES - HEAD // 2, 1), pltpu.roll(x, HEAD // 2, 1)
    )


def heads_of(kv):
    low = lax.broadcasted_iota(jnp.int32, kv.shape, 1) < HEAD
    kv = kv.astype(F32)
    turned = pltpu.roll(kv, HEAD, 1)
    keys = (jnp.where(low, kv, 0.0).astype(BF16), jnp.where(low, 0.0, turned).astype(BF16))
    values = (jnp.where(low, turned, 0.0).astype(BF16), jnp.where(low, 0.0, kv).astype(BF16))
    return (keys, values)


def attend_kernel(qkv_ref, table_ref, bias_ref, rot_ref, mixed_ref, lse_ref):
    q_cols = mixed_ref.shape[1]
    cosine, sine_part = (table_ref[0], table_ref[1])
    kv = qkv_ref[:, q_cols:]
    kv = (kv * table_ref[2] + half_swap(kv) * table_ref[3]).astype(BF16)
    rot_ref[:, q_cols:] = kv
    keys, values = heads_of(kv)
    bias = bias_ref[...]
    log_totals = []
    for slab in range(q_cols // LANES):
        cols = slice(slab * LANES, (slab + 1) * LANES)
        query = qkv_ref[:, cols]
        query = (query * cosine + half_swap(query) * sine_part).astype(BF16)
        rot_ref[:, cols] = query
        mixed = 0.0
        for odd in range(2):
            scores = contract(query, keys[odd], 1, 1) * SCALE + bias
            row_max = jnp.max(scores, axis=1, keepdims=True)
            exponent = jnp.exp(scores - row_max)
            totals = jnp.sum(exponent, axis=1, keepdims=True)
            log_totals.append(row_max + jnp.log(totals))
            mixed = mixed + contract((exponent / totals).astype(BF16), values[odd], 1, 0)
        mixed_ref[:, cols] = mixed.astype(BF16)
    lse_ref[...] = jnp.concatenate(log_totals, axis=1)


def attend(normed_one, geo, w_attn, kv_cols):
    group = normed_one.shape[0]
    q_cols = w_attn.shape[1] // 2 - kv_cols
    both = q_cols + 2 * kv_cols
    qkv = jnp.dot(normed_one, w_attn[:, :both], preferred_element_type=F32)
    rotated, mixed, log_total = pl.pallas_call(
        attend_kernel,
        out_shape=(
            jax.ShapeDtypeStruct((group, both), BF16),
            jax.ShapeDtypeStruct((group, q_cols), BF16),
            jax.ShapeDtypeStruct((group, q_cols // HEAD), F32),
        ),
        compiler_params=pltpu.CompilerParams(vmem_limit_bytes=VMEM_BYTES),
    )(qkv, *geo)
    return (contract(mixed, w_attn[:, both:], 1, 1), rotated, log_total, mixed)


def attend_back_kernel(d_mixed_ref, rot_ref, lse_ref, table_ref, bias_ref, out_ref):
    q_cols = d_mixed_ref.shape[1]
    cosine, sine_part = (table_ref[0], table_ref[1])
    keys, values = heads_of(rot_ref[:, q_cols:])
    bias = bias_ref[...]
    d_keys = [0.0, 0.0]
    d_values = [0.0, 0.0]
    for slab in range(q_cols // LANES):
        cols = slice(slab * LANES, (slab + 1) * LANES)
        query = rot_ref[:, cols]
        d_mixed = d_mixed_ref[:, cols]
        d_query = 0.0
        for odd in range(2):
            head = 2 * slab + odd
            scores = contract(query, keys[odd], 1, 1) * SCALE + bias
            probs = jnp.exp(scores - lse_ref[:, head : head + 1])
            d_probs = contract(d_mixed, values[odd], 1, 1)
            total = jnp.sum(d_probs * probs, axis=1, keepdims=True)
            d_scores = (probs * (d_probs - total)).astype(BF16)
            d_query = d_query + contract(d_scores, keys[odd], 1, 0)
            d_values[odd] = d_values[odd] + contract(probs.astype(BF16), d_mixed, 0, 0)
            d_keys[odd] = d_keys[odd] + contract(d_scores, query, 0, 0)
        d_query = d_query * SCALE
        out_ref[:, cols] = (d_query * cosine - half_swap(d_query) * sine_part).astype(BF16)
    low = lax.broadcasted_iota(jnp.int32, d_keys[0].shape, 1) < HEAD
    d_kv = jnp.where(
        low,
        (d_keys[0] + pltpu.roll(d_keys[1], HEAD, 1)) * SCALE,
        d_values[1] + pltpu.roll(d_values[0], HEAD, 1),
    )
    d_kv = d_kv * table_ref[2] - half_swap(d_kv) * table_ref[3]
    out_ref[:, q_cols:] = d_kv.astype(BF16)


def attend_back(grad_attn, geo, w_attn, rotated, log_total):
    both = rotated.shape[1]
    d_mixed = jnp.dot(grad_attn, w_attn[:, both:], preferred_element_type=F32).astype(BF16)
    d_qkv = pl.pallas_call(
        attend_back_kernel,
        out_shape=jax.ShapeDtypeStruct(rotated.shape, BF16),
        compiler_params=pltpu.CompilerParams(vmem_limit_bytes=VMEM_BYTES),
    )(d_mixed, rotated, log_total, *geo)
    return (d_qkv, contract(d_qkv, w_attn[:, :both], 1, 1))


def feed(normed_two, w_ffn, units):
    gate_up = jnp.dot(normed_two, w_ffn[:, : 2 * units], preferred_element_type=F32)
    hidden = (jax.nn.silu(gate_up[:, :units]) * gate_up[:, units:]).astype(BF16)
    return (gate_up, hidden)


def feed_back(grad_feed, gate_up, w_ffn, w_down):
    units = gate_up.shape[1] // 2
    d_hidden = jnp.dot(grad_feed, w_down[:, -units:], preferred_element_type=F32)
    gate, up = (gate_up[:, :units], gate_up[:, units:])
    sigmoid_gate = jax.nn.sigmoid(gate)
    d_up = (d_hidden * gate * sigmoid_gate).astype(BF16)
    d_gate = (d_hidden * up * sigmoid_gate * (1.0 + gate * (1.0 - sigmoid_gate))).astype(BF16)
    d_gate_up = jnp.concatenate([d_gate, d_up], axis=1)
    return (d_gate_up, contract(d_gate_up, w_ffn[:, : 2 * units], 1, 1))


def core_half(rows, at_first, own):
    width = rows.shape[1] // (2 * lax.axis_size("dp"))
    low, high = (
        jnp.concatenate(
            [rows[:, start : start + width] for start in range(first, rows.shape[1], 2 * width)],
            axis=1,
        )
        for first in (0, width)
    )
    return jnp.where(at_first, low, high) if own else jnp.where(at_first, high, low)


def sent_grad(rows, grads, at_first):
    return swap(contract(core_half(rows, at_first, False), grads, 0, 0).astype(BF16))


def kept_grad(rows, grads, got, at_first):
    kept = contract(core_half(rows, at_first, True), grads, 0, 0)
    return (kept + got.astype(F32)).astype(BF16)


def scatter(half):
    return lax.psum_scatter(half, "dp", scatter_dimension=0, tiled=True)


def norm_back(rows, inverse, gain, d_normed):
    unit = rows * inverse
    scaled = d_normed * gain
    return inverse * (scaled - unit * jnp.mean(scaled * unit, axis=1, keepdims=True))


def backward(
    kept, grad_feed, grad_result, geo, weights, at_first, layer_in, normed_one, aside, arriving
):
    (rotated, log_total, mixed, middle, normed_two, gate_up, hidden) = kept
    norm_gain, ffn_gain, w_attn, w_ffn, w_down = weights
    d_gate_up, d_norm_two_all = aside.run(feed_back, grad_feed, gate_up, w_ffn, w_down)
    ffn_sent = Job(
        lambda rows, grads, *rest: (sent_grad(rows, grads, at_first), *rest),
        normed_two,
        d_gate_up,
        *arriving,
    )
    ffn_kept = Job(lambda *given: (kept_grad(*given, at_first),))
    ffn_kept.inputs = lambda: (normed_two, d_gate_up, ffn_sent[0])
    down_sent = Job(lambda *given: (sent_grad(*given, at_first),), grad_feed, hidden)
    d_norm_two = collect(d_norm_two_all, (ffn_sent, ffn_kept, down_sent))
    r_ffn = scatter(ffn_kept[0])
    d_middle = grad_result + norm_back(middle, normalizer(middle), ffn_gain, d_norm_two)
    down_kept = Job(lambda *given: (kept_grad(*given, at_first),))
    down_kept.inputs = lambda: (grad_feed, hidden, down_sent[0])
    ffn_gain_job = Job(
        lambda d_all, normed: (jnp.sum(d_all * (normed.astype(F32) / ffn_gain), axis=0),),
        d_norm_two_all,
        normed_two,
    )
    ffn_done = Job(lambda *given: given, r_ffn)
    grad_attn = spread(d_middle.astype(BF16), (down_kept, ffn_gain_job, ffn_done))
    r_down = scatter(down_kept[0])
    d_qkv, d_norm_one_all = aside.run(
        lambda grad_attn, w_attn, *rest: attend_back(grad_attn, geo, w_attn, *rest),
        grad_attn,
        w_attn,
        rotated,
        log_total,
    )
    attn_sent = Job(
        lambda rows, grads, above, heads: (
            sent_grad(rows, grads, at_first),
            sent_grad(above, heads, at_first),
        ),
        normed_one,
        d_qkv,
        grad_attn,
        mixed,
    )
    attn_kept = Job(
        lambda rows, grads, got, above, heads, got_out: (
            jnp.concatenate(
                [
                    kept_grad(rows, grads, got, at_first),
                    kept_grad(above, heads, got_out, at_first),
                ],
                axis=1,
            ),
        )
    )
    attn_kept.inputs = lambda: (normed_one, d_qkv, attn_sent[0], grad_attn, mixed, attn_sent[1])
    attn_gain_job = Job(
        lambda d_all, normed, done: (
            jnp.sum(d_all * (normed.astype(F32) / norm_gain), axis=0),
            done,
        ),
        d_norm_one_all,
        normed_one,
        r_down,
    )
    d_norm_one = collect(d_norm_one_all, (attn_sent, attn_kept, attn_gain_job))
    r_attn = scatter(attn_kept[0])
    d_input = d_middle + norm_back(layer_in, normalizer(layer_in), norm_gain, d_norm_one)
    return (
        d_input.astype(BF16),
        (r_attn, ffn_done[0], attn_gain_job[1]),
        jnp.stack([attn_gain_job[0], ffn_gain_job[0]]),
        ffn_sent.results[1:],
    )


def both_layers(own, at_first):
    rows = own.shape[0] // 2
    low, high = (own[:rows], own[rows:])
    mine = jnp.where(at_first, low, high)
    got = swap(jnp.where(at_first, high, low))
    return (jnp.where(at_first, mine, got), jnp.where(at_first, got, mine))


def own_layer(first, second, at_first):
    mine = jnp.where(at_first, first, second)
    got = swap(jnp.where(at_first, second, first))
    return jnp.concatenate([jnp.where(at_first, mine, got), jnp.where(at_first, got, mine)], axis=0)


def gather(shard):
    return lax.all_gather(shard, ("dp", "section"), axis=0, tiled=True)


def gather_small(piece):
    return gather_direct(piece).transpose(1, 0, 2).reshape(piece.shape[0], -1)


def reduce_small(rows):
    for axis in ("tensor", "dp"):
        count = lax.axis_size(axis)
        if axis == "tensor":
            parts = rows.reshape(rows.shape[0], lax.axis_size("dp"), count, -1).transpose(2, 0, 1, 3)
        else:
            parts = rows.transpose(1, 0, 2)
        me = lax.axis_index(axis)
        rows = lax.dynamic_index_in_dim(parts, me, 0, keepdims=False)
        for k in range(1, count):
            part = lax.dynamic_index_in_dim(parts, (me + k) % count, 0, keepdims=False)
            rows = rows + turn(part, axis, k)
    return rows + swap(rows)


def local(
    tokens_in,
    cotangent,
    lengths,
    attn_gain,
    w_query,
    w_key,
    w_value,
    w_out,
    ffn_gain,
    w_gate,
    w_up,
    w_down,
):
    at_first = lax.axis_index("section") == 0
    rows = tokens_in.shape[1]
    q_cols, kv_cols, units = (w_query.shape[2], w_key.shape[2], w_gate.shape[2])
    tokens = jnp.where(at_first, tokens_in[0], tokens_in[1])
    upstream = jnp.where(at_first, cotangent[0], cotangent[1])
    own_gains = jnp.concatenate([attn_gain, ffn_gain], axis=0)
    attn_rows = jnp.concatenate([w_query[0], w_key[0], w_value[0], w_out[0].T], axis=1)
    attn_rows, tokens = barrier(attn_rows, tokens)
    attn_parts = both_layers(attn_rows, at_first)

    def collect_gains(own):
        other = swap(own)
        own, other = (jnp.where(at_first, own, other), jnp.where(at_first, other, own))
        return (gather_small(jnp.concatenate([own, other])).astype(F32),)

    def prepare_ffn(gate, up, down):
        parts = both_layers(jnp.concatenate([gate, up, down.T], axis=1), at_first)
        return (parts[0][:, : 2 * units], parts[0][:, 2 * units :], parts[1])

    gains_job = Job(collect_gains, own_gains)
    prepare = Job(prepare_ffn, w_gate[0], w_up[0], w_down[0])
    tokens_all = spread(tokens, (prepare, gains_job))
    gains = gains_job[0]
    tokens_all, upstream = barrier(tokens_all, upstream)
    upstream_ring = SpreadRing(upstream)
    geo = geometry(jnp.where(at_first, lengths[0, 0], lengths[1, 0]), rows)
    tokens_all = tokens_all.astype(F32)
    layer_in = tokens.astype(F32)
    normed_one = (tokens_all * normalizer(tokens_all) * gains[0]).astype(BF16)

    def whole_down(half):
        got = swap(half)
        return (
            jnp.where(
                at_first, jnp.stack([half, got], axis=1), jnp.stack([got, half], axis=1)
            ).reshape(-1, half.shape[-1]),
        )

    w_attn, down_part, ffn_part = barrier(gather(attn_parts[0]), prepare[1], prepare[0])
    w_attns = [w_attn]
    w_ffns = [gather(ffn_part)]
    down_job = Job(whole_down, gather_direct(down_part))
    w_attns.append(gather(attn_parts[1]))
    w_ffns.append(gather(prepare[2]))
    layers = []
    for layer in range(2):
        norm_gain, ffn_gain = (gains[2 * layer], gains[2 * layer + 1])
        w_attn, w_ffn = (w_attns[layer], w_ffns[layer])
        if layer:
            normed_one = spread((layer_in * normalizer(layer_in) * norm_gain).astype(BF16))
        out_term, *attn_kept = upstream_ring.run(
            lambda normed, w: attend(normed, geo, w, kv_cols), normed_one, w_attn
        )
        middle = layer_in + collect(out_term)
        normed_two = spread(
            (middle * normalizer(middle) * ffn_gain).astype(BF16), () if layer else (None, down_job)
        )
        w_down_all = w_ffn if layer else down_job[0]
        gate_up, hidden = upstream_ring.run(
            lambda normed, w: feed(normed, w, units), normed_two, w_ffn
        )
        kept = (*attn_kept, middle, normed_two, gate_up, hidden)
        weights = (norm_gain, ffn_gain, w_attn, w_ffn, w_down_all)
        layers.append((kept, weights, layer_in, normed_one))
        if layer == 0:
            first_out = (middle + collect(contract(hidden, w_down_all[:, -units:], 1, 1))).astype(BF16)
            layer_in = first_out.astype(F32)
    upstream_all = upstream_ring.finish()
    out_ring = CollectRing(contract(hidden, w_down_all[:, -units:], 1, 1))

    def back(layer, grad_all, grad, arriving):
        kept, weights, layer_in, normed_one = layers[layer]
        return backward(
            kept,
            grad_all,
            grad.astype(F32),
            geo,
            weights,
            at_first,
            layer_in,
            normed_one,
            out_ring,
            arriving,
        )

    d_second, second_reduced, second_gains, _ = back(1, upstream_all, upstream, ())
    d_first, first_reduced, first_gains, second_attn = back(
        0, spread(d_second), d_second, second_reduced[:1]
    )
    second_out = (middle + out_ring.finish()).astype(BF16)
    second_reduced = (second_attn[0], *second_reduced[1:])
    g_attn, g_ffn, g_down = (
        own_layer(first, second, at_first).astype(F32)
        for first, second in zip(first_reduced, second_reduced)
    )
    g_gains = reduce_small(jnp.concatenate([first_gains, second_gains]))
    gain_own = jnp.where(at_first, g_gains[:2], g_gains[2:])
    results = (first_out, second_out)
    input_grads = (d_first, d_second)

    def by_layer(first, second):
        mine = jnp.where(at_first, first, second)
        got = swap(jnp.where(at_first, second, first))
        return jnp.stack([jnp.where(at_first, mine, got), jnp.where(at_first, got, mine)])

    section_out = by_layer(results[0], results[1])
    input_grad = by_layer(input_grads[0], input_grads[1])
    qkv = q_cols + 2 * kv_cols
    return (
        section_out[None],
        input_grad[None],
        gain_own[0][None],
        g_attn[:, :q_cols][None],
        g_attn[:, q_cols : q_cols + kv_cols][None],
        g_attn[:, q_cols + kv_cols : qkv][None],
        g_attn[:, qkv:].T[None],
        gain_own[1][None],
        g_ffn[:, :units][None],
        g_ffn[:, units:][None],
        g_down.T[None],
    )


def solution(mesh):
    return jax.shard_map(
        local,
        mesh=mesh,
        in_specs=(
            P(None, ("dp", "tensor"), None),
            P(None, ("dp", "tensor"), None),
            P(None, "dp", None),
            P("section", "dp"),
            P("section", "dp", "tensor"),
            P("section", "dp", "tensor"),
            P("section", "dp", "tensor"),
            P("section", "tensor", "dp"),
            P("section", "dp"),
            P("section", "dp", "tensor"),
            P("section", "dp", "tensor"),
            P("section", "tensor", "dp"),
        ),
        out_specs=(
            P("section", None, ("dp", "tensor"), None),
            P("section", None, ("dp", "tensor"), None),
            P("section", ("dp", "tensor")),
            P("section", "dp", "tensor"),
            P("section", "dp", "tensor"),
            P("section", "dp", "tensor"),
            P("section", "tensor", "dp"),
            P("section", ("dp", "tensor")),
            P("section", "dp", "tensor"),
            P("section", "dp", "tensor"),
            P("section", "tensor", "dp"),
        ),
        check_vma=False,
    )
```

time: 1720 us -> 810 us (0.47)
  waiting for transfers between devices: 1170 us -> 492 us
  matrix products: 292 us -> 115 us
  blocking collectives: 110 us -> 0 us
  local copies, waits for them, and re-layouts: 23.2 us -> 46.2 us
  starting transfers between devices: 10.5 us -> 30 us
    all_gather x17 -> x4, waiting for transfers between devices: 639 us -> 22.8 us  [gather(): return lax.all_gather(shard, ('dp', 'section'), axis=0, tiled=True)]
    reduce_scatter x19 -> x6, waiting for transfers between devices: 525 us -> 33.6 us  [scatter(): return lax.psum_scatter(half, 'dp', scatter_dimension=0, tiled=True)]
    ppermute x4 -> x78, waiting for transfers between devices: 7.24 us -> 434 us  [the longest x60 425 us: turn(): lax.ppermute(value, axis, [(i, (i + steps) % count) for i in range(count)])]
    dot_general x42 -> x24, matrix products: 171 us -> 70.5 us  [contract(): lax.dot_general(left, right, (((left_dim,), (right_dim,)), ((), ())), pre...]
    dot_general x39 -> x8, matrix products: 120 us -> 44.4 us  [the longest x2 17.5 us: feed(): jnp.dot(normed_two, w_ffn[:, :2 * units], preferred_element_type=F32)]
    unnamed x1 -> x0, blocking collectives: 75.7 us -> none
    all_gather x4 -> x0, blocking collectives: 34.7 us -> none  [the longest x1 9.64 us: gather_weights(): lax.all_gather(local_params[0], 'dp', axis=0, tiled=True)]
    ppermute x4 -> x78, starting transfers between devices: 5.9 us -> 29.4 us  [the longest x60 25.1 us: turn(): lax.ppermute(value, axis, [(i, (i + steps) % count) for i in range(count)])]
  transfers between devices with their start and end apart: 40 -> 88, of which waited for: 34 -> 64; matrix products, arithmetic and copies ran while one was open for 11% -> 24% of each run, Pallas kernels for 0% -> 2%
where the time goes in v1:
time: 810 us; the launch traced here: 800 us
  waiting for transfers between devices  492 us (61%)
  matrix products  115 us (14%)
  other arithmetic  83.9 us (10%)
  local copies, waits for them, and re-layouts  46.2 us (6%)
  starting transfers between devices  30 us (4%)
  Pallas kernels  17 us (2%)
  between operations  16.5 us (2%)
    ppermute x60, waiting for transfers between devices, turn(): lax.ppermute(value, axis, [(i, (i + steps) % count) for i in range(count)])  425 us
    dot_general x24, matrix products, contract(): lax.dot_general(left, right, (((left_dim,), (right_dim,)), ((), ())), pre...  70.5 us
    reduce_scatter x6, waiting for transfers between devices, scatter(): return lax.psum_scatter(half, 'dp', scatter_dimension=0, tiled=True)  33.6 us
    ppermute x60, starting transfers between devices, turn(): lax.ppermute(value, axis, [(i, (i + steps) % count) for i in range(count)])  25.1 us
    unnamed x181, local copies, waits for them, and re-layouts  25 us
    all_gather x4, waiting for transfers between devices, gather(): return lax.all_gather(shard, ('dp', 'section'), axis=0, tiled=True)  22.8 us
    dot_general x2, matrix products, feed(): jnp.dot(normed_two, w_ffn[:, :2 * units], preferred_element_type=F32)  17.5 us
  transfers between devices with their start and end apart: 88, of which 64 were waited for; matrix products, arithmetic and copies ran while one was open for 24% of the time, Pallas kernels for 2%

profile of v1, /device:TPU:0, one launch (start us, length us, event | category | flops | bytes accessed | tf_op | source)
XLA Modules:
  0.0 800.0 jit_solution(12261424142197321246)
XLA Ops:
  35.3 22.8 %all-gather.5.cloned.1.call-done = bf16[2048,1152]{1,0:T(8,128)(2,1)} async-done(((bf16[256,1152]{1,0:T(8,128)(2,1)}), bf16[2048,1152]{1,0:T(8,128)(2,1)}) %all-gather.5.cloned.1.call-update) | async-done | bytes 4718608 | tf_op jit(solution)/shard_map/all_gather | solution.py:404
  75.6 12.2 %collective-permute-done.7 = bf16[96,2048]{1,0:T(8,128)(2,1)S(1)} collective-permute-done((bf16[96,2048]{1,0:T(8,128)(2,1)S(1)}, bf16[96,2048]{1,0:T(8,128)(2,1)S(1)}, u32[]{:S(2)}, u32[]{:S(2)}) %collective-permute-start.7) | collective-permute-done | bytes 393248 | tf_op jit(solution)/shard_map/ppermute | solution.py:22
  124.5 12.9 %collective-permute-done.15 = bf16[256,1408]{1,0:T(8,128)(2,1)S(1)} collective-permute-done((bf16[256,1408]{1,0:T(8,128)(2,1)S(1)}, bf16[256,1408]{1,0:T(8,128)(2,1)S(1)}, u32[]{:S(2)}, u32[]{:S(2)}) %collective-permute-start.15) | collective-permute-done | bytes 720928 | tf_op jit(solution)/shard_map/ppermute | solution.py:22
  138.5 13.0 %collective-permute-done.16 = bf16[256,1408]{1,0:T(8,128)(2,1)S(1)} collective-permute-done((bf16[256,1408]{1,0:T(8,128)(2,1)S(1)}, bf16[256,1408]{1,0:T(8,128)(2,1)S(1)}, u32[]{:S(2)}, u32[]{:S(2)}) %collective-permute-start.16) | collective-permute-done | bytes 720928 | tf_op jit(solution)/shard_map/ppermute | solution.py:22
  165.0 12.5 %collective-permute-done.19 = bf16[96,2048]{1,0:T(8,128)(2,1)S(1)} collective-permute-done((bf16[96,2048]{1,0:T(8,128)(2,1)S(1)}, bf16[96,2048]{1,0:T(8,128)(2,1)S(1)}, u32[]{:S(2)}, u32[]{:S(2)}) %collective-permute-start.19) | collective-permute-done | bytes 393248 | tf_op jit(solution)/shard_map/ppermute | solution.py:22
  193.2 10.6 %collective-permute-done.21 = bf16[96,2048]{1,0:T(8,128)(2,1)S(1)} collective-permute-done((bf16[96,2048]{1,0:T(8,128)(2,1)S(1)}, bf16[96,2048]{1,0:T(8,128)(2,1)S(1)}, u32[]{:S(2)}, u32[]{:S(2)}) %collective-permute-start.21) | collective-permute-done | bytes 393248 | tf_op jit(solution)/shard_map/ppermute | solution.py:22
  204.0 9.7 %collective-permute-done.22 = bf16[96,2048]{1,0:T(8,128)(2,1)S(1)} collective-permute-done((bf16[96,2048]{1,0:T(8,128)(2,1)S(1)}, bf16[96,2048]{1,0:T(8,128)(2,1)S(1)}, u32[]{:S(2)}, u32[]{:S(2)}) %collective-permute-start.22) | collective-permute-done | bytes 393248 | tf_op jit(solution)/shard_map/ppermute | solution.py:22
  213.9 9.7 %collective-permute-done.23 = bf16[96,2048]{1,0:T(8,128)(2,1)S(1)} collective-permute-done((bf16[96,2048]{1,0:T(8,128)(2,1)S(1)}, bf16[96,2048]{1,0:T(8,128)(2,1)S(1)}, u32[]{:S(2)}, u32[]{:S(2)}) %collective-permute-start.23) | collective-permute-done | bytes 393248 | tf_op jit(solution)/shard_map/ppermute | solution.py:22
  224.1 11.3 %collective-permute-done.24 = bf16[96,2048]{1,0:T(8,128)(2,1)S(1)} collective-permute-done((bf16[96,2048]{1,0:T(8,128)(2,1)S(1)}, bf16[96,2048]{1,0:T(8,128)(2,1)S(1)}, u32[]{:S(2)}, u32[]{:S(2)}) %collective-permute-start.24) | collective-permute-done | bytes 393248 | tf_op jit(solution)/shard_map/ppermute | solution.py:22
  235.5 12.4 %collective-permute-done.25 = bf16[96,2048]{1,0:T(8,128)(2,1)S(1)} collective-permute-done((bf16[96,2048]{1,0:T(8,128)(2,1)S(1)}, bf16[96,2048]{1,0:T(8,128)(2,1)S(1)}, u32[]{:S(2)}, u32[]{:S(2)}) %collective-permute-start.25) | collective-permute-done | bytes 393248 | tf_op jit(solution)/shard_map/ppermute | solution.py:22
  247.9 11.8 %collective-permute-done.26 = bf16[96,2048]{1,0:T(8,128)(2,1)S(1)} collective-permute-done((bf16[96,2048]{1,0:T(8,128)(2,1)S(1)}, bf16[96,2048]{1,0:T(8,128)(2,1)S(1)}, u32[]{:S(2)}, u32[]{:S(2)}) %collective-permute-start.26) | collective-permute-done | bytes 393248 | tf_op jit(solution)/shard_map/ppermute | solution.py:22
  274.6 12.2 %collective-permute-done.28 = bf16[96,2048]{1,0:T(8,128)(2,1)S(1)} collective-permute-done((bf16[96,2048]{1,0:T(8,128)(2,1)S(1)}, bf16[96,2048]{1,0:T(8,128)(2,1)S(1)}, u32[]{:S(2)}, u32[]{:S(2)}) %collective-permute-start.28) | collective-permute-done | bytes 393248 | tf_op jit(solution)/shard_map/ppermute | solution.py:22
  286.9 11.2 %collective-permute-done.29 = bf16[96,2048]{1,0:T(8,128)(2,1)S(1)} collective-permute-done((bf16[96,2048]{1,0:T(8,128)(2,1)S(1)}, bf16[96,2048]{1,0:T(8,128)(2,1)S(1)}, u32[]{:S(2)}, u32[]{:S(2)}) %collective-permute-start.29) | collective-permute-done | bytes 393248 | tf_op jit(solution)/shard_map/ppermute | solution.py:22
  298.3 11.5 %collective-permute-done.30 = bf16[96,2048]{1,0:T(8,128)(2,1)S(1)} collective-permute-done((bf16[96,2048]{1,0:T(8,128)(2,1)S(1)}, bf16[96,2048]{1,0:T(8,128)(2,1)S(1)}, u32[]{:S(2)}, u32[]{:S(2)}) %collective-permute-start.30) | collective-permute-done | bytes 393248 | tf_op jit(solution)/shard_map/ppermute | solution.py:22
  375.6 13.2 %collective-permute-done.35 = bf16[96,2048]{1,0:T(8,128)(2,1)S(1)} collective-permute-done((bf16[96,2048]{1,0:T(8,128)(2,1)S(1)}, bf16[96,2048]{1,0:T(8,128)(2,1)S(1)}, u32[]{:S(2)}, u32[]{:S(2)}) %collective-permute-start.35) | collective-permute-done | bytes 393248 | tf_op jit(solution)/shard_map/ppermute | solution.py:22
  407.7 13.2 %collective-permute-done.38 = bf16[96,2048]{1,0:T(8,128)(2,1)S(1)} collective-permute-done((bf16[96,2048]{1,0:T(8,128)(2,1)S(1)}, bf16[96,2048]{1,0:T(8,128)(2,1)S(1)}, u32[]{:S(2)}, u32[]{:S(2)}) %collective-permute-start.38) | collective-permute-done | bytes 393248 | tf_op jit(solution)/shard_map/ppermute | solution.py:22
  447.5 19.0 %reduce-scatter.7.cloned.1.call-done = bf16[256,2816]{1,0:T(8,128)(2,1)} async-done(((bf16[1024,2816]{1,0:T(8,128)(2,1)}), bf16[256,2816]{1,0:T(8,128)(2,1)}) %reduce-scatter.7.cloned.1.call-update) | async-done | bytes 1441808 | tf_op jit(solution)/shard_map/reduce_scatter | solution.py:303
  495.6 12.9 %collective-permute-done.44 = bf16[96,2048]{1,0:T(8,128)(2,1)S(1)} collective-permute-done((bf16[96,2048]{1,0:T(8,128)(2,1)S(1)}, bf16[96,2048]{1,0:T(8,128)(2,1)S(1)}, u32[]{:S(2)}, u32[]{:S(2)}) %collective-permute-start.44) | collective-permute-done | bytes 393248 | tf_op jit(solution)/shard_map/ppermute | solution.py:22
  537.5 10.2 %collective-permute-done.49 = bf16[96,2048]{1,0:T(8,128)(2,1)S(1)} collective-permute-done((bf16[96,2048]{1,0:T(8,128)(2,1)S(1)}, bf16[96,2048]{1,0:T(8,128)(2,1)S(1)}, u32[]{:S(2)}, u32[]{:S(2)}) %collective-permute-start.49) | collective-permute-done | bytes 393248 | tf_op jit(solution)/shard_map/ppermute | solution.py:22
  547.7 9.8 %collective-permute-done.50 = bf16[96,2048]{1,0:T(8,128)(2,1)S(1)} collective-permute-done((bf16[96,2048]{1,0:T(8,128)(2,1)S(1)}, bf16[96,2048]{1,0:T(8,128)(2,1)S(1)}, u32[]{:S(2)}, u32[]{:S(2)}) %collective-permute-start.50) | collective-permute-done | bytes 393248 | tf_op jit(solution)/shard_map/ppermute | solution.py:22
  592.3 13.2 %collective-permute-done.54 = bf16[96,2048]{1,0:T(8,128)(2,1)S(1)} collective-permute-done((bf16[96,2048]{1,0:T(8,128)(2,1)S(1)}, bf16[96,2048]{1,0:T(8,128)(2,1)S(1)}, u32[]{:S(2)}, u32[]{:S(2)}) %collective-permute-start.54) | collective-permute-done | bytes 393248 | tf_op jit(solution)/shard_map/ppermute | solution.py:22
  625.9 13.1 %collective-permute-done.57 = bf16[96,2048]{1,0:T(8,128)(2,1)} collective-permute-done((bf16[96,2048]{1,0:T(8,128)(2,1)}, bf16[96,2048]{1,0:T(8,128)(2,1)}, u32[]{:S(2)}, u32[]{:S(2)}) %collective-permute-start.57) | collective-permute-done | bytes 393248 | tf_op jit(solution)/shard_map/ppermute | solution.py:22
  668.0 14.6 %reduce-scatter.13.cloned.1.call-done = bf16[256,2816]{1,0:T(8,128)(2,1)} async-done(((bf16[1024,2816]{1,0:T(8,128)(2,1)}), bf16[256,2816]{1,0:T(8,128)(2,1)}) %reduce-scatter.13.cloned.1.call-update) | async-done | bytes 1441808 | tf_op jit(solution)/shard_map/reduce_scatter | solution.py:303
  714.7 11.1 %collective-permute-done.62 = bf16[96,2048]{1,0:T(8,128)(2,1)S(1)} collective-permute-done((bf16[96,2048]{1,0:T(8,128)(2,1)S(1)}, bf16[96,2048]{1,0:T(8,128)(2,1)S(1)}, u32[]{:S(2)}, u32[]{:S(2)}) %collective-permute-start.62) | collective-permute-done | bytes 393248 | tf_op jit(solution)/shard_map/ppermute | solution.py:22
  (532 shorter events, 479.1 us)
Async XLA Ops:
  7.2 51.0 %all-gather.5.cloned.1.call-start = ((), (), s32[]{:S(2)}) async-start(), calls=%async_computation.6 | async-start | bytes 5308416 | tf_op jit(solution)/shard_map/all_gather | solution.py:404
  16.4 162.3 %all-gather.7.cloned.1.call-start = ((), (), s32[]{:S(2)}) async-start(), calls=%async_computation.7 | async-start | bytes 12976128 | tf_op jit(solution)/shard_map/all_gather | solution.py:404
  20.9 14.4 %collective-permute-start = (bf16[96,2048]{1,0:T(8,128)(2,1)S(1)}, bf16[96,2048]{1,0:T(8,128)(2,1)S(1)}, u32[]{:S(2)}, u32[]{:S(2)}) collective-permute-start(bf16[96,2048]{1,0:T(8,128)(2,1)S(1)} %select_bitcast_fusion.5), channel_id=1, source_target_pairs={{0,1},{1,2},{2,3},{3,0},{4,5},{5,6},{6,7},{7,4},{8,9},{9,10},{10,1... | collective-permute-start | bytes 1179656 | tf_op jit(solution)/shard_map/ppermute | solution.py:22
  58.2 202.9 %all-gather.9.cloned.1.call-start = ((), (), s32[]{:S(2)}) async-start(), calls=%async_computation.8 | async-start | bytes 5308416 | tf_op jit(solution)/shard_map/all_gather | solution.py:404
  58.9 274.1 %all-gather.11.cloned.1.call-start = ((), (), s32[]{:S(2)}) async-start(), calls=%async_computation.9 | async-start | bytes 19464192 | tf_op jit(solution)/shard_map/all_gather | solution.py:404
  59.5 406.9 %reduce-scatter.7.cloned.1.call-start = ((), (), s32[]{:S(2)}) async-start(), calls=%async_computation.10 | async-start | bytes 7208960 | tf_op jit(solution)/shard_map/reduce_scatter | solution.py:303
  89.0 33.3 %collective-permute-start.14 = (bf16[256,1408]{1,0:T(8,128)(2,1)S(1)}, bf16[256,1408]{1,0:T(8,128)(2,1)S(1)}, u32[]{:S(2)}, u32[]{:S(2)}) collective-permute-start(bf16[256,1408]{1,0:T(8,128)(2,1)S(1)} %copy-done.38), channel_id=1, source_target_pairs={{0,4},{4,8},{8,12},{12,0},{1,5},{5,9},{9,13},{13,1},{2,6},{6,10},{... | collective-permute-start | bytes 2162696 | tf_op jit(solution)/shard_map/ppermute | solution.py:22
  90.5 46.9 %collective-permute-start.15 = (bf16[256,1408]{1,0:T(8,128)(2,1)S(1)}, bf16[256,1408]{1,0:T(8,128)(2,1)S(1)}, u32[]{:S(2)}, u32[]{:S(2)}) collective-permute-start(bf16[256,1408]{1,0:T(8,128)(2,1)S(1)} %copy-done.38), channel_id=1, source_target_pairs={{0,8},{4,12},{8,0},{12,4},{1,9},{5,13},{9,1},{13,5},{2,10},{6,14},... | collective-permute-start | bytes 2162696 | tf_op jit(solution)/shard_map/ppermute | solution.py:22
  91.1 60.4 %collective-permute-start.16 = (bf16[256,1408]{1,0:T(8,128)(2,1)S(1)}, bf16[256,1408]{1,0:T(8,128)(2,1)S(1)}, u32[]{:S(2)}, u32[]{:S(2)}) collective-permute-start(bf16[256,1408]{1,0:T(8,128)(2,1)S(1)} %copy-done.38), channel_id=1, source_target_pairs={{0,12},{4,0},{8,4},{12,8},{1,13},{5,1},{9,5},{13,9},{2,14},{6,2},{... | collective-permute-start | bytes 2162696 | tf_op jit(solution)/shard_map/ppermute | solution.py:22
  354.5 16.9 %collective-permute-start.34 = (bf16[96,2048]{1,0:T(8,128)(2,1)S(1)}, bf16[96,2048]{1,0:T(8,128)(2,1)S(1)}, u32[]{:S(2)}, u32[]{:S(2)}) collective-permute-start(bf16[96,2048]{1,0:T(8,128)(2,1)S(1)} %slice.1054), channel_id=1, source_target_pairs={{0,1},{1,2},{2,3},{3,0},{4,5},{5,6},{6,7},{7,4},{8,9},{9,10},{10,1... | collective-permute-start | bytes 1179656 | tf_op jit(solution)/shard_map/ppermute | solution.py:22
  402.6 120.6 %reduce-scatter.9.cloned.1.call-start = ((), (), s32[]{:S(2)}) async-start(), calls=%async_computation.11 | async-start | bytes 3604480 | tf_op jit(solution)/shard_map/reduce_scatter | solution.py:303
  470.0 116.0 %reduce-scatter.11.cloned.1.call-start = ((), (), s32[]{:S(2)}) async-start(), calls=%async_computation.12 | async-start | bytes 2949120 | tf_op jit(solution)/shard_map/reduce_scatter | solution.py:303
  494.1 14.4 %collective-permute-start.45 = (bf16[1024,640]{1,0:T(8,128)(2,1)S(1)}, bf16[1024,640]{1,0:T(8,128)(2,1)S(1)}, u32[]{:S(2)}, u32[]{:S(2)}) collective-permute-start(bf16[1024,640]{1,0:T(8,128)(2,1)S(1)} %convolution_convert_fusion.5), channel_id=1, source_target_pairs={{0,16},{16,0},{1,17},{17,1},{2,18},{18,2},{3,19},{19,3},{4,20},{20... | collective-permute-start | bytes 3932168 | tf_op jit(solution)/shard_map/ppermute | solution.py:26
  523.3 159.3 %reduce-scatter.13.cloned.1.call-start = ((), (), s32[]{:S(2)}) async-start(), calls=%async_computation.13 | async-start | bytes 7208960 | tf_op jit(solution)/shard_map/reduce_scatter | solution.py:303
  568.3 16.1 %collective-permute-start.52 = (bf16[96,2048]{1,0:T(8,128)(2,1)S(1)}, bf16[96,2048]{1,0:T(8,128)(2,1)S(1)}, u32[]{:S(2)}, u32[]{:S(2)}) collective-permute-start(bf16[96,2048]{1,0:T(8,128)(2,1)S(1)} %fusion.58), channel_id=1, source_target_pairs={{0,1},{1,2},{2,3},{3,0},{4,5},{5,6},{6,7},{7,4},{8,9},{9,10},{10,1... | collective-permute-start | bytes 1179656 | tf_op jit(solution)/shard_map/ppermute | solution.py:22
  619.4 128.1 %reduce-scatter.15.cloned.1.call-start = ((), (), s32[]{:S(2)}) async-start(), calls=%async_computation.14 | async-start | bytes 3604480 | tf_op jit(solution)/shard_map/reduce_scatter | solution.py:303
  625.3 13.6 %collective-permute-start.58 = (bf16[1024,1408]{1,0:T(8,128)(2,1)}, bf16[1024,1408]{1,0:T(8,128)(2,1)}, u32[]{:S(2)}, u32[]{:S(2)}) collective-permute-start(bf16[1024,1408]{1,0:T(8,128)(2,1)} %convolution_convert_fusion.2), channel_id=1, source_target_pairs={{0,16},{16,0},{1,17},{17,1},{2,18},{18,2},{3,19},{19,3},{4,20},{20... | collective-permute-start | bytes 8650760 | tf_op jit(solution)/shard_map/ppermute | solution.py:26
  625.3 13.6 %collective-permute-start.57 = (bf16[96,2048]{1,0:T(8,128)(2,1)}, bf16[96,2048]{1,0:T(8,128)(2,1)}, u32[]{:S(2)}, u32[]{:S(2)}) collective-permute-start(bf16[96,2048]{1,0:T(8,128)(2,1)} %add_convert_fusion.8), channel_id=1, source_target_pairs={{0,1},{1,2},{2,3},{3,0},{4,5},{5,6},{6,7},{7,4},{8,9},{9,10},{10,1... | collective-permute-start | bytes 1179656 | tf_op jit(solution)/shard_map/ppermute | solution.py:22
  686.4 25.1 %collective-permute-start.53 = (bf16[96,2048]{1,0:T(8,128)(2,1)}, bf16[96,2048]{1,0:T(8,128)(2,1)S(1)}, u32[]{:S(2)}, u32[]{:S(2)}) collective-permute-start(bf16[96,2048]{1,0:T(8,128)(2,1)} %get-tuple-element.422), channel_id=1, source_target_pairs={{0,16},{16,0},{1,17},{17,1},{2,18},{18,2},{3,19},{19,3},{4,20},{20... | collective-permute-start | bytes 1179656 | tf_op jit(solution)/shard_map/ppermute | solution.py:26
  686.4 89.5 %reduce-scatter.17.cloned.1.call-start = ((), (), s32[]{:S(2)}) async-start(), calls=%async_computation.15 | async-start | bytes 2949120 | tf_op jit(solution)/shard_map/reduce_scatter | solution.py:303
  709.6 16.2 %collective-permute-start.64 = (bf16[1024,512]{1,0:T(8,128)(2,1)S(1)}, bf16[1024,512]{1,0:T(8,128)(2,1)S(1)}, u32[]{:S(2)}, u32[]{:S(2)}) collective-permute-start(bf16[1024,512]{1,0:T(8,128)(2,1)S(1)} %convolution_convert_fusion.6), channel_id=1, source_target_pairs={{0,16},{16,0},{1,17},{17,1},{2,18},{18,2},{3,19},{19,3},{4,20},{20... | collective-permute-start | bytes 3145736 | tf_op jit(solution)/shard_map/ppermute | solution.py:26
  711.4 14.4 %collective-permute-start.63 = (bf16[1024,640]{1,0:T(8,128)(2,1)S(1)}, bf16[1024,640]{1,0:T(8,128)(2,1)S(1)}, u32[]{:S(2)}, u32[]{:S(2)}) collective-permute-start(bf16[1024,640]{1,0:T(8,128)(2,1)S(1)} %convolution_convert_fusion.4), channel_id=1, source_target_pairs={{0,16},{16,0},{1,17},{17,1},{2,18},{18,2},{3,19},{19,3},{4,20},{20... | collective-permute-start | bytes 3932168 | tf_op jit(solution)/shard_map/ppermute | solution.py:26
  714.7 15.9 %collective-permute-start.76 = (bf16[256,2816]{1,0:T(8,128)(2,1)}, bf16[256,2816]{1,0:T(8,128)(2,1)}, u32[]{:S(2)}, u32[]{:S(2)}) collective-permute-start(bf16[256,2816]{1,0:T(8,128)(2,1)} %broadcast_select_fusion.6), channel_id=1, source_target_pairs={{0,16},{16,0},{1,17},{17,1},{2,18},{18,2},{3,19},{19,3},{4,20},{20... | collective-permute-start | bytes 4325384 | tf_op jit(solution)/shard_map/ppermute | solution.py:26
  760.3 17.9 %collective-permute-start.77 = (bf16[256,1408]{1,0:T(8,128)(2,1)}, bf16[256,1408]{1,0:T(8,128)(2,1)}, u32[]{:S(2)}, u32[]{:S(2)}) collective-permute-start(bf16[256,1408]{1,0:T(8,128)(2,1)} %broadcast_select_fusion.10), channel_id=1, source_target_pairs={{0,16},{16,0},{1,17},{17,1},{2,18},{18,2},{3,19},{19,3},{4,20},{20... | collective-permute-start | bytes 2162696 | tf_op jit(solution)/shard_map/ppermute | solution.py:26
  (149 other events, 1811.3 us)
Sparse Core Ops, SparseCore 0:
  16.6 41.5 all-gather.4
  60.0 97.7 all-gather.6
  160.3 36.7 all-gather.8
  199.4 92.0 all-gather.10
  402.8 63.6 reduce-scatter.6
  470.1 41.5 reduce-scatter.8
  523.4 37.8 reduce-scatter.10
  619.5 63.0 reduce-scatter.12
  686.6 41.4 reduce-scatter.14
  740.0 34.6 reduce-scatter.16

commit v2 on v1

--- a/solution.py
+++ b/solution.py
@@ -14,7 +14,7 @@
 F32 = jnp.float32
 LANES = 128
 SCALE = HEAD ** (-0.5)
-VMEM_BYTES = 24 * 2**20
+VMEM_BYTES = 28 * 2**20
 
 
 def turn(value, axis, steps):
@@ -61,8 +61,8 @@
 
 
 class Job:
-    def __init__(self, fn, *inputs):
-        self.fn, self.inputs, self.results = (fn, inputs, None)
+    def __init__(self, fn, *inputs, held=()):
+        self.fn, self.inputs, self.held, self.results = (fn, inputs, held, None)
 
     def __getitem__(self, which):
         return self.results[which]
@@ -73,9 +73,9 @@
         return turn(value, "tensor", 1)
     inputs = job.inputs() if callable(job.inputs) else job.inputs
     value, *inputs = barrier(value, *inputs)
-    recv = turn(value, "tensor", 1)
-    recv, *results = barrier(recv, *job.fn(*inputs))
-    job.results = results
+    results = job.fn(*inputs)
+    recv, *values = barrier(turn(value, "tensor", 1), *results, *job.held)
+    job.results, job.held = (values[: len(results)], values[len(results) :])
     return recv
 
 
@@ -93,7 +93,7 @@
     total = blocks[1 % count]
     for k in range(count - 1):
         recv = step(total.astype(BF16), jobs[k] if k < len(jobs) else None)
-        total = recv.astype(F32) + blocks[(k + 2) % count]
+        total = recv.astype(F32) + blocks[(k + 2) % count].astype(F32)
     return total
 
 
@@ -136,20 +136,12 @@
         super().__init__(self.total.astype(BF16))
 
     def accept(self, recv):
-        self.total = recv.astype(F32) + self.blocks[(self.taken + 2) % self.count]
+        block = self.blocks[(self.taken + 2) % self.count]
+        self.total = recv.astype(F32) + block.astype(F32)
         self.value = self.total.astype(BF16)
 
     def result(self):
         return self.total
-
-
-def gather_direct(piece):
-    count, me = (lax.axis_size("dp"), lax.axis_index("dp"))
-    whole = jnp.zeros((count,) + piece.shape, piece.dtype)
-    for k in range(count):
-        part = turn(piece, "dp", k) if k else piece
-        whole = lax.dynamic_update_index_in_dim(whole, part, (me - k) % count, 0)
-    return whole
 
 
 def normalizer(rows):
@@ -199,9 +191,8 @@
     lse_ref[...] = jnp.concatenate(log_totals, axis=1)
 
 
-def attend(normed_one, geo, w_attn, kv_cols):
+def attend(normed_one, geo, w_attn, q_cols, kv_cols):
     group = normed_one.shape[0]
-    q_cols = w_attn.shape[1] // 2 - kv_cols
     both = q_cols + 2 * kv_cols
     qkv = jnp.dot(normed_one, w_attn[:, :both], preferred_element_type=F32)
     rotated, mixed, log_total = pl.pallas_call(
@@ -213,7 +204,8 @@
         ),
         compiler_params=pltpu.CompilerParams(vmem_limit_bytes=VMEM_BYTES),
     )(qkv, *geo)
-    return (contract(mixed, w_attn[:, both:], 1, 1), rotated, log_total, mixed)
+    out_term = contract(mixed, w_attn[:, both : both + q_cols], 1, 1).astype(BF16)
+    return (out_term, rotated, log_total, mixed)
 
 
 def attend_back_kernel(d_mixed_ref, rot_ref, lse_ref, table_ref, bias_ref, out_ref):
@@ -250,15 +242,19 @@
     out_ref[:, q_cols:] = d_kv.astype(BF16)
 
 
-def attend_back(grad_attn, geo, w_attn, rotated, log_total):
+def attend_back(grad_attn, geo, w_attn, at_first, rotated, log_total):
+    other_attn = swap(core_half(grad_attn, at_first, False))
     both = rotated.shape[1]
-    d_mixed = jnp.dot(grad_attn, w_attn[:, both:], preferred_element_type=F32).astype(BF16)
+    q_cols = log_total.shape[1] * HEAD
+    w_out = w_attn[:, both : both + q_cols]
+    d_mixed = jnp.dot(grad_attn, w_out, preferred_element_type=F32).astype(BF16)
     d_qkv = pl.pallas_call(
         attend_back_kernel,
         out_shape=jax.ShapeDtypeStruct(rotated.shape, BF16),
         compiler_params=pltpu.CompilerParams(vmem_limit_bytes=VMEM_BYTES),
     )(d_mixed, rotated, log_total, *geo)
-    return (d_qkv, contract(d_qkv, w_attn[:, :both], 1, 1))
+    d_norm_one = contract(d_qkv, w_attn[:, :both], 1, 1).astype(BF16)
+    return (d_qkv, swap(d_qkv), other_attn, d_norm_one)
 
 
 def feed(normed_two, w_ffn, units):
@@ -267,15 +263,16 @@
     return (gate_up, hidden)
 
 
-def feed_back(grad_feed, gate_up, w_ffn, w_down):
+def feed_back(grad_feed, gate_up, w_ffn):
     units = gate_up.shape[1] // 2
-    d_hidden = jnp.dot(grad_feed, w_down[:, -units:], preferred_element_type=F32)
+    d_hidden = jnp.dot(grad_feed, w_ffn[:, 2 * units :], preferred_element_type=F32)
     gate, up = (gate_up[:, :units], gate_up[:, units:])
     sigmoid_gate = jax.nn.sigmoid(gate)
     d_up = (d_hidden * gate * sigmoid_gate).astype(BF16)
     d_gate = (d_hidden * up * sigmoid_gate * (1.0 + gate * (1.0 - sigmoid_gate))).astype(BF16)
     d_gate_up = jnp.concatenate([d_gate, d_up], axis=1)
-    return (d_gate_up, contract(d_gate_up, w_ffn[:, : 2 * units], 1, 1))
+    other = swap(d_gate_up)
+    return (d_gate_up, other, contract(d_gate_up, w_ffn[:, : 2 * units], 1, 1).astype(BF16))
 
 
 def core_half(rows, at_first, own):
@@ -290,13 +287,38 @@
     return jnp.where(at_first, low, high) if own else jnp.where(at_first, high, low)
 
 
-def sent_grad(rows, grads, at_first):
-    return swap(contract(core_half(rows, at_first, False), grads, 0, 0).astype(BF16))
-
-
-def kept_grad(rows, grads, got, at_first):
-    kept = contract(core_half(rows, at_first, True), grads, 0, 0)
-    return (kept + got.astype(F32)).astype(BF16)
+def exchange(at_first, rows, *whole):
+    return tuple(swap(core_half(x, at_first, False)) for x in rows) + tuple(map(swap, whole))
+
+
+def weight_grads_kernel(*refs):
+    *pairs, out_ref = refs
+    at = 0
+    for k in range(0, len(pairs), 4):
+        rows, other_rows, grads, other_grads = (ref[...] for ref in pairs[k : k + 4])
+        total = contract(rows, grads, 0, 0) + contract(other_rows, other_grads, 0, 0)
+        out_ref[:, at : at + total.shape[1]] = total.astype(BF16)
+        at += total.shape[1]
+
+
+def weight_grads(at_first, *pairs):
+    pairs = [(core_half(rows, at_first, True), *rest) for rows, *rest in pairs]
+    group, half = pairs[0][0].shape
+    tile = min(256, half)
+    specs = []
+    for _, _, grads, _ in pairs:
+        rows_spec = pl.BlockSpec((group, tile), lambda i: (0, i))
+        grads_spec = pl.BlockSpec((group, grads.shape[1]), lambda i: (0, 0))
+        specs += [rows_spec, rows_spec, grads_spec, grads_spec]
+    total = sum(grads.shape[1] for _, _, grads, _ in pairs)
+    return pl.pallas_call(
+        weight_grads_kernel,
+        grid=(half // tile,),
+        in_specs=specs,
+        out_specs=pl.BlockSpec((tile, total), lambda i: (i, 0)),
+        out_shape=pltpu.HBM((half, total), BF16),
+        compiler_params=pltpu.CompilerParams(vmem_limit_bytes=VMEM_BYTES),
+    )(*[x for pair in pairs for x in pair])
 
 
 def scatter(half):
@@ -310,80 +332,62 @@
 
 
 def backward(
-    kept, grad_feed, grad_result, geo, weights, at_first, layer_in, normed_one, aside, arriving
+    kept, grad_all, grad, geo, weights, at_first, others, early, aside, down_job, last
 ):
-    (rotated, log_total, mixed, middle, normed_two, gate_up, hidden) = kept
-    norm_gain, ffn_gain, w_attn, w_ffn, w_down = weights
-    d_gate_up, d_norm_two_all = aside.run(feed_back, grad_feed, gate_up, w_ffn, w_down)
-    ffn_sent = Job(
-        lambda rows, grads, *rest: (sent_grad(rows, grads, at_first), *rest),
-        normed_two,
-        d_gate_up,
-        *arriving,
-    )
-    ffn_kept = Job(lambda *given: (kept_grad(*given, at_first),))
-    ffn_kept.inputs = lambda: (normed_two, d_gate_up, ffn_sent[0])
-    down_sent = Job(lambda *given: (sent_grad(*given, at_first),), grad_feed, hidden)
-    d_norm_two = collect(d_norm_two_all, (ffn_sent, ffn_kept, down_sent))
-    r_ffn = scatter(ffn_kept[0])
-    d_middle = grad_result + norm_back(middle, normalizer(middle), ffn_gain, d_norm_two)
-    down_kept = Job(lambda *given: (kept_grad(*given, at_first),))
-    down_kept.inputs = lambda: (grad_feed, hidden, down_sent[0])
+    (layer_in, normed_one, rotated, log_total, mixed, middle, normed_two, gate_up, hidden) = kept
+    norm_gain, ffn_gain, w_attn, w_ffn = weights
+    run = aside.run if aside else lambda fn, *inputs: fn(*inputs)
+    d_gate_up, other_gate_up, d_norm_two_all = run(feed_back, grad_all, gate_up, w_ffn)
+    ffn_pair = (normed_two, others["normed_two"], d_gate_up, other_gate_up)
+    down_pair = (grad_all, others["grad_all"], hidden, others["hidden"])
+    d_norm_two_all, *ready = barrier(d_norm_two_all, *ffn_pair, *down_pair)
+    ffn_pair, down_pair = (ready[:4], ready[4:])
+
+    def grads(*given):
+        pairs = [given[k : k + 4] for k in range(0, len(given), 4)]
+        return (weight_grads(at_first, *pairs),)
+
+    if last:
+        jobs = (Job(grads, *ffn_pair, *down_pair), Job(lambda: (), held=early))
+    else:
+        jobs = (Job(grads, *ffn_pair), Job(grads, *down_pair, held=early))
+    d_norm_two = collect(d_norm_two_all, jobs)
+    early = jobs[1].held
+    reduced = [scatter(job[0]) for job in jobs if job.results]
+    d_middle = grad.astype(F32) + norm_back(middle, normalizer(middle), ffn_gain, d_norm_two)
     ffn_gain_job = Job(
-        lambda d_all, normed: (jnp.sum(d_all * (normed.astype(F32) / ffn_gain), axis=0),),
+        lambda d_all, normed: (
+            jnp.sum(d_all.astype(F32) * (normed.astype(F32) / ffn_gain), axis=0),
+        ),
         d_norm_two_all,
         normed_two,
     )
-    ffn_done = Job(lambda *given: given, r_ffn)
-    grad_attn = spread(d_middle.astype(BF16), (down_kept, ffn_gain_job, ffn_done))
-    r_down = scatter(down_kept[0])
-    d_qkv, d_norm_one_all = aside.run(
-        lambda grad_attn, w_attn, *rest: attend_back(grad_attn, geo, w_attn, *rest),
-        grad_attn,
-        w_attn,
-        rotated,
-        log_total,
-    )
-    attn_sent = Job(
-        lambda rows, grads, above, heads: (
-            sent_grad(rows, grads, at_first),
-            sent_grad(above, heads, at_first),
-        ),
-        normed_one,
-        d_qkv,
-        grad_attn,
-        mixed,
-    )
-    attn_kept = Job(
-        lambda rows, grads, got, above, heads, got_out: (
-            jnp.concatenate(
-                [
-                    kept_grad(rows, grads, got, at_first),
-                    kept_grad(above, heads, got_out, at_first),
-                ],
-                axis=1,
-            ),
-        )
-    )
-    attn_kept.inputs = lambda: (normed_one, d_qkv, attn_sent[0], grad_attn, mixed, attn_sent[1])
+    grad_attn = spread(d_middle.astype(BF16), (ffn_gain_job, down_job))
+    if down_job:
+        aside = CollectRing(down_job[0])
+    d_qkv, other_qkv, other_attn, d_norm_one_all = attend_back(
+        grad_attn, geo, w_attn, at_first, rotated, log_total
+    )
+    pairs = (
+        *(normed_one, others["normed_one"], d_qkv, other_qkv),
+        *(grad_attn, other_attn, mixed, others["mixed"]),
+    )
+    d_norm_one_all, *pairs = barrier(d_norm_one_all, *pairs)
+    attn_job = Job(grads, *pairs, held=reduced[:1] if last else ())
     attn_gain_job = Job(
-        lambda d_all, normed, done: (
-            jnp.sum(d_all * (normed.astype(F32) / norm_gain), axis=0),
-            done,
+        lambda d_all, normed: (
+            jnp.sum(d_all.astype(F32) * (normed.astype(F32) / norm_gain), axis=0),
         ),
         d_norm_one_all,
         normed_one,
-        r_down,
-    )
-    d_norm_one = collect(d_norm_one_all, (attn_sent, attn_kept, attn_gain_job))
-    r_attn = scatter(attn_kept[0])
+    )
+    ffn_done = Job(lambda: (), held=() if last else reduced[:1])
+    d_norm_one = collect(d_norm_one_all, (attn_job, attn_gain_job, ffn_done))
+    reduced[:1] = attn_job.held or ffn_done.held
+    g_attn = attn_job[0]
     d_input = d_middle + norm_back(layer_in, normalizer(layer_in), norm_gain, d_norm_one)
-    return (
-        d_input.astype(BF16),
-        (r_attn, ffn_done[0], attn_gain_job[1]),
-        jnp.stack([attn_gain_job[0], ffn_gain_job[0]]),
-        ffn_sent.results[1:],
-    )
+    gain_grads = jnp.stack([attn_gain_job[0], ffn_gain_job[0]])
+    return (d_input.astype(BF16), (scatter(g_attn), *reduced), gain_grads, early, aside)
 
 
 def both_layers(own, at_first):
@@ -402,10 +406,6 @@
 
 def gather(shard):
     return lax.all_gather(shard, ("dp", "section"), axis=0, tiled=True)
-
-
-def gather_small(piece):
-    return gather_direct(piece).transpose(1, 0, 2).reshape(piece.shape[0], -1)
 
 
 def reduce_small(rows):
@@ -442,108 +442,130 @@
     q_cols, kv_cols, units = (w_query.shape[2], w_key.shape[2], w_gate.shape[2])
     tokens = jnp.where(at_first, tokens_in[0], tokens_in[1])
     upstream = jnp.where(at_first, cotangent[0], cotangent[1])
-    own_gains = jnp.concatenate([attn_gain, ffn_gain], axis=0)
-    attn_rows = jnp.concatenate([w_query[0], w_key[0], w_value[0], w_out[0].T], axis=1)
+    gains_cols = jnp.pad(
+        jnp.concatenate([attn_gain, ffn_gain], axis=0).T, ((0, 0), (0, LANES - 2))
+    )
+    attn_rows = jnp.concatenate(
+        [w_query[0], w_key[0], w_value[0], w_out[0].T, gains_cols], axis=1
+    )
     attn_rows, tokens = barrier(attn_rows, tokens)
     attn_parts = both_layers(attn_rows, at_first)
-
-    def collect_gains(own):
-        other = swap(own)
-        own, other = (jnp.where(at_first, own, other), jnp.where(at_first, other, own))
-        return (gather_small(jnp.concatenate([own, other])).astype(F32),)
-
-    def prepare_ffn(gate, up, down):
-        parts = both_layers(jnp.concatenate([gate, up, down.T], axis=1), at_first)
-        return (parts[0][:, : 2 * units], parts[0][:, 2 * units :], parts[1])
-
-    gains_job = Job(collect_gains, own_gains)
-    prepare = Job(prepare_ffn, w_gate[0], w_up[0], w_down[0])
-    tokens_all = spread(tokens, (prepare, gains_job))
-    gains = gains_job[0]
-    tokens_all, upstream = barrier(tokens_all, upstream)
-    upstream_ring = SpreadRing(upstream)
+    prepare = Job(
+        lambda gate, up, down: both_layers(
+            jnp.concatenate([gate, up, down.T], axis=1), at_first
+        ),
+        w_gate[0],
+        w_up[0],
+        w_down[0],
+    )
+    tokens_all = spread(tokens, (prepare,))
+    first_attn = gather(attn_parts[0])
+    first_ffn = gather(prepare[0])
+    w_attns = [first_attn, gather(attn_parts[1])]
+    w_ffns = [first_ffn, gather(prepare[1])]
     geo = geometry(jnp.where(at_first, lengths[0, 0], lengths[1, 0]), rows)
     tokens_all = tokens_all.astype(F32)
     layer_in = tokens.astype(F32)
-    normed_one = (tokens_all * normalizer(tokens_all) * gains[0]).astype(BF16)
-
-    def whole_down(half):
-        got = swap(half)
-        return (
-            jnp.where(
-                at_first, jnp.stack([half, got], axis=1), jnp.stack([got, half], axis=1)
-            ).reshape(-1, half.shape[-1]),
-        )
-
-    w_attn, down_part, ffn_part = barrier(gather(attn_parts[0]), prepare[1], prepare[0])
-    w_attns = [w_attn]
-    w_ffns = [gather(ffn_part)]
-    down_job = Job(whole_down, gather_direct(down_part))
-    w_attns.append(gather(attn_parts[1]))
-    w_ffns.append(gather(prepare[2]))
     layers = []
     for layer in range(2):
-        norm_gain, ffn_gain = (gains[2 * layer], gains[2 * layer + 1])
         w_attn, w_ffn = (w_attns[layer], w_ffns[layer])
+        norm_gain, ffn_gain = (
+            w_attn[:, 2 * (q_cols + kv_cols) :][:, :2].T.astype(F32)
+        )
         if layer:
             normed_one = spread((layer_in * normalizer(layer_in) * norm_gain).astype(BF16))
-        out_term, *attn_kept = upstream_ring.run(
-            lambda normed, w: attend(normed, geo, w, kv_cols), normed_one, w_attn
+        else:
+            normed_one = (tokens_all * normalizer(tokens_all) * norm_gain).astype(BF16)
+        out_term, rotated, log_total, mixed = attend(normed_one, geo, w_attn, q_cols, kv_cols)
+        attn_swap = Job(lambda one, heads: exchange(at_first, (one,), heads), normed_one, mixed)
+        others = {}
+        grad_swap = None
+        if layer:
+            grad_swap = Job(lambda x: exchange(at_first, (x,)), upstream_all)
+        middle = layer_in + collect(out_term, (None, attn_swap, grad_swap))
+        others.update(normed_one=attn_swap[0], mixed=attn_swap[1])
+        if layer:
+            others.update(grad_all=grad_swap[0])
+        normed_two = spread((middle * normalizer(middle) * ffn_gain).astype(BF16))
+        if layer:
+            gate_up, hidden = feed(normed_two, w_ffn, units)
+        else:
+            normed_two, upstream = barrier(normed_two, upstream)
+            upstream_ring = SpreadRing(upstream)
+            upstream_ring.run(lambda: ())
+            upstream_ring.run(lambda: ())
+            gate_up, hidden = upstream_ring.run(
+                lambda normed, w: feed(normed, w, units), normed_two, w_ffn
+            )
+            upstream_all = upstream_ring.finish()
+        down_job = Job(
+            lambda hidden, w: (contract(hidden, w[:, 2 * units :], 1, 1).astype(BF16),),
+            hidden,
+            w_ffn,
         )
-        middle = layer_in + collect(out_term)
-        normed_two = spread(
-            (middle * normalizer(middle) * ffn_gain).astype(BF16), () if layer else (None, down_job)
+        if layer == 0:
+            (down_term,) = down_job.fn(*down_job.inputs)
+            ffn_swap = Job(
+                lambda two, units: exchange(at_first, (two,), units), normed_two, hidden
+            )
+            first_out = (middle + collect(down_term, (None, ffn_swap))).astype(BF16)
+            others.update(normed_two=ffn_swap[0], hidden=ffn_swap[1])
+        else:
+            others.update(
+                zip(("normed_two", "hidden"), exchange(at_first, (normed_two,), hidden))
+            )
+        kept = (
+            layer_in, normed_one, rotated, log_total, mixed, middle, normed_two, gate_up, hidden
         )
-        w_down_all = w_ffn if layer else down_job[0]
-        gate_up, hidden = upstream_ring.run(
-            lambda normed, w: feed(normed, w, units), normed_two, w_ffn
-        )
-        kept = (*attn_kept, middle, normed_two, gate_up, hidden)
-        weights = (norm_gain, ffn_gain, w_attn, w_ffn, w_down_all)
-        layers.append((kept, weights, layer_in, normed_one))
-        if layer == 0:
-            first_out = (middle + collect(contract(hidden, w_down_all[:, -units:], 1, 1))).astype(BF16)
-            layer_in = first_out.astype(F32)
-    upstream_all = upstream_ring.finish()
-    out_ring = CollectRing(contract(hidden, w_down_all[:, -units:], 1, 1))
-
-    def back(layer, grad_all, grad, arriving):
-        kept, weights, layer_in, normed_one = layers[layer]
+        layers.append((kept, (norm_gain, ffn_gain, w_attn, w_ffn), others))
+        layer_in = first_out.astype(F32)
+
+    def back(layer, grad_all, grad, early, aside, down_job):
+        kept, weights, others = layers[layer]
+        if "grad_all" not in others:
+            others["grad_all"] = exchange(at_first, (grad_all,))[0]
         return backward(
             kept,
             grad_all,
-            grad.astype(F32),
+            grad,
             geo,
             weights,
             at_first,
-            layer_in,
-            normed_one,
-            out_ring,
-            arriving,
+            others,
+            early,
+            aside,
+            down_job,
+            layer == 0,
         )
 
-    d_second, second_reduced, second_gains, _ = back(1, upstream_all, upstream, ())
-    d_first, first_reduced, first_gains, second_attn = back(
-        0, spread(d_second), d_second, second_reduced[:1]
+    d_second, (second_attn, second_ffn, second_down), second_gains, _, out_ring = back(
+        1, upstream_all, upstream, (), None, down_job
+    )
+    down_done = Job(lambda: (), held=(second_down,))
+    d_second_all = spread(d_second, (None, down_done))
+    d_first, (first_attn, first_ffn), first_gains, (second_attn,), _ = back(
+        0, d_second_all, d_second, (second_attn,), out_ring, None
     )
     second_out = (middle + out_ring.finish()).astype(BF16)
-    second_reduced = (second_attn[0], *second_reduced[1:])
-    g_attn, g_ffn, g_down = (
-        own_layer(first, second, at_first).astype(F32)
-        for first, second in zip(first_reduced, second_reduced)
-    )
+    second_ffn = jnp.concatenate([second_ffn, *down_done.held], axis=1)
     g_gains = reduce_small(jnp.concatenate([first_gains, second_gains]))
     gain_own = jnp.where(at_first, g_gains[:2], g_gains[2:])
-    results = (first_out, second_out)
-    input_grads = (d_first, d_second)
 
     def by_layer(first, second):
         mine = jnp.where(at_first, first, second)
         got = swap(jnp.where(at_first, second, first))
         return jnp.stack([jnp.where(at_first, mine, got), jnp.where(at_first, got, mine)])
 
-    section_out = by_layer(results[0], results[1])
-    input_grad = by_layer(input_grads[0], input_grads[1])
+    section_out = by_layer(first_out, second_out)
+    input_grad = by_layer(d_first, d_second)
+    g_ffn = own_layer(first_ffn, second_ffn, at_first).astype(F32)
+    g_gate, g_up, g_down = (
+        g_ffn[:, :units], g_ffn[:, units : 2 * units], g_ffn[:, 2 * units :].T
+    )
+    first_attn, gain_own, section_out, input_grad, g_gate, g_up, g_down = barrier(
+        first_attn, gain_own, section_out, input_grad, g_gate, g_up, g_down
+    )
+    g_attn = own_layer(first_attn, second_attn, at_first).astype(F32)
     qkv = q_cols + 2 * kv_cols
     return (
         section_out[None],
@@ -554,9 +576,9 @@
         g_attn[:, q_cols + kv_cols : qkv][None],
         g_attn[:, qkv:].T[None],
         gain_own[1][None],
-        g_ffn[:, :units][None],
-        g_ffn[:, units:][None],
-        g_down.T[None],
+        g_gate[None],
+        g_up[None],
+        g_down[None],
     )
 
 

time: 810 us -> 742 us (0.916)
  waiting for transfers between devices: 492 us -> 438 us
  Pallas kernels: 17 us -> 52.3 us
  matrix products: 115 us -> 87.2 us
  other arithmetic: 83.9 us -> 69.3 us
    pallas_call x0 -> x5, Pallas kernels: none -> 35.3 us  [weight_grads(): pl.pallas_call(weight_grads_kernel, grid=(half // tile,), in_specs=specs,...]
    reduce_scatter x6 -> x5, waiting for transfers between devices: 33.6 us -> 0.01 us  [scatter(): return lax.psum_scatter(half, 'dp', scatter_dimension=0, tiled=True)]
    dot_general x24 -> x8, matrix products: 70.5 us -> 44.2 us  [contract(): lax.dot_general(left, right, (((left_dim,), (right_dim,)), ((), ())), pre...]
    all_gather x4, waiting for transfers between devices: 22.8 us -> 3.68 us  [gather(): return lax.all_gather(shard, ('dp', 'section'), axis=0, tiled=True)]
    ppermute x60 -> x54, starting transfers between devices: 25.1 us -> 14.8 us  [turn(): lax.ppermute(value, axis, [(i, (i + steps) % count) for i in range(count)])]
    unnamed x181 -> x279, local copies, waits for them, and re-layouts: 25 us -> 29.1 us
    ppermute x60 -> x54, waiting for transfers between devices: 425 us -> 429 us  [turn(): lax.ppermute(value, axis, [(i, (i + steps) % count) for i in range(count)])]
  transfers between devices with their start and end apart: 88 -> 86, of which waited for: 64 -> 55; matrix products, arithmetic and copies ran while one was open for 24% -> 21% of each run, Pallas kernels for 2% -> 7%
where the time goes in v2:
time: 742 us; the launch traced here: 731 us
  waiting for transfers between devices  438 us (59%)
  matrix products  87.2 us (12%)
  other arithmetic  69.3 us (9%)
  Pallas kernels  52.3 us (7%)
  local copies, waits for them, and re-layouts  46.2 us (6%)
  starting transfers between devices  22 us (3%)
  between operations  16.8 us (2%)
    ppermute x54, waiting for transfers between devices, turn(): lax.ppermute(value, axis, [(i, (i + steps) % count) for i in range(count)])  429 us
    dot_general x8, matrix products, contract(): lax.dot_general(left, right, (((left_dim,), (right_dim,)), ((), ())), pre...  44.2 us
    pallas_call x5, Pallas kernels, weight_grads(): pl.pallas_call(weight_grads_kernel, grid=(half // tile,), in_specs=specs,...  35.3 us
    unnamed x279, local copies, waits for them, and re-layouts  29.1 us
    dot_general x2, matrix products, feed(): jnp.dot(normed_two, w_ffn[:, :2 * units], preferred_element_type=F32)  16.3 us
  transfers between devices with their start and end apart: 86, of which 55 were waited for; matrix products, arithmetic and copies ran while one was open for 21% of the time, Pallas kernels for 7%

profile of v2, /device:TPU:0, one launch (start us, length us, event | category | flops | bytes accessed | tf_op | source)
XLA Modules:
  0.0 731.5 jit_solution(2450166162158687067)
XLA Ops:
  34.7 12.0 %collective-permute-done.2 = bf16[96,2048]{1,0:T(8,128)(2,1)S(1)} collective-permute-done((bf16[96,2048]{1,0:T(8,128)(2,1)S(1)}, bf16[96,2048]{1,0:T(8,128)(2,1)S(1)}, u32[]{:S(2)}, u32[]{:S(2)}) %collective-permute-start.2) | collective-permute-done | bytes 393248 | tf_op jit(solution)/shard_map/ppermute | solution.py:22
  47.2 11.3 %collective-permute-done.3 = bf16[96,2048]{1,0:T(8,128)(2,1)S(1)} collective-permute-done((bf16[96,2048]{1,0:T(8,128)(2,1)S(1)}, bf16[96,2048]{1,0:T(8,128)(2,1)S(1)}, u32[]{:S(2)}, u32[]{:S(2)}) %collective-permute-start.3) | collective-permute-done | bytes 393248 | tf_op jit(solution)/shard_map/ppermute | solution.py:22
  71.4 11.6 %collective-permute-done.5 = bf16[96,2048]{1,0:T(8,128)(2,1)S(1)} collective-permute-done((bf16[96,2048]{1,0:T(8,128)(2,1)S(1)}, bf16[96,2048]{1,0:T(8,128)(2,1)S(1)}, u32[]{:S(2)}, u32[]{:S(2)}) %collective-permute-start.5) | collective-permute-done | bytes 393248 | tf_op jit(solution)/shard_map/ppermute | solution.py:22
  84.0 12.8 %collective-permute-done.6 = bf16[96,2048]{1,0:T(8,128)(2,1)S(1)} collective-permute-done((bf16[96,2048]{1,0:T(8,128)(2,1)S(1)}, bf16[96,2048]{1,0:T(8,128)(2,1)S(1)}, u32[]{:S(2)}, u32[]{:S(2)}) %collective-permute-start.6) | collective-permute-done | bytes 393248 | tf_op jit(solution)/shard_map/ppermute | solution.py:22
  98.7 12.5 %collective-permute-done.9 = bf16[96,2048]{1,0:T(8,128)(2,1)S(1)} collective-permute-done((bf16[96,2048]{1,0:T(8,128)(2,1)S(1)}, bf16[96,2048]{1,0:T(8,128)(2,1)S(1)}, u32[]{:S(2)}, u32[]{:S(2)}) %collective-permute-start.9) | collective-permute-done | bytes 393248 | tf_op jit(solution)/shard_map/ppermute | solution.py:22
  111.7 11.6 %collective-permute-done.10 = bf16[96,2048]{1,0:T(8,128)(2,1)S(1)} collective-permute-done((bf16[96,2048]{1,0:T(8,128)(2,1)S(1)}, bf16[96,2048]{1,0:T(8,128)(2,1)S(1)}, u32[]{:S(2)}, u32[]{:S(2)}) %collective-permute-start.10) | collective-permute-done | bytes 393248 | tf_op jit(solution)/shard_map/ppermute | solution.py:22
  123.3 10.7 %collective-permute-done.11 = bf16[96,2048]{1,0:T(8,128)(2,1)S(1)} collective-permute-done((bf16[96,2048]{1,0:T(8,128)(2,1)S(1)}, bf16[96,2048]{1,0:T(8,128)(2,1)S(1)}, u32[]{:S(2)}, u32[]{:S(2)}) %collective-permute-start.11) | collective-permute-done | bytes 393248 | tf_op jit(solution)/shard_map/ppermute | solution.py:22
  154.4 11.4 %collective-permute-done.14 = bf16[96,2048]{1,0:T(8,128)(2,1)S(1)} collective-permute-done((bf16[96,2048]{1,0:T(8,128)(2,1)S(1)}, bf16[96,2048]{1,0:T(8,128)(2,1)S(1)}, u32[]{:S(2)}, u32[]{:S(2)}) %collective-permute-start.14) | collective-permute-done | bytes 393248 | tf_op jit(solution)/shard_map/ppermute | solution.py:22
  208.8 12.0 %collective-permute-done.20 = bf16[96,2048]{1,0:T(8,128)(2,1)S(1)} collective-permute-done((bf16[96,2048]{1,0:T(8,128)(2,1)S(1)}, bf16[96,2048]{1,0:T(8,128)(2,1)S(1)}, u32[]{:S(2)}, u32[]{:S(2)}) %collective-permute-start.20) | collective-permute-done | bytes 393248 | tf_op jit(solution)/shard_map/ppermute | solution.py:22
  222.8 11.1 %collective-permute-done.21 = bf16[96,2048]{1,0:T(8,128)(2,1)S(1)} collective-permute-done((bf16[96,2048]{1,0:T(8,128)(2,1)S(1)}, bf16[96,2048]{1,0:T(8,128)(2,1)S(1)}, u32[]{:S(2)}, u32[]{:S(2)}) %collective-permute-start.21) | collective-permute-done | bytes 393248 | tf_op jit(solution)/shard_map/ppermute | solution.py:22
  233.9 10.2 %collective-permute-done.22 = bf16[96,2048]{1,0:T(8,128)(2,1)S(1)} collective-permute-done((bf16[96,2048]{1,0:T(8,128)(2,1)S(1)}, bf16[96,2048]{1,0:T(8,128)(2,1)S(1)}, u32[]{:S(2)}, u32[]{:S(2)}) %collective-permute-start.22) | collective-permute-done | bytes 393248 | tf_op jit(solution)/shard_map/ppermute | solution.py:22
  274.4 12.6 %collective-permute-done.25 = bf16[96,2048]{1,0:T(8,128)(2,1)S(1)} collective-permute-done((bf16[96,2048]{1,0:T(8,128)(2,1)S(1)}, bf16[96,2048]{1,0:T(8,128)(2,1)S(1)}, u32[]{:S(2)}, u32[]{:S(2)}) %collective-permute-start.25) | collective-permute-done | bytes 393248 | tf_op jit(solution)/shard_map/ppermute | solution.py:22
  288.4 13.2 %collective-permute-done.28 = bf16[96,2048]{1,0:T(8,128)(2,1)S(1)} collective-permute-done((bf16[96,2048]{1,0:T(8,128)(2,1)S(1)}, bf16[96,2048]{1,0:T(8,128)(2,1)S(1)}, u32[]{:S(2)}, u32[]{:S(2)}) %collective-permute-start.28) | collective-permute-done | bytes 393248 | tf_op jit(solution)/shard_map/ppermute | solution.py:22
  303.8 11.8 %collective-permute-done.30 = bf16[96,2048]{1,0:T(8,128)(2,1)S(1)} collective-permute-done((bf16[96,2048]{1,0:T(8,128)(2,1)S(1)}, bf16[96,2048]{1,0:T(8,128)(2,1)S(1)}, u32[]{:S(2)}, u32[]{:S(2)}) %collective-permute-start.30) | collective-permute-done | bytes 393248 | tf_op jit(solution)/shard_map/ppermute | solution.py:22
  316.4 11.7 %collective-permute-done.31 = bf16[96,2048]{1,0:T(8,128)(2,1)} collective-permute-done((bf16[96,2048]{1,0:T(8,128)(2,1)S(1)}, bf16[96,2048]{1,0:T(8,128)(2,1)}, u32[]{:S(2)}, u32[]{:S(2)}) %collective-permute-start.31) | collective-permute-done | bytes 393248 | tf_op jit(solution)/shard_map/ppermute | solution.py:22
  328.1 10.9 %collective-permute-done.32 = bf16[96,2048]{1,0:T(8,128)(2,1)} collective-permute-done((bf16[96,2048]{1,0:T(8,128)(2,1)}, bf16[96,2048]{1,0:T(8,128)(2,1)}, u32[]{:S(2)}, u32[]{:S(2)}) %collective-permute-start.32) | collective-permute-done | bytes 393248 | tf_op jit(solution)/shard_map/ppermute | solution.py:22
  359.7 10.7 %fusion.19 = bf16[384,2048]{1,0:T(8,128)(2,1)} fusion(bf16[2048,4224]{1,0:T(8,128)(2,1)} %all-gather.11.cloned.1.call-done, bf16[384,1408]{1,0:T(8,128)(2,1)} %copy-done.90, bf16[384,1408]{1,0:T(8,128)(2,1)} %copy-done.89), kind=kOutput, calls=%fused_computation.28 | convolution fusion | flops 4434296832 | bytes 15269888 | tf_op jit(solution)/shard_map/dot_general | solution.py:30
  401.5 11.0 %collective-permute-done.38 = bf16[96,2048]{1,0:T(8,128)(2,1)S(1)} collective-permute-done((bf16[96,2048]{1,0:T(8,128)(2,1)S(1)}, bf16[96,2048]{1,0:T(8,128)(2,1)S(1)}, u32[]{:S(2)}, u32[]{:S(2)}) %collective-permute-start.38) | collective-permute-done | bytes 393248 | tf_op jit(solution)/shard_map/ppermute | solution.py:22
  488.1 11.4 %collective-permute-done.46 = bf16[96,2048]{1,0:T(8,128)(2,1)} collective-permute-done((bf16[96,2048]{1,0:T(8,128)(2,1)S(1)}, bf16[96,2048]{1,0:T(8,128)(2,1)}, u32[]{:S(2)}, u32[]{:S(2)}) %collective-permute-start.46) | collective-permute-done | bytes 393248 | tf_op jit(solution)/shard_map/ppermute | solution.py:22
  504.4 10.5 %collective-permute-done.47 = bf16[96,2048]{1,0:T(8,128)(2,1)} collective-permute-done((bf16[96,2048]{1,0:T(8,128)(2,1)S(1)}, bf16[96,2048]{1,0:T(8,128)(2,1)}, u32[]{:S(2)}, u32[]{:S(2)}) %collective-permute-start.47) | collective-permute-done | bytes 393248 | tf_op jit(solution)/shard_map/ppermute | solution.py:22
  546.9 10.7 %fusion.22 = bf16[384,2048]{1,0:T(8,128)(2,1)} fusion(bf16[2048,4224]{1,0:T(8,128)(2,1)} %all-gather.7.cloned.1.call-done, bf16[384,1408]{1,0:T(8,128)(2,1)} %copy-done.91, bf16[384,1408]{1,0:T(8,128)(2,1)S(1)} %get-tuple-element.407), kind=kOutput, calls=%fused_computation.29 | convolution fusion | flops 4434296832 | bytes 15269888 | tf_op jit(solution)/shard_map/dot_general | solution.py:30
  562.5 12.5 %shard_map.209 = bf16[1024,4224]{1,0:T(8,128)(2,1)} custom-call(bf16[384,1024]{1,0:T(8,128)(2,1)S(1)} %maximum_select_fusion.11.refs_0_, bf16[384,1024]{1,0:T(8,128)(2,1)} %collective-permute-done.18.refs_1_, bf16[384,2816]{1,0:T(8,128)(2,1)S(1)} %pad_maximum_fusion.2.refs_2_, bf16[384,2816]{1,0:T(8,128)(2,1)S(1)} %collective-permute-done.51.refs_3_, ...), custom_call_target="tpu_custom_call" | custom-call | tf_op jit(solution)/shard_map/pallas_call | solution.py:314
  627.3 10.4 %collective-permute-done.57 = bf16[96,2048]{1,0:T(8,128)(2,1)S(1)} collective-permute-done((bf16[96,2048]{1,0:T(8,128)(2,1)S(1)}, bf16[96,2048]{1,0:T(8,128)(2,1)S(1)}, u32[]{:S(2)}, u32[]{:S(2)}) %collective-permute-start.57) | collective-permute-done | bytes 393248 | tf_op jit(solution)/shard_map/ppermute | solution.py:22
  675.1 11.6 %collective-permute-done.62 = bf16[96,2048]{1,0:T(8,128)(2,1)S(1)} collective-permute-done((bf16[96,2048]{1,0:T(8,128)(2,1)S(1)}, bf16[96,2048]{1,0:T(8,128)(2,1)S(1)}, u32[]{:S(2)}, u32[]{:S(2)}) %collective-permute-start.62) | collective-permute-done | bytes 393248 | tf_op jit(solution)/shard_map/ppermute | solution.py:22
  (611 shorter events, 438.6 us)
Async XLA Ops:
  7.2 51.7 %all-gather.5.cloned.1.call-start = ((), (), s32[]{:S(2)}) async-start(), calls=%async_computation.5 | async-start | bytes 5898240 | tf_op jit(solution)/shard_map/all_gather | solution.py:408
  12.4 153.4 %all-gather.7.cloned.1.call-start = ((), (), s32[]{:S(2)}) async-start(), calls=%async_computation.6 | async-start | bytes 19464192 | tf_op jit(solution)/shard_map/all_gather | solution.py:408
  16.9 14.4 %collective-permute-start = (bf16[96,2048]{1,0:T(8,128)(2,1)S(1)}, bf16[96,2048]{1,0:T(8,128)(2,1)S(1)}, u32[]{:S(2)}, u32[]{:S(2)}) collective-permute-start(bf16[96,2048]{1,0:T(8,128)(2,1)S(1)} %select_bitcast_fusion.5), channel_id=1, source_target_pairs={{0,1},{1,2},{2,3},{3,0},{4,5},{5,6},{6,7},{7,4},{8,9},{9,10},{10,1... | collective-permute-start | bytes 1179656 | tf_op jit(solution)/shard_map/ppermute | solution.py:22
  31.4 166.5 %all-gather.9.cloned.1.call-start = ((), (), s32[]{:S(2)}) async-start(), calls=%async_computation.7 | async-start | bytes 5898240 | tf_op jit(solution)/shard_map/all_gather | solution.py:408
  32.1 296.0 %all-gather.11.cloned.1.call-start = ((), (), s32[]{:S(2)}) async-start(), calls=%async_computation.8 | async-start | bytes 19464192 | tf_op jit(solution)/shard_map/all_gather | solution.py:408
  32.7 466.8 %reduce-scatter.6.cloned.1.call-start = ((), (), s32[]{:S(2)}) async-start(), calls=%async_computation.9 | async-start | bytes 7208960 | tf_op jit(solution)/shard_map/reduce_scatter | solution.py:325
  83.5 14.1 %collective-permute-start.7 = (bf16[384,1024]{1,0:T(8,128)(2,1)S(1)}, bf16[384,1024]{1,0:T(8,128)(2,1)S(1)}, u32[]{:S(2)}, u32[]{:S(2)}) collective-permute-start(bf16[384,1024]{1,0:T(8,128)(2,1)S(1)} %maximum_select_fusion), channel_id=1, source_target_pairs={{0,16},{16,0},{1,17},{17,1},{2,18},{18,2},{3,19},{19,3},{4,20},{20... | collective-permute-start | bytes 2359304 | tf_op jit(solution)/shard_map/ppermute | solution.py:26
  192.5 14.9 %collective-permute-start.19 = (bf16[384,1408]{1,0:T(8,128)(2,1)S(1)}, bf16[384,1408]{1,0:T(8,128)(2,1)S(1)}, u32[]{:S(2)}, u32[]{:S(2)}) collective-permute-start(bf16[384,1408]{1,0:T(8,128)(2,1)S(1)} %fusion.37.refs_6_), channel_id=1, source_target_pairs={{0,16},{16,0},{1,17},{17,1},{2,18},{18,2},{3,19},{19,3},{4,20},{20... | collective-permute-start | bytes 3244040 | tf_op jit(solution)/shard_map/ppermute | solution.py:26
  193.7 13.6 %collective-permute-start.18 = (bf16[384,1024]{1,0:T(8,128)(2,1)}, bf16[384,1024]{1,0:T(8,128)(2,1)}, u32[]{:S(2)}, u32[]{:S(2)}) collective-permute-start(bf16[384,1024]{1,0:T(8,128)(2,1)} %maximum_select_fusion.1), channel_id=1, source_target_pairs={{0,16},{16,0},{1,17},{17,1},{2,18},{18,2},{3,19},{19,3},{4,20},{20... | collective-permute-start | bytes 2359304 | tf_op jit(solution)/shard_map/ppermute | solution.py:26
  273.2 13.8 %collective-permute-start.26 = (bf16[384,1024]{1,0:T(8,128)(2,1)S(1)}, bf16[384,1024]{1,0:T(8,128)(2,1)S(1)}, u32[]{:S(2)}, u32[]{:S(2)}) collective-permute-start(bf16[384,1024]{1,0:T(8,128)(2,1)S(1)} %maximum_select_fusion.2), channel_id=1, source_target_pairs={{0,16},{16,0},{1,17},{17,1},{2,18},{18,2},{3,19},{19,3},{4,20},{20... | collective-permute-start | bytes 2359304 | tf_op jit(solution)/shard_map/ppermute | solution.py:26
  273.3 13.7 %collective-permute-start.25 = (bf16[96,2048]{1,0:T(8,128)(2,1)S(1)}, bf16[96,2048]{1,0:T(8,128)(2,1)S(1)}, u32[]{:S(2)}, u32[]{:S(2)}) collective-permute-start(bf16[96,2048]{1,0:T(8,128)(2,1)S(1)} %add_convert_fusion.12), channel_id=1, source_target_pairs={{0,1},{1,2},{2,3},{3,0},{4,5},{5,6},{6,7},{7,4},{8,9},{9,10},{10,1... | collective-permute-start | bytes 1179656 | tf_op jit(solution)/shard_map/ppermute | solution.py:22
  354.8 15.7 %collective-permute-start.34 = (bf16[384,2816]{1,0:T(8,128)(2,1)S(1)}, bf16[384,2816]{1,0:T(8,128)(2,1)S(1)}, u32[]{:S(2)}, u32[]{:S(2)}) collective-permute-start(bf16[384,2816]{1,0:T(8,128)(2,1)S(1)} %pad_maximum_fusion.1.refs_2_), channel_id=1, source_target_pairs={{0,16},{16,0},{1,17},{17,1},{2,18},{18,2},{3,19},{19,3},{4,20},{20... | collective-permute-start | bytes 6488072 | tf_op jit(solution)/shard_map/ppermute | solution.py:26
  385.8 129.1 %reduce-scatter.8.cloned.1.call-start = ((), (), s32[]{:S(2)}) async-start(), calls=%async_computation.10 | async-start | bytes 3604480 | tf_op jit(solution)/shard_map/reduce_scatter | solution.py:325
  436.1 156.1 %reduce-scatter.10.cloned.1.call-start = ((), (), s32[]{:S(2)}) async-start(), calls=%async_computation.11 | async-start | bytes 2949120 | tf_op jit(solution)/shard_map/reduce_scatter | solution.py:325
  526.6 146.7 %reduce-scatter.12.cloned.1.call-start = ((), (), s32[]{:S(2)}) async-start(), calls=%async_computation.12 | async-start | bytes 10813440 | tf_op jit(solution)/shard_map/reduce_scatter | solution.py:325
  545.1 13.7 %collective-permute-start.51 = (bf16[384,2816]{1,0:T(8,128)(2,1)S(1)}, bf16[384,2816]{1,0:T(8,128)(2,1)S(1)}, u32[]{:S(2)}, u32[]{:S(2)}) collective-permute-start(bf16[384,2816]{1,0:T(8,128)(2,1)S(1)} %pad_maximum_fusion.2.refs_2_), channel_id=1, source_target_pairs={{0,16},{16,0},{1,17},{17,1},{2,18},{18,2},{3,19},{19,3},{4,20},{20... | collective-permute-start | bytes 6488072 | tf_op jit(solution)/shard_map/ppermute | solution.py:26
  545.2 13.6 %collective-permute-start.50 = (bf16[96,2048]{1,0:T(8,128)(2,1)}, bf16[96,2048]{1,0:T(8,128)(2,1)}, u32[]{:S(2)}, u32[]{:S(2)}) collective-permute-start(bf16[96,2048]{1,0:T(8,128)(2,1)} %slice.768), channel_id=1, source_target_pairs={{0,1},{1,2},{2,3},{3,0},{4,5},{5,6},{6,7},{7,4},{8,9},{9,10},{10,1... | collective-permute-start | bytes 1179656 | tf_op jit(solution)/shard_map/ppermute | solution.py:22
  560.6 14.4 %collective-permute-start.53 = (bf16[96,2048]{1,0:T(8,128)(2,1)}, bf16[96,2048]{1,0:T(8,128)(2,1)}, u32[]{:S(2)}, u32[]{:S(2)}) collective-permute-start(bf16[96,2048]{1,0:T(8,128)(2,1)} %slice.781), channel_id=1, source_target_pairs={{0,1},{1,2},{2,3},{3,0},{4,5},{5,6},{6,7},{7,4},{8,9},{9,10},{10,1... | collective-permute-start | bytes 1179656 | tf_op jit(solution)/shard_map/ppermute | solution.py:22
  575.1 135.2 %reduce-scatter.14.cloned.1.call-start = ((), (), s32[]{:S(2)}) async-start(), calls=%async_computation.13 | async-start | bytes 2949120 | tf_op jit(solution)/shard_map/reduce_scatter | solution.py:325
  576.5 13.9 %collective-permute-start.70 = (bf16[96,2048]{1,0:T(8,128)(2,1)S(1)}, bf16[96,2048]{1,0:T(8,128)(2,1)S(1)}, u32[]{:S(2)}, u32[]{:S(2)}) collective-permute-start(bf16[96,2048]{1,0:T(8,128)(2,1)S(1)} %add_convert_fusion.3), channel_id=1, source_target_pairs={{0,1},{1,2},{2,3},{3,0},{4,5},{5,6},{6,7},{7,4},{8,9},{9,10},{10,1... | collective-permute-start | bytes 1179656 | tf_op jit(solution)/shard_map/ppermute | solution.py:22
  577.8 21.0 %collective-permute-start.54 = (bf16[96,2048]{1,0:T(8,128)(2,1)S(1)}, bf16[96,2048]{1,0:T(8,128)(2,1)S(1)}, u32[]{:S(2)}, u32[]{:S(2)}) collective-permute-start(bf16[96,2048]{1,0:T(8,128)(2,1)S(1)} %add_convert_fusion.6), channel_id=1, source_target_pairs={{0,1},{1,2},{2,3},{3,0},{4,5},{5,6},{6,7},{7,4},{8,9},{9,10},{10,1... | collective-permute-start | bytes 1179656 | tf_op jit(solution)/shard_map/ppermute | solution.py:22
  592.2 15.1 %collective-permute-start.71 = (bf16[96,2048]{1,0:T(8,128)(2,1)}, bf16[96,2048]{1,0:T(8,128)(2,1)}, u32[]{:S(2)}, u32[]{:S(2)}) collective-permute-start(bf16[96,2048]{1,0:T(8,128)(2,1)} %add_convert_fusion.2), channel_id=1, source_target_pairs={{0,1},{1,2},{2,3},{3,0},{4,5},{5,6},{6,7},{7,4},{8,9},{9,10},{10,1... | collective-permute-start | bytes 1179656 | tf_op jit(solution)/shard_map/ppermute | solution.py:22
  600.0 14.2 %collective-permute-start.55 = (bf16[96,2048]{1,0:T(8,128)(2,1)S(1)}, bf16[96,2048]{1,0:T(8,128)(2,1)S(1)}, u32[]{:S(2)}, u32[]{:S(2)}) collective-permute-start(bf16[96,2048]{1,0:T(8,128)(2,1)S(1)} %add_convert_fusion.5), channel_id=1, source_target_pairs={{0,1},{1,2},{2,3},{3,0},{4,5},{5,6},{6,7},{7,4},{8,9},{9,10},{10,1... | collective-permute-start | bytes 1179656 | tf_op jit(solution)/shard_map/ppermute | solution.py:22
  608.9 28.9 %collective-permute-start.72 = (bf16[96,2048]{1,0:T(8,128)(2,1)S(1)}, bf16[96,2048]{1,0:T(8,128)(2,1)S(1)}, u32[]{:S(2)}, u32[]{:S(2)}) collective-permute-start(bf16[96,2048]{1,0:T(8,128)(2,1)S(1)} %get-tuple-element.398), channel_id=1, source_target_pairs={{0,16},{16,0},{1,17},{17,1},{2,18},{18,2},{3,19},{19,3},{4,20},{20... | collective-permute-start | bytes 1179656 | tf_op jit(solution)/shard_map/ppermute | solution.py:26
  (196 other events, 1862.8 us)
Sparse Core Ops, SparseCore 0:
  12.6 44.6 all-gather.4
  59.7 92.0 all-gather.6
  154.3 43.5 all-gather.8
  200.2 91.4 all-gather.10
  385.9 62.9 reduce-scatter.5
  452.4 41.7 reduce-scatter.7
  526.7 37.5 reduce-scatter.9
  575.2 88.6 reduce-scatter.11
  673.4 34.2 reduce-scatter.13

commit v3 on v2

--- a/solution.py
+++ b/solution.py
@@ -14,7 +14,8 @@
 F32 = jnp.float32
 LANES = 128
 SCALE = HEAD ** (-0.5)
-VMEM_BYTES = 28 * 2**20
+VMEM_BYTES = 12 * 2**20
+GRADS_VMEM_BYTES = 20 * 2**20
 
 
 def turn(value, axis, steps):
@@ -144,6 +145,10 @@
         return self.total
 
 
+def estimate(us):
+    return pl.CostEstimate(flops=0, bytes_accessed=int(us * 3.3e6), transcendentals=0)
+
+
 def normalizer(rows):
     return lax.rsqrt(jnp.mean(rows * rows, axis=1, keepdims=True) + EPSILON)
 
@@ -173,9 +178,10 @@
     rot_ref[:, q_cols:] = kv
     keys, values = heads_of(kv)
     bias = bias_ref[...]
-    log_totals = []
-    for slab in range(q_cols // LANES):
-        cols = slice(slab * LANES, (slab + 1) * LANES)
+    head_ids = lax.broadcasted_iota(jnp.int32, lse_ref.shape, 1)
+
+    def one_slab(slab, log_totals):
+        cols = pl.ds(pl.multiple_of(slab * LANES, LANES), LANES)
         query = qkv_ref[:, cols]
         query = (query * cosine + half_swap(query) * sine_part).astype(BF16)
         rot_ref[:, cols] = query
@@ -185,10 +191,15 @@
             row_max = jnp.max(scores, axis=1, keepdims=True)
             exponent = jnp.exp(scores - row_max)
             totals = jnp.sum(exponent, axis=1, keepdims=True)
-            log_totals.append(row_max + jnp.log(totals))
+            log_total = row_max + jnp.log(totals)
+            log_totals = jnp.where(head_ids == 2 * slab + odd, log_total, log_totals)
             mixed = mixed + contract((exponent / totals).astype(BF16), values[odd], 1, 0)
         mixed_ref[:, cols] = mixed.astype(BF16)
-    lse_ref[...] = jnp.concatenate(log_totals, axis=1)
+        return log_totals
+
+    lse_ref[...] = lax.fori_loop(
+        0, q_cols // LANES, one_slab, jnp.zeros(lse_ref.shape, F32)
+    )
 
 
 def attend(normed_one, geo, w_attn, q_cols, kv_cols):
@@ -202,6 +213,7 @@
             jax.ShapeDtypeStruct((group, q_cols), BF16),
             jax.ShapeDtypeStruct((group, q_cols // HEAD), F32),
         ),
+        cost_estimate=estimate(3),
         compiler_params=pltpu.CompilerParams(vmem_limit_bytes=VMEM_BYTES),
     )(qkv, *geo)
     out_term = contract(mixed, w_attn[:, both : both + q_cols], 1, 1).astype(BF16)
@@ -213,17 +225,21 @@
     cosine, sine_part = (table_ref[0], table_ref[1])
     keys, values = heads_of(rot_ref[:, q_cols:])
     bias = bias_ref[...]
-    d_keys = [0.0, 0.0]
-    d_values = [0.0, 0.0]
-    for slab in range(q_cols // LANES):
-        cols = slice(slab * LANES, (slab + 1) * LANES)
+    log_totals = lse_ref[...]
+    head_ids = lax.broadcasted_iota(jnp.int32, log_totals.shape, 1)
+
+    def one_slab(slab, sums):
+        d_keys, d_values = (list(sums[:2]), list(sums[2:]))
+        cols = pl.ds(pl.multiple_of(slab * LANES, LANES), LANES)
         query = rot_ref[:, cols]
         d_mixed = d_mixed_ref[:, cols]
         d_query = 0.0
         for odd in range(2):
-            head = 2 * slab + odd
+            log_total = jnp.sum(
+                jnp.where(head_ids == 2 * slab + odd, log_totals, 0.0), axis=1, keepdims=True
+            )
             scores = contract(query, keys[odd], 1, 1) * SCALE + bias
-            probs = jnp.exp(scores - lse_ref[:, head : head + 1])
+            probs = jnp.exp(scores - log_total)
             d_probs = contract(d_mixed, values[odd], 1, 1)
             total = jnp.sum(d_probs * probs, axis=1, keepdims=True)
             d_scores = (probs * (d_probs - total)).astype(BF16)
@@ -232,6 +248,11 @@
             d_keys[odd] = d_keys[odd] + contract(d_scores, query, 0, 0)
         d_query = d_query * SCALE
         out_ref[:, cols] = (d_query * cosine - half_swap(d_query) * sine_part).astype(BF16)
+        return (*d_keys, *d_values)
+
+    zeros = jnp.zeros((d_mixed_ref.shape[0], LANES), F32)
+    sums = lax.fori_loop(0, q_cols // LANES, one_slab, (zeros,) * 4)
+    d_keys, d_values = (sums[:2], sums[2:])
     low = lax.broadcasted_iota(jnp.int32, d_keys[0].shape, 1) < HEAD
     d_kv = jnp.where(
         low,
@@ -251,6 +272,7 @@
     d_qkv = pl.pallas_call(
         attend_back_kernel,
         out_shape=jax.ShapeDtypeStruct(rotated.shape, BF16),
+        cost_estimate=estimate(6),
         compiler_params=pltpu.CompilerParams(vmem_limit_bytes=VMEM_BYTES),
     )(d_mixed, rotated, log_total, *geo)
     d_norm_one = contract(d_qkv, w_attn[:, :both], 1, 1).astype(BF16)
@@ -270,9 +292,11 @@
     sigmoid_gate = jax.nn.sigmoid(gate)
     d_up = (d_hidden * gate * sigmoid_gate).astype(BF16)
     d_gate = (d_hidden * up * sigmoid_gate * (1.0 + gate * (1.0 - sigmoid_gate))).astype(BF16)
-    d_gate_up = jnp.concatenate([d_gate, d_up], axis=1)
-    other = swap(d_gate_up)
-    return (d_gate_up, other, contract(d_gate_up, w_ffn[:, : 2 * units], 1, 1).astype(BF16))
+    return (jnp.concatenate([d_gate, d_up], axis=1),)
+
+
+def feed_back_rows(d_gate_up, w_ffn):
+    return (contract(d_gate_up, w_ffn[:, : d_gate_up.shape[1]], 1, 1).astype(BF16),)
 
 
 def core_half(rows, at_first, own):
@@ -291,7 +315,7 @@
     return tuple(swap(core_half(x, at_first, False)) for x in rows) + tuple(map(swap, whole))
 
 
-def weight_grads_kernel(*refs):
+def weight_grads_kernel(_, *refs):
     *pairs, out_ref = refs
     at = 0
     for k in range(0, len(pairs), 4):
@@ -302,23 +326,37 @@
 
 
 def weight_grads(at_first, *pairs):
-    pairs = [(core_half(rows, at_first, True), *rest) for rows, *rest in pairs]
-    group, half = pairs[0][0].shape
-    tile = min(256, half)
+    group, half = pairs[0][1].shape
+    n_dp = lax.axis_size("dp")
+    tile = half // n_dp
+    direct = tile % LANES == 0
+    if not direct:
+        pairs = [(core_half(rows, at_first, True), *rest) for rows, *rest in pairs]
+        tile = min(256, half)
     specs = []
     for _, _, grads, _ in pairs:
-        rows_spec = pl.BlockSpec((group, tile), lambda i: (0, i))
-        grads_spec = pl.BlockSpec((group, grads.shape[1]), lambda i: (0, 0))
-        specs += [rows_spec, rows_spec, grads_spec, grads_spec]
+        own_spec = pl.BlockSpec((group, tile), lambda i, core: (0, 2 * i + core[0]))
+        half_spec = pl.BlockSpec((group, tile), lambda i, core: (0, i))
+        grads_spec = pl.BlockSpec(
+            (group, grads.shape[1]), lambda i, core: (0, 0), pipeline_mode=pl.Buffered(1)
+        )
+        specs += [own_spec if direct else half_spec, half_spec, grads_spec, grads_spec]
     total = sum(grads.shape[1] for _, _, grads, _ in pairs)
     return pl.pallas_call(
         weight_grads_kernel,
-        grid=(half // tile,),
-        in_specs=specs,
-        out_specs=pl.BlockSpec((tile, total), lambda i: (i, 0)),
+        grid_spec=pltpu.PrefetchScalarGridSpec(
+            num_scalar_prefetch=1,
+            grid=(half // tile,),
+            in_specs=specs,
+            out_specs=pl.BlockSpec((tile, total), lambda i, core: (i, 0)),
+        ),
         out_shape=pltpu.HBM((half, total), BF16),
-        compiler_params=pltpu.CompilerParams(vmem_limit_bytes=VMEM_BYTES),
-    )(*[x for pair in pairs for x in pair])
+        cost_estimate=estimate(total / 330),
+        compiler_params=pltpu.CompilerParams(vmem_limit_bytes=GRADS_VMEM_BYTES),
+    )(
+        jnp.where(at_first, 0, 1).astype(jnp.int32).reshape(1),
+        *[x for pair in pairs for x in pair],
+    )
 
 
 def scatter(half):
@@ -332,28 +370,46 @@
 
 
 def backward(
-    kept, grad_all, grad, geo, weights, at_first, others, early, aside, down_job, last
+    kept, grad_all, grad, geo, weights, at_first, others, early, aside, down_job
 ):
     (layer_in, normed_one, rotated, log_total, mixed, middle, normed_two, gate_up, hidden) = kept
     norm_gain, ffn_gain, w_attn, w_ffn = weights
+    last = down_job is None
     run = aside.run if aside else lambda fn, *inputs: fn(*inputs)
-    d_gate_up, other_gate_up, d_norm_two_all = run(feed_back, grad_all, gate_up, w_ffn)
-    ffn_pair = (normed_two, others["normed_two"], d_gate_up, other_gate_up)
-    down_pair = (grad_all, others["grad_all"], hidden, others["hidden"])
-    d_norm_two_all, *ready = barrier(d_norm_two_all, *ffn_pair, *down_pair)
-    ffn_pair, down_pair = (ready[:4], ready[4:])
+    (d_gate_up,) = run(feed_back, grad_all, gate_up, w_ffn)
+    (d_norm_two_all,) = run(feed_back_rows, d_gate_up, w_ffn)
+    if last:
+        d_gate_up, grad_all = barrier(d_gate_up, grad_all)
+        others["grad_all"] = exchange(at_first, (grad_all,))[0]
 
     def grads(*given):
         pairs = [given[k : k + 4] for k in range(0, len(given), 4)]
         return (weight_grads(at_first, *pairs),)
 
     if last:
-        jobs = (Job(grads, *ffn_pair, *down_pair), Job(lambda: (), held=early))
+        pairs = (
+            *(normed_two, others["normed_two"], d_gate_up, swap(d_gate_up)),
+            *(grad_all, others["grad_all"], hidden, others["hidden"]),
+        )
+        d_norm_two_all, *pairs = barrier(d_norm_two_all, *pairs)
+        grads_jobs = (Job(grads, *pairs), Job(lambda: (), held=early))
+        d_norm_two = collect(d_norm_two_all, grads_jobs)
+        early = grads_jobs[1].held
     else:
-        jobs = (Job(grads, *ffn_pair), Job(grads, *down_pair, held=early))
-    d_norm_two = collect(d_norm_two_all, jobs)
-    early = jobs[1].held
-    reduced = [scatter(job[0]) for job in jobs if job.results]
+        swap_job = Job(
+            lambda d_gate_up, hidden, *rows: (
+                swap(d_gate_up), swap(hidden), *exchange(at_first, rows)
+            ),
+            d_gate_up,
+            hidden,
+            normed_two,
+            grad_all,
+        )
+        grads_jobs = (Job(grads), Job(grads))
+        grads_jobs[0].inputs = lambda: (normed_two, swap_job[2], d_gate_up, swap_job[0])
+        grads_jobs[1].inputs = lambda: (grad_all, swap_job[3], hidden, swap_job[1])
+        d_norm_two = collect(d_norm_two_all, (swap_job, *grads_jobs))
+    reduced = [scatter(job[0]) for job in grads_jobs if job.results]
     d_middle = grad.astype(F32) + norm_back(middle, normalizer(middle), ffn_gain, d_norm_two)
     ffn_gain_job = Job(
         lambda d_all, normed: (
@@ -362,15 +418,21 @@
         d_norm_two_all,
         normed_two,
     )
-    grad_attn = spread(d_middle.astype(BF16), (ffn_gain_job, down_job))
-    if down_job:
+    if last:
+        aside_job = Job(lambda value: (turn(value, "tensor", 1),), aside.value)
+        grad_attn = spread(d_middle.astype(BF16), (ffn_gain_job, aside_job))
+        aside.accept(aside_job[0])
+        aside.taken += 1
+    else:
+        grad_attn = spread(d_middle.astype(BF16), (ffn_gain_job, down_job))
         aside = CollectRing(down_job[0])
     d_qkv, other_qkv, other_attn, d_norm_one_all = attend_back(
         grad_attn, geo, w_attn, at_first, rotated, log_total
     )
+    other_one, other_mixed = others.get("attn") or exchange(at_first, (normed_one,), mixed)
     pairs = (
-        *(normed_one, others["normed_one"], d_qkv, other_qkv),
-        *(grad_attn, other_attn, mixed, others["mixed"]),
+        *(normed_one, other_one, d_qkv, other_qkv),
+        *(grad_attn, other_attn, mixed, other_mixed),
     )
     d_norm_one_all, *pairs = barrier(d_norm_one_all, *pairs)
     attn_job = Job(grads, *pairs, held=reduced[:1] if last else ())
@@ -381,9 +443,9 @@
         d_norm_one_all,
         normed_one,
     )
-    ffn_done = Job(lambda: (), held=() if last else reduced[:1])
-    d_norm_one = collect(d_norm_one_all, (attn_job, attn_gain_job, ffn_done))
-    reduced[:1] = attn_job.held or ffn_done.held
+    last_job = Job(lambda: (), held=() if last else reduced[:1])
+    d_norm_one = collect(d_norm_one_all, (attn_job, attn_gain_job, last_job))
+    reduced[:1] = attn_job.held or last_job.held
     g_attn = attn_job[0]
     d_input = d_middle + norm_back(layer_in, normalizer(layer_in), norm_gain, d_norm_one)
     gain_grads = jnp.stack([attn_gain_job[0], ffn_gain_job[0]])
@@ -458,11 +520,13 @@
         w_up[0],
         w_down[0],
     )
-    tokens_all = spread(tokens, (prepare,))
+    tokens_all = spread(tokens, (None, prepare))
+    tokens_all, upstream = barrier(tokens_all, upstream)
+    upstream_ring = SpreadRing(upstream)
     first_attn = gather(attn_parts[0])
     first_ffn = gather(prepare[0])
     w_attns = [first_attn, gather(attn_parts[1])]
-    w_ffns = [first_ffn, gather(prepare[1])]
+    w_ffns = [first_ffn]
     geo = geometry(jnp.where(at_first, lengths[0, 0], lengths[1, 0]), rows)
     tokens_all = tokens_all.astype(F32)
     layer_in = tokens.astype(F32)
@@ -476,28 +540,20 @@
             normed_one = spread((layer_in * normalizer(layer_in) * norm_gain).astype(BF16))
         else:
             normed_one = (tokens_all * normalizer(tokens_all) * norm_gain).astype(BF16)
-        out_term, rotated, log_total, mixed = attend(normed_one, geo, w_attn, q_cols, kv_cols)
-        attn_swap = Job(lambda one, heads: exchange(at_first, (one,), heads), normed_one, mixed)
+        attention = (lambda normed, w: attend(normed, geo, w, q_cols, kv_cols), normed_one, w_attn)
+        out_term, rotated, log_total, mixed = upstream_ring.run(*attention)
+        middle = layer_in + collect(out_term)
+        normed_two = spread((middle * normalizer(middle) * ffn_gain).astype(BF16))
         others = {}
-        grad_swap = None
-        if layer:
-            grad_swap = Job(lambda x: exchange(at_first, (x,)), upstream_all)
-        middle = layer_in + collect(out_term, (None, attn_swap, grad_swap))
-        others.update(normed_one=attn_swap[0], mixed=attn_swap[1])
-        if layer:
-            others.update(grad_all=grad_swap[0])
-        normed_two = spread((middle * normalizer(middle) * ffn_gain).astype(BF16))
-        if layer:
-            gate_up, hidden = feed(normed_two, w_ffn, units)
-        else:
-            normed_two, upstream = barrier(normed_two, upstream)
-            upstream_ring = SpreadRing(upstream)
-            upstream_ring.run(lambda: ())
-            upstream_ring.run(lambda: ())
-            gate_up, hidden = upstream_ring.run(
-                lambda normed, w: feed(normed, w, units), normed_two, w_ffn
+        if layer == 0:
+            normed_two, upstream_ring.value = barrier(normed_two, upstream_ring.value)
+            others.update(
+                attn=upstream_ring.run(
+                    lambda one, heads: exchange(at_first, (one,), heads), normed_one, mixed
+                )
             )
-            upstream_all = upstream_ring.finish()
+            normed_two, upstream_ring.value = barrier(normed_two, upstream_ring.value)
+        gate_up, hidden = feed(normed_two, w_ffn, units)
         down_job = Job(
             lambda hidden, w: (contract(hidden, w[:, 2 * units :], 1, 1).astype(BF16),),
             hidden,
@@ -510,10 +566,8 @@
             )
             first_out = (middle + collect(down_term, (None, ffn_swap))).astype(BF16)
             others.update(normed_two=ffn_swap[0], hidden=ffn_swap[1])
-        else:
-            others.update(
-                zip(("normed_two", "hidden"), exchange(at_first, (normed_two,), hidden))
-            )
+            first_out, ffn_part = barrier(first_out, prepare[1])
+            w_ffns.append(gather(ffn_part))
         kept = (
             layer_in, normed_one, rotated, log_total, mixed, middle, normed_two, gate_up, hidden
         )
@@ -522,8 +576,6 @@
 
     def back(layer, grad_all, grad, early, aside, down_job):
         kept, weights, others = layers[layer]
-        if "grad_all" not in others:
-            others["grad_all"] = exchange(at_first, (grad_all,))[0]
         return backward(
             kept,
             grad_all,
@@ -535,9 +587,9 @@
             early,
             aside,
             down_job,
-            layer == 0,
-        )
-
+        )
+
+    upstream_all = upstream_ring.finish()
     d_second, (second_attn, second_ffn, second_down), second_gains, _, out_ring = back(
         1, upstream_all, upstream, (), None, down_job
     )
@@ -567,13 +619,14 @@
     )
     g_attn = own_layer(first_attn, second_attn, at_first).astype(F32)
     qkv = q_cols + 2 * kv_cols
+    g_key_value = g_attn[:, q_cols:qkv].T
     return (
         section_out[None],
         input_grad[None],
         gain_own[0][None],
         g_attn[:, :q_cols][None],
-        g_attn[:, q_cols : q_cols + kv_cols][None],
-        g_attn[:, q_cols + kv_cols : qkv][None],
+        g_key_value[:kv_cols].T[None],
+        g_key_value[kv_cols:].T[None],
         g_attn[:, qkv:].T[None],
         gain_own[1][None],
         g_gate[None],

time: 742 us -> 730 us (0.984)
  waiting for transfers between devices: 438 us -> 428 us
    ppermute x54, waiting for transfers between devices: 429 us -> 419 us  [turn(): lax.ppermute(value, axis, [(i, (i + steps) % count) for i in range(count)])]
    unnamed x279 -> x254, local copies, waits for them, and re-layouts: 29.1 us -> 35.3 us
  transfers between devices with their start and end apart: 86 -> 86, of which waited for: 55 -> 55; matrix products, arithmetic and copies ran while one was open for 21% -> 19% of each run, Pallas kernels for 7% -> 8%
where the time goes in v3:
time: 730 us; the launch traced here: 720 us
  waiting for transfers between devices  428 us (59%)
  matrix products  83.9 us (11%)
  other arithmetic  72.4 us (10%)
  Pallas kernels  55.1 us (8%)
  local copies, waits for them, and re-layouts  45.3 us (6%)
  starting transfers between devices  19.4 us (3%)
  between operations  16.5 us (2%)
    ppermute x54, waiting for transfers between devices, turn(): lax.ppermute(value, axis, [(i, (i + steps) % count) for i in range(count)])  419 us
    dot_general x8, matrix products, contract(): lax.dot_general(left, right, (((left_dim,), (right_dim,)), ((), ())), pre...  43.9 us
    unnamed x254, local copies, waits for them, and re-layouts  35.3 us
    pallas_call x5, Pallas kernels, weight_grads(): pl.pallas_call(weight_grads_kernel, grid_spec=pltpu.PrefetchScalarGridSpe...  34.7 us
    dot_general x2, matrix products, feed(): jnp.dot(normed_two, w_ffn[:, :2 * units], preferred_element_type=F32)  16.4 us
  transfers between devices with their start and end apart: 86, of which 55 were waited for; matrix products, arithmetic and copies ran while one was open for 19% of the time, Pallas kernels for 8%

profile of v3, /device:TPU:0, one launch (start us, length us, event | category | flops | bytes accessed | tf_op | source)
XLA Modules:
  0.0 720.3 jit_solution(3488987629066619837)
XLA Ops:
  46.4 11.2 %collective-permute-done.3 = bf16[96,2048]{1,0:T(8,128)(2,1)S(1)} collective-permute-done((bf16[96,2048]{1,0:T(8,128)(2,1)S(1)}, bf16[96,2048]{1,0:T(8,128)(2,1)S(1)}, u32[]{:S(2)}, u32[]{:S(2)}) %collective-permute-start.3) | collective-permute-done | bytes 393248 | tf_op jit(solution)/shard_map/ppermute | solution.py:23
  75.3 11.3 %collective-permute-done.6 = bf16[96,2048]{1,0:T(8,128)(2,1)S(1)} collective-permute-done((bf16[96,2048]{1,0:T(8,128)(2,1)S(1)}, bf16[96,2048]{1,0:T(8,128)(2,1)S(1)}, u32[]{:S(2)}, u32[]{:S(2)}) %collective-permute-start.6) | collective-permute-done | bytes 393248 | tf_op jit(solution)/shard_map/ppermute | solution.py:23
  86.8 10.4 %collective-permute-done.7 = bf16[96,2048]{1,0:T(8,128)(2,1)S(1)} collective-permute-done((bf16[96,2048]{1,0:T(8,128)(2,1)S(1)}, bf16[96,2048]{1,0:T(8,128)(2,1)S(1)}, u32[]{:S(2)}, u32[]{:S(2)}) %collective-permute-start.7) | collective-permute-done | bytes 393248 | tf_op jit(solution)/shard_map/ppermute | solution.py:23
  109.6 10.7 %collective-permute-done.9 = bf16[96,2048]{1,0:T(8,128)(2,1)S(1)} collective-permute-done((bf16[96,2048]{1,0:T(8,128)(2,1)S(1)}, bf16[96,2048]{1,0:T(8,128)(2,1)S(1)}, u32[]{:S(2)}, u32[]{:S(2)}) %collective-permute-start.9) | collective-permute-done | bytes 393248 | tf_op jit(solution)/shard_map/ppermute | solution.py:23
  120.3 11.8 %collective-permute-done.10 = bf16[96,2048]{1,0:T(8,128)(2,1)S(1)} collective-permute-done((bf16[96,2048]{1,0:T(8,128)(2,1)S(1)}, bf16[96,2048]{1,0:T(8,128)(2,1)S(1)}, u32[]{:S(2)}, u32[]{:S(2)}) %collective-permute-start.10) | collective-permute-done | bytes 393248 | tf_op jit(solution)/shard_map/ppermute | solution.py:23
  143.5 12.5 %collective-permute-done.12 = bf16[96,2048]{1,0:T(8,128)(2,1)S(1)} collective-permute-done((bf16[96,2048]{1,0:T(8,128)(2,1)S(1)}, bf16[96,2048]{1,0:T(8,128)(2,1)S(1)}, u32[]{:S(2)}, u32[]{:S(2)}) %collective-permute-start.12) | collective-permute-done | bytes 393248 | tf_op jit(solution)/shard_map/ppermute | solution.py:23
  174.2 11.6 %collective-permute-done.15 = bf16[96,2048]{1,0:T(8,128)(2,1)S(1)} collective-permute-done((bf16[96,2048]{1,0:T(8,128)(2,1)S(1)}, bf16[96,2048]{1,0:T(8,128)(2,1)S(1)}, u32[]{:S(2)}, u32[]{:S(2)}) %collective-permute-start.15) | collective-permute-done | bytes 393248 | tf_op jit(solution)/shard_map/ppermute | solution.py:23
  186.9 12.9 %collective-permute-done.16 = bf16[96,2048]{1,0:T(8,128)(2,1)S(1)} collective-permute-done((bf16[96,2048]{1,0:T(8,128)(2,1)S(1)}, bf16[96,2048]{1,0:T(8,128)(2,1)S(1)}, u32[]{:S(2)}, u32[]{:S(2)}) %collective-permute-start.16) | collective-permute-done | bytes 393248 | tf_op jit(solution)/shard_map/ppermute | solution.py:23
  201.9 12.0 %collective-permute-done.19 = bf16[96,2048]{1,0:T(8,128)(2,1)S(1)} collective-permute-done((bf16[96,2048]{1,0:T(8,128)(2,1)S(1)}, bf16[96,2048]{1,0:T(8,128)(2,1)S(1)}, u32[]{:S(2)}, u32[]{:S(2)}) %collective-permute-start.19) | collective-permute-done | bytes 393248 | tf_op jit(solution)/shard_map/ppermute | solution.py:23
  217.1 11.1 %collective-permute-done.20 = bf16[96,2048]{1,0:T(8,128)(2,1)S(1)} collective-permute-done((bf16[96,2048]{1,0:T(8,128)(2,1)S(1)}, bf16[96,2048]{1,0:T(8,128)(2,1)S(1)}, u32[]{:S(2)}, u32[]{:S(2)}) %collective-permute-start.20) | collective-permute-done | bytes 393248 | tf_op jit(solution)/shard_map/ppermute | solution.py:23
  259.7 11.2 %collective-permute-done.24 = bf16[96,2048]{1,0:T(8,128)(2,1)S(1)} collective-permute-done((bf16[96,2048]{1,0:T(8,128)(2,1)S(1)}, bf16[96,2048]{1,0:T(8,128)(2,1)S(1)}, u32[]{:S(2)}, u32[]{:S(2)}) %collective-permute-start.24) | collective-permute-done | bytes 393248 | tf_op jit(solution)/shard_map/ppermute | solution.py:23
  271.1 12.3 %collective-permute-done.25 = bf16[96,2048]{1,0:T(8,128)(2,1)S(1)} collective-permute-done((bf16[96,2048]{1,0:T(8,128)(2,1)S(1)}, bf16[96,2048]{1,0:T(8,128)(2,1)S(1)}, u32[]{:S(2)}, u32[]{:S(2)}) %collective-permute-start.25) | collective-permute-done | bytes 393248 | tf_op jit(solution)/shard_map/ppermute | solution.py:23
  283.6 13.1 %collective-permute-done.26 = bf16[96,2048]{1,0:T(8,128)(2,1)S(1)} collective-permute-done((bf16[96,2048]{1,0:T(8,128)(2,1)S(1)}, bf16[96,2048]{1,0:T(8,128)(2,1)S(1)}, u32[]{:S(2)}, u32[]{:S(2)}) %collective-permute-start.26) | collective-permute-done | bytes 393248 | tf_op jit(solution)/shard_map/ppermute | solution.py:23
  297.3 12.7 %collective-permute-done.27 = bf16[96,2048]{1,0:T(8,128)(2,1)S(1)} collective-permute-done((bf16[96,2048]{1,0:T(8,128)(2,1)S(1)}, bf16[96,2048]{1,0:T(8,128)(2,1)S(1)}, u32[]{:S(2)}, u32[]{:S(2)}) %collective-permute-start.27) | collective-permute-done | bytes 393248 | tf_op jit(solution)/shard_map/ppermute | solution.py:23
  311.3 10.8 %collective-permute-done.28 = bf16[96,2048]{1,0:T(8,128)(2,1)S(1)} collective-permute-done((bf16[96,2048]{1,0:T(8,128)(2,1)S(1)}, bf16[96,2048]{1,0:T(8,128)(2,1)S(1)}, u32[]{:S(2)}, u32[]{:S(2)}) %collective-permute-start.28) | collective-permute-done | bytes 393248 | tf_op jit(solution)/shard_map/ppermute | solution.py:23
  347.2 11.1 %fusion.19 = bf16[384,2048]{1,0:T(8,128)(2,1)} fusion(bf16[2048,4224]{1,0:T(8,128)(2,1)} %all-gather.11.cloned.1.call-done, bf16[384,1408]{1,0:T(8,128)(2,1)S(1)} %get-tuple-element.440, bf16[384,1408]{1,0:T(8,128)(2,1)S(1)} %get-tuple-element.439), kind=kOutput, calls=%fused_computation.28 | convolution fusion | flops 4434296832 | bytes 15269888 | tf_op jit(solution)/shard_map/dot_general | solution.py:31
  361.3 12.9 %collective-permute-done.30 = bf16[96,2048]{1,0:T(8,128)(2,1)S(1)} collective-permute-done((bf16[96,2048]{1,0:T(8,128)(2,1)S(1)}, bf16[96,2048]{1,0:T(8,128)(2,1)S(1)}, u32[]{:S(2)}, u32[]{:S(2)}) %collective-permute-start.30) | collective-permute-done | bytes 393248 | tf_op jit(solution)/shard_map/ppermute | solution.py:23
  486.5 11.4 %collective-permute-done.46 = bf16[96,2048]{1,0:T(8,128)(2,1)S(1)} collective-permute-done((bf16[96,2048]{1,0:T(8,128)(2,1)S(1)}, bf16[96,2048]{1,0:T(8,128)(2,1)S(1)}, u32[]{:S(2)}, u32[]{:S(2)}) %collective-permute-start.46) | collective-permute-done | bytes 393248 | tf_op jit(solution)/shard_map/ppermute | solution.py:23
  501.8 10.5 %collective-permute-done.47 = bf16[96,2048]{1,0:T(8,128)(2,1)S(1)} collective-permute-done((bf16[96,2048]{1,0:T(8,128)(2,1)S(1)}, bf16[96,2048]{1,0:T(8,128)(2,1)S(1)}, u32[]{:S(2)}, u32[]{:S(2)}) %collective-permute-start.47) | collective-permute-done | bytes 393248 | tf_op jit(solution)/shard_map/ppermute | solution.py:23
  545.7 10.5 %fusion.22 = bf16[384,2048]{1,0:T(8,128)(2,1)} fusion(bf16[384,2816]{1,0:T(8,128)(2,1)S(1)} %pad_maximum_fusion.2.refs_2_, bf16[2048,4224]{1,0:T(8,128)(2,1)} %all-gather.7.cloned.1.call-done), kind=kOutput, calls=%fused_computation.29 | convolution fusion | flops 4429971456 | bytes 15269888 | tf_op jit(solution)/shard_map/dot_general | solution.py:31
  559.5 11.8 %shard_map.209 = bf16[1024,4224]{1,0:T(8,128)(2,1)} custom-call(s32[1]{0:T(128)} %bitcast.26._, bf16[384,2048]{1,0:T(8,128)(2,1)S(1)} %pad_maximum_fusion.4.refs_0_, bf16[384,1024]{1,0:T(8,128)(2,1)S(1)} %copy-done.29, bf16[384,2816]{1,0:T(8,128)(2,1)S(1)} %pad_maximum_fusion.2.refs_2_, bf16[384,2816]{1,0:T(8,128)(2,1)S(1)} %collective-permute-done.52.refs_3_, ...), custom_call_target="tpu_custom_call" | custom-call | bytes 42240000 | tf_op jit(solution)/shard_map/pallas_call | solution.py:345
  574.9 12.2 %collective-permute-done.55 = bf16[96,2048]{1,0:T(8,128)(2,1)} collective-permute-done((bf16[96,2048]{1,0:T(8,128)(2,1)}, bf16[96,2048]{1,0:T(8,128)(2,1)}, u32[]{:S(2)}, u32[]{:S(2)}) %collective-permute-start.55) | collective-permute-done | bytes 393248 | tf_op jit(solution)/shard_map/ppermute | solution.py:23
  612.9 13.1 %collective-permute-done.58 = bf16[96,2048]{1,0:T(8,128)(2,1)S(1)} collective-permute-done((bf16[96,2048]{1,0:T(8,128)(2,1)S(1)}, bf16[96,2048]{1,0:T(8,128)(2,1)S(1)}, u32[]{:S(2)}, u32[]{:S(2)}) %collective-permute-start.58) | collective-permute-done | bytes 393248 | tf_op jit(solution)/shard_map/ppermute | solution.py:23
  667.3 10.2 %collective-permute-done.64 = bf16[96,2048]{1,0:T(8,128)(2,1)S(1)} collective-permute-done((bf16[96,2048]{1,0:T(8,128)(2,1)S(1)}, bf16[96,2048]{1,0:T(8,128)(2,1)S(1)}, u32[]{:S(2)}, u32[]{:S(2)}) %collective-permute-start.64) | collective-permute-done | bytes 393248 | tf_op jit(solution)/shard_map/ppermute | solution.py:23
  (573 shorter events, 424.3 us)
Async XLA Ops:
  7.2 53.5 %all-gather.5.cloned.1.call-start = ((), (), s32[]{:S(2)}) async-start(), calls=%async_computation.5 | async-start | bytes 5898240 | tf_op jit(solution)/shard_map/all_gather | solution.py:470
  12.5 146.0 %all-gather.7.cloned.1.call-start = ((), (), s32[]{:S(2)}) async-start(), calls=%async_computation.6 | async-start | bytes 19464192 | tf_op jit(solution)/shard_map/all_gather | solution.py:470
  12.5 14.4 %collective-permute-start = (bf16[96,2048]{1,0:T(8,128)(2,1)S(1)}, bf16[96,2048]{1,0:T(8,128)(2,1)S(1)}, u32[]{:S(2)}, u32[]{:S(2)}) collective-permute-start(bf16[96,2048]{1,0:T(8,128)(2,1)S(1)} %select_bitcast_fusion.5), channel_id=1, source_target_pairs={{0,1},{1,2},{2,3},{3,0},{4,5},{5,6},{6,7},{7,4},{8,9},{9,10},{10,1... | collective-permute-start | bytes 1179656 | tf_op jit(solution)/shard_map/ppermute | solution.py:23
  42.7 172.6 %all-gather.9.cloned.1.call-start = ((), (), s32[]{:S(2)}) async-start(), calls=%async_computation.7 | async-start | bytes 5898240 | tf_op jit(solution)/shard_map/all_gather | solution.py:470
  97.4 235.4 %all-gather.11.cloned.1.call-start = ((), (), s32[]{:S(2)}) async-start(), calls=%async_computation.8 | async-start | bytes 19464192 | tf_op jit(solution)/shard_map/all_gather | solution.py:470
  142.2 15.4 %collective-permute-start.13 = (bf16[384,1024]{1,0:T(8,128)(2,1)S(1)}, bf16[384,1024]{1,0:T(8,128)(2,1)S(1)}, u32[]{:S(2)}, u32[]{:S(2)}) collective-permute-start(bf16[384,1024]{1,0:T(8,128)(2,1)S(1)} %maximum_select_fusion), channel_id=1, source_target_pairs={{0,16},{16,0},{1,17},{17,1},{2,18},{18,2},{3,19},{19,3},{4,20},{20... | collective-permute-start | bytes 2359304 | tf_op jit(solution)/shard_map/ppermute | solution.py:27
  185.9 14.8 %collective-permute-start.18 = (bf16[384,1408]{1,0:T(8,128)(2,1)S(1)}, bf16[384,1408]{1,0:T(8,128)(2,1)S(1)}, u32[]{:S(2)}, u32[]{:S(2)}) collective-permute-start(bf16[384,1408]{1,0:T(8,128)(2,1)S(1)} %fusion.37.refs_6_), channel_id=1, source_target_pairs={{0,16},{16,0},{1,17},{17,1},{2,18},{18,2},{3,19},{19,3},{4,20},{20... | collective-permute-start | bytes 3244040 | tf_op jit(solution)/shard_map/ppermute | solution.py:27
  186.4 13.4 %collective-permute-start.17 = (bf16[384,1024]{1,0:T(8,128)(2,1)S(1)}, bf16[384,1024]{1,0:T(8,128)(2,1)S(1)}, u32[]{:S(2)}, u32[]{:S(2)}) collective-permute-start(bf16[384,1024]{1,0:T(8,128)(2,1)S(1)} %maximum_select_fusion.1), channel_id=1, source_target_pairs={{0,16},{16,0},{1,17},{17,1},{2,18},{18,2},{3,19},{19,3},{4,20},{20... | collective-permute-start | bytes 2359304 | tf_op jit(solution)/shard_map/ppermute | solution.py:27
  215.3 282.7 %reduce-scatter.6.cloned.1.call-start = ((), (), s32[]{:S(2)}) async-start(), calls=%async_computation.9 | async-start | bytes 7208960 | tf_op jit(solution)/shard_map/reduce_scatter | solution.py:363
  359.4 17.5 %collective-permute-start.31 = (bf16[384,2816]{1,0:T(8,128)(2,1)S(1)}, bf16[384,2816]{1,0:T(8,128)(2,1)S(1)}, u32[]{:S(2)}, u32[]{:S(2)}) collective-permute-start(bf16[384,2816]{1,0:T(8,128)(2,1)S(1)} %pad_maximum_fusion.1.refs_2_), channel_id=1, source_target_pairs={{0,16},{16,0},{1,17},{17,1},{2,18},{18,2},{3,19},{19,3},{4,20},{20... | collective-permute-start | bytes 6488072 | tf_op jit(solution)/shard_map/ppermute | solution.py:27
  359.5 16.5 %collective-permute-start.32 = (bf16[384,1408]{1,0:T(8,128)(2,1)S(1)}, bf16[384,1408]{1,0:T(8,128)(2,1)S(1)}, u32[]{:S(2)}, u32[]{:S(2)}) collective-permute-start(bf16[384,1408]{1,0:T(8,128)(2,1)S(1)} %get-tuple-element.271.refs_2_), channel_id=1, source_target_pairs={{0,16},{16,0},{1,17},{17,1},{2,18},{18,2},{3,19},{19,3},{4,20},{20... | collective-permute-start | bytes 3244040 | tf_op jit(solution)/shard_map/ppermute | solution.py:27
  360.3 13.9 %collective-permute-start.33 = (bf16[384,1024]{1,0:T(8,128)(2,1)S(1)}, bf16[384,1024]{1,0:T(8,128)(2,1)S(1)}, u32[]{:S(2)}, u32[]{:S(2)}) collective-permute-start(bf16[384,1024]{1,0:T(8,128)(2,1)S(1)} %maximum_select_fusion.2), channel_id=1, source_target_pairs={{0,16},{16,0},{1,17},{17,1},{2,18},{18,2},{3,19},{19,3},{4,20},{20... | collective-permute-start | bytes 2359304 | tf_op jit(solution)/shard_map/ppermute | solution.py:27
  360.8 14.3 %collective-permute-start.34 = (bf16[384,1024]{1,0:T(8,128)(2,1)S(1)}, bf16[384,1024]{1,0:T(8,128)(2,1)S(1)}, u32[]{:S(2)}, u32[]{:S(2)}) collective-permute-start(bf16[384,1024]{1,0:T(8,128)(2,1)S(1)} %maximum_select_fusion.3), channel_id=1, source_target_pairs={{0,16},{16,0},{1,17},{17,1},{2,18},{18,2},{3,19},{19,3},{4,20},{20... | collective-permute-start | bytes 2359304 | tf_op jit(solution)/shard_map/ppermute | solution.py:27
  392.8 119.6 %reduce-scatter.8.cloned.1.call-start = ((), (), s32[]{:S(2)}) async-start(), calls=%async_computation.10 | async-start | bytes 3604480 | tf_op jit(solution)/shard_map/reduce_scatter | solution.py:363
  412.1 162.7 %reduce-scatter.10.cloned.1.call-start = ((), (), s32[]{:S(2)}) async-start(), calls=%async_computation.11 | async-start | bytes 2949120 | tf_op jit(solution)/shard_map/reduce_scatter | solution.py:363
  434.8 22.1 %collective-permute-start.40 = (bf16[384,1024]{1,0:T(8,128)(2,1)S(1)}, bf16[384,1024]{1,0:T(8,128)(2,1)S(1)}, u32[]{:S(2)}, u32[]{:S(2)}) collective-permute-start(bf16[384,1024]{1,0:T(8,128)(2,1)S(1)} %maximum_select_fusion.4), channel_id=1, source_target_pairs={{0,16},{16,0},{1,17},{17,1},{2,18},{18,2},{3,19},{19,3},{4,20},{20... | collective-permute-start | bytes 2359304 | tf_op jit(solution)/shard_map/ppermute | solution.py:27
  458.2 13.5 %collective-permute-start.44 = (bf16[96,2048]{1,0:T(8,128)(2,1)}, bf16[96,2048]{1,0:T(8,128)(2,1)}, u32[]{:S(2)}, u32[]{:S(2)}) collective-permute-start(bf16[96,2048]{1,0:T(8,128)(2,1)} %slice.553), channel_id=1, source_target_pairs={{0,1},{1,2},{2,3},{3,0},{4,5},{5,6},{6,7},{7,4},{8,9},{9,10},{10,1... | collective-permute-start | bytes 1179656 | tf_op jit(solution)/shard_map/ppermute | solution.py:23
  512.3 151.5 %reduce-scatter.12.cloned.1.call-start = ((), (), s32[]{:S(2)}) async-start(), calls=%async_computation.12 | async-start | bytes 10813440 | tf_op jit(solution)/shard_map/reduce_scatter | solution.py:363
  542.9 15.5 %collective-permute-start.52 = (bf16[384,2816]{1,0:T(8,128)(2,1)S(1)}, bf16[384,2816]{1,0:T(8,128)(2,1)S(1)}, u32[]{:S(2)}, u32[]{:S(2)}) collective-permute-start(bf16[384,2816]{1,0:T(8,128)(2,1)S(1)} %pad_maximum_fusion.2.refs_2_), channel_id=1, source_target_pairs={{0,16},{16,0},{1,17},{17,1},{2,18},{18,2},{3,19},{19,3},{4,20},{20... | collective-permute-start | bytes 6488072 | tf_op jit(solution)/shard_map/ppermute | solution.py:27
  544.7 13.6 %collective-permute-start.51 = (bf16[96,2048]{1,0:T(8,128)(2,1)}, bf16[96,2048]{1,0:T(8,128)(2,1)}, u32[]{:S(2)}, u32[]{:S(2)}) collective-permute-start(bf16[96,2048]{1,0:T(8,128)(2,1)} %add_convert_fusion.6), channel_id=1, source_target_pairs={{0,1},{1,2},{2,3},{3,0},{4,5},{5,6},{6,7},{7,4},{8,9},{9,10},{10,1... | collective-permute-start | bytes 1179656 | tf_op jit(solution)/shard_map/ppermute | solution.py:23
  572.8 130.4 %reduce-scatter.14.cloned.1.call-start = ((), (), s32[]{:S(2)}) async-start(), calls=%async_computation.13 | async-start | bytes 2949120 | tf_op jit(solution)/shard_map/reduce_scatter | solution.py:363
  612.6 17.5 %collective-permute-start.59 = (bf16[96,2048]{1,0:T(8,128)(2,1)S(1)}, bf16[96,2048]{1,0:T(8,128)(2,1)S(1)}, u32[]{:S(2)}, u32[]{:S(2)}) collective-permute-start(bf16[96,2048]{1,0:T(8,128)(2,1)S(1)} %add_convert_fusion.3), channel_id=1, source_target_pairs={{0,1},{1,2},{2,3},{3,0},{4,5},{5,6},{6,7},{7,4},{8,9},{9,10},{10,1... | collective-permute-start | bytes 1179656 | tf_op jit(solution)/shard_map/ppermute | solution.py:23
  632.0 18.5 %collective-permute-start.72 = (bf16[96,2048]{1,0:T(8,128)(2,1)S(1)}, bf16[96,2048]{1,0:T(8,128)(2,1)S(1)}, u32[]{:S(2)}, u32[]{:S(2)}) collective-permute-start(bf16[96,2048]{1,0:T(8,128)(2,1)S(1)} %get-tuple-element.430), channel_id=1, source_target_pairs={{0,16},{16,0},{1,17},{17,1},{2,18},{18,2},{3,19},{19,3},{4,20},{20... | collective-permute-start | bytes 1179656 | tf_op jit(solution)/shard_map/ppermute | solution.py:27
  650.4 13.3 %collective-permute-start.63 = (bf16[96,2048]{1,0:T(8,128)(2,1)S(1)}, bf16[96,2048]{1,0:T(8,128)(2,1)}, u32[]{:S(2)}, u32[]{:S(2)}) collective-permute-start(bf16[96,2048]{1,0:T(8,128)(2,1)S(1)} %slice.586), channel_id=1, source_target_pairs={{0,1},{1,2},{2,3},{3,0},{4,5},{5,6},{6,7},{7,4},{8,9},{9,10},{10,1... | collective-permute-start | bytes 1179656 | tf_op jit(solution)/shard_map/ppermute | solution.py:23
  (182 other events, 1896.0 us)
Sparse Core Ops, SparseCore 0:
  12.6 44.6 all-gather.4
  59.7 92.0 all-gather.6
  154.3 42.0 all-gather.8
  215.4 90.4 all-gather.10
  392.9 67.4 reduce-scatter.5
  463.9 41.7 reduce-scatter.7
  512.4 38.5 reduce-scatter.9
  572.9 89.1 reduce-scatter.11
  665.7 37.4 reduce-scatter.13

commit v4 on v3

--- a/solution.py
+++ b/solution.py
@@ -80,10 +80,11 @@
     return recv
 
 
-def spread(block, jobs=()):
-    pieces = [block]
+def spread(block, jobs=(), parts=1):
+    pieces = list(jnp.split(block, parts))
     for k in range(lax.axis_size("tensor") - 1):
-        pieces.append(step(pieces[-1], jobs[k] if k < len(jobs) else None))
+        for _ in range(parts):
+            pieces.append(step(pieces[-parts], jobs[k] if k < len(jobs) else None))
     return jnp.concatenate(pieces, axis=0)
 
 
@@ -296,7 +297,7 @@
 
 
 def feed_back_rows(d_gate_up, w_ffn):
-    return (contract(d_gate_up, w_ffn[:, : d_gate_up.shape[1]], 1, 1).astype(BF16),)
+    return (contract(d_gate_up, w_ffn[:, : d_gate_up.shape[1]], 1, 1),)
 
 
 def core_half(rows, at_first, own):
@@ -537,13 +538,15 @@
             w_attn[:, 2 * (q_cols + kv_cols) :][:, :2].T.astype(F32)
         )
         if layer:
-            normed_one = spread((layer_in * normalizer(layer_in) * norm_gain).astype(BF16))
+            normed_one = spread(
+                (layer_in * normalizer(layer_in) * norm_gain).astype(BF16), parts=2
+            )
         else:
             normed_one = (tokens_all * normalizer(tokens_all) * norm_gain).astype(BF16)
         attention = (lambda normed, w: attend(normed, geo, w, q_cols, kv_cols), normed_one, w_attn)
         out_term, rotated, log_total, mixed = upstream_ring.run(*attention)
         middle = layer_in + collect(out_term)
-        normed_two = spread((middle * normalizer(middle) * ffn_gain).astype(BF16))
+        normed_two = spread((middle * normalizer(middle) * ffn_gain).astype(BF16), parts=2)
         others = {}
         if layer == 0:
             normed_two, upstream_ring.value = barrier(normed_two, upstream_ring.value)

time: 730 us -> 727 us (level)
  waiting for transfers between devices: 428 us -> 416 us
  local copies, waits for them, and re-layouts: 45.3 us -> 53.9 us
    ppermute x54 -> x63, waiting for transfers between devices: 419 us -> 408 us  [turn(): lax.ppermute(value, axis, [(i, (i + steps) % count) for i in range(count)])]
    unnamed x254 -> x215, local copies, waits for them, and re-layouts: 35.3 us -> 37.3 us
  transfers between devices with their start and end apart: 86 -> 95, of which waited for: 55 -> 63; matrix products, arithmetic and copies ran while one was open for 19% -> 21% of each run, Pallas kernels for 8% -> 8%
where the time goes in v4:
time: 727 us; the launch traced here: 717 us
  waiting for transfers between devices  416 us (57%)
  matrix products  78.6 us (11%)
  other arithmetic  75.2 us (10%)
  Pallas kernels  57.4 us (8%)
  local copies, waits for them, and re-layouts  53.9 us (7%)
  starting transfers between devices  19.8 us (3%)
  between operations  16.4 us (2%)
    ppermute x63, waiting for transfers between devices, turn(): lax.ppermute(value, axis, [(i, (i + steps) % count) for i in range(count)])  408 us
    dot_general x8, matrix products, contract(): lax.dot_general(left, right, (((left_dim,), (right_dim,)), ((), ())), pre...  38.5 us
    unnamed x215, local copies, waits for them, and re-layouts  37.3 us
    pallas_call x5, Pallas kernels, weight_grads(): pl.pallas_call(weight_grads_kernel, grid_spec=pltpu.PrefetchScalarGridSpe...  37.1 us
    dot_general x2, matrix products, feed(): jnp.dot(normed_two, w_ffn[:, :2 * units], preferred_element_type=F32)  16.7 us
  transfers between devices with their start and end apart: 95, of which 63 were waited for; matrix products, arithmetic and copies ran while one was open for 21% of the time, Pallas kernels for 8%

profile of v4, /device:TPU:0, one launch (start us, length us, event | category | flops | bytes accessed | tf_op | source)
XLA Modules:
  0.0 716.8 jit_solution(963173047847035983)
XLA Ops:
  16.3 10.7 %collective-permute-done = bf16[96,2048]{1,0:T(8,128)(2,1)} collective-permute-done((bf16[96,2048]{1,0:T(8,128)(2,1)S(1)}, bf16[96,2048]{1,0:T(8,128)(2,1)}, u32[]{:S(2)}, u32[]{:S(2)}) %collective-permute-start) | collective-permute-done | bytes 393248 | tf_op jit(solution)/shard_map/ppermute | solution.py:23
  46.7 11.4 %collective-permute-done.3 = bf16[96,2048]{1,0:T(8,128)(2,1)S(1)} collective-permute-done((bf16[96,2048]{1,0:T(8,128)(2,1)S(1)}, bf16[96,2048]{1,0:T(8,128)(2,1)S(1)}, u32[]{:S(2)}, u32[]{:S(2)}) %collective-permute-start.3) | collective-permute-done | bytes 393248 | tf_op jit(solution)/shard_map/ppermute | solution.py:23
  74.2 10.6 %collective-permute-done.6 = bf16[96,2048]{1,0:T(8,128)(2,1)S(1)} collective-permute-done((bf16[96,2048]{1,0:T(8,128)(2,1)S(1)}, bf16[96,2048]{1,0:T(8,128)(2,1)S(1)}, u32[]{:S(2)}, u32[]{:S(2)}) %collective-permute-start.6) | collective-permute-done | bytes 393248 | tf_op jit(solution)/shard_map/ppermute | solution.py:23
  85.0 9.7 %collective-permute-done.7 = bf16[96,2048]{1,0:T(8,128)(2,1)S(1)} collective-permute-done((bf16[96,2048]{1,0:T(8,128)(2,1)S(1)}, bf16[96,2048]{1,0:T(8,128)(2,1)S(1)}, u32[]{:S(2)}, u32[]{:S(2)}) %collective-permute-start.7) | collective-permute-done | bytes 393248 | tf_op jit(solution)/shard_map/ppermute | solution.py:23
  95.7 9.8 %collective-permute-done.8 = bf16[96,2048]{1,0:T(8,128)(2,1)} collective-permute-done((bf16[96,2048]{1,0:T(8,128)(2,1)}, bf16[96,2048]{1,0:T(8,128)(2,1)}, u32[]{:S(2)}, u32[]{:S(2)}) %collective-permute-start.8) | collective-permute-done | bytes 393248 | tf_op jit(solution)/shard_map/ppermute | solution.py:23
  141.4 12.5 %collective-permute-done.15 = bf16[96,2048]{1,0:T(8,128)(2,1)S(1)} collective-permute-done((bf16[96,2048]{1,0:T(8,128)(2,1)S(1)}, bf16[96,2048]{1,0:T(8,128)(2,1)S(1)}, u32[]{:S(2)}, u32[]{:S(2)}) %collective-permute-start.15) | collective-permute-done | bytes 393248 | tf_op jit(solution)/shard_map/ppermute | solution.py:23
  172.4 11.8 %collective-permute-done.18 = bf16[96,2048]{1,0:T(8,128)(2,1)S(1)} collective-permute-done((bf16[96,2048]{1,0:T(8,128)(2,1)S(1)}, bf16[96,2048]{1,0:T(8,128)(2,1)S(1)}, u32[]{:S(2)}, u32[]{:S(2)}) %collective-permute-start.18) | collective-permute-done | bytes 393248 | tf_op jit(solution)/shard_map/ppermute | solution.py:23
  186.7 12.9 %collective-permute-done.19 = bf16[96,2048]{1,0:T(8,128)(2,1)S(1)} collective-permute-done((bf16[96,2048]{1,0:T(8,128)(2,1)S(1)}, bf16[96,2048]{1,0:T(8,128)(2,1)S(1)}, u32[]{:S(2)}, u32[]{:S(2)}) %collective-permute-start.19) | collective-permute-done | bytes 393248 | tf_op jit(solution)/shard_map/ppermute | solution.py:23
  201.7 12.0 %collective-permute-done.22 = bf16[96,2048]{1,0:T(8,128)(2,1)S(1)} collective-permute-done((bf16[96,2048]{1,0:T(8,128)(2,1)S(1)}, bf16[96,2048]{1,0:T(8,128)(2,1)S(1)}, u32[]{:S(2)}, u32[]{:S(2)}) %collective-permute-start.22) | collective-permute-done | bytes 393248 | tf_op jit(solution)/shard_map/ppermute | solution.py:23
  261.3 11.4 %collective-permute-done.30 = bf16[96,2048]{1,0:T(8,128)(2,1)S(1)} collective-permute-done((bf16[96,2048]{1,0:T(8,128)(2,1)S(1)}, bf16[96,2048]{1,0:T(8,128)(2,1)S(1)}, u32[]{:S(2)}, u32[]{:S(2)}) %collective-permute-start.30) | collective-permute-done | bytes 393248 | tf_op jit(solution)/shard_map/ppermute | solution.py:23
  273.7 11.8 %collective-permute-done.31 = bf16[96,2048]{1,0:T(8,128)(2,1)S(1)} collective-permute-done((bf16[96,2048]{1,0:T(8,128)(2,1)S(1)}, bf16[96,2048]{1,0:T(8,128)(2,1)S(1)}, u32[]{:S(2)}, u32[]{:S(2)}) %collective-permute-start.31) | collective-permute-done | bytes 393248 | tf_op jit(solution)/shard_map/ppermute | solution.py:23
  287.3 10.8 %collective-permute-done.32 = bf16[96,2048]{1,0:T(8,128)(2,1)S(1)} collective-permute-done((bf16[96,2048]{1,0:T(8,128)(2,1)S(1)}, bf16[96,2048]{1,0:T(8,128)(2,1)S(1)}, u32[]{:S(2)}, u32[]{:S(2)}) %collective-permute-start.32) | collective-permute-done | bytes 393248 | tf_op jit(solution)/shard_map/ppermute | solution.py:23
  357.2 12.9 %collective-permute-done.39 = bf16[96,2048]{1,0:T(8,128)(2,1)S(1)} collective-permute-done((bf16[96,2048]{1,0:T(8,128)(2,1)S(1)}, bf16[96,2048]{1,0:T(8,128)(2,1)S(1)}, u32[]{:S(2)}, u32[]{:S(2)}) %collective-permute-start.39) | collective-permute-done | bytes 393248 | tf_op jit(solution)/shard_map/ppermute | solution.py:23
  379.4 9.0 %shard_map.205 = bf16[1024,2816]{1,0:T(8,128)(2,1)} custom-call(s32[1]{0:T(128)} %bitcast.26._, bf16[384,2048]{1,0:T(8,128)(2,1)} %constant_dynamic-update-slice_fusion.20.refs_0_, bf16[384,1024]{1,0:T(8,128)(2,1)S(1)} %copy-done.20, bf16[384,2816]{1,0:T(8,128)(2,1)S(1)} %copy-done.3, bf16[384,2816]{1,0:T(8,128)(2,1)S(1)} %copy-done.7), custom_call_target="tpu_custom_call" | custom-call | bytes 28160000 | tf_op jit(solution)/shard_map/pallas_call | solution.py:346
  430.8 9.1 %collective-permute-done.48 = bf16[96,2048]{1,0:T(8,128)(2,1)S(1)} collective-permute-done((bf16[96,2048]{1,0:T(8,128)(2,1)S(1)}, bf16[96,2048]{1,0:T(8,128)(2,1)S(1)}, u32[]{:S(2)}, u32[]{:S(2)}) %collective-permute-start.48) | collective-permute-done | bytes 393248 | tf_op jit(solution)/shard_map/ppermute | solution.py:23
  471.4 9.9 %collective-permute-done.54 = bf16[96,2048]{1,0:T(8,128)(2,1)S(1)} collective-permute-done((bf16[96,2048]{1,0:T(8,128)(2,1)S(1)}, bf16[96,2048]{1,0:T(8,128)(2,1)S(1)}, u32[]{:S(2)}, u32[]{:S(2)}) %collective-permute-start.54) | collective-permute-done | bytes 393248 | tf_op jit(solution)/shard_map/ppermute | solution.py:23
  482.4 11.6 %collective-permute-done.55 = bf16[96,2048]{1,0:T(8,128)(2,1)} collective-permute-done((bf16[96,2048]{1,0:T(8,128)(2,1)S(1)}, bf16[96,2048]{1,0:T(8,128)(2,1)}, u32[]{:S(2)}, u32[]{:S(2)}) %collective-permute-start.55) | collective-permute-done | bytes 393248 | tf_op jit(solution)/shard_map/ppermute | solution.py:23
  498.0 10.6 %collective-permute-done.56 = bf16[96,2048]{1,0:T(8,128)(2,1)} collective-permute-done((bf16[96,2048]{1,0:T(8,128)(2,1)S(1)}, bf16[96,2048]{1,0:T(8,128)(2,1)}, u32[]{:S(2)}, u32[]{:S(2)}) %collective-permute-start.56) | collective-permute-done | bytes 393248 | tf_op jit(solution)/shard_map/ppermute | solution.py:23
  508.8 9.8 %collective-permute-done.57 = bf16[96,2048]{1,0:T(8,128)(2,1)} collective-permute-done((bf16[96,2048]{1,0:T(8,128)(2,1)}, bf16[96,2048]{1,0:T(8,128)(2,1)}, u32[]{:S(2)}, u32[]{:S(2)}) %collective-permute-start.57) | collective-permute-done | bytes 393248 | tf_op jit(solution)/shard_map/ppermute | solution.py:23
  555.9 12.5 %shard_map.209 = bf16[1024,4224]{1,0:T(8,128)(2,1)} custom-call(s32[1]{0:T(128)} %bitcast.26._, bf16[384,2048]{1,0:T(8,128)(2,1)} %constant_dynamic-update-slice_fusion.2.refs_0_, bf16[384,1024]{1,0:T(8,128)(2,1)S(1)} %copy-done.16, bf16[384,2816]{1,0:T(8,128)(2,1)S(1)} %pad_maximum_fusion.2.refs_2_, bf16[384,2816]{1,0:T(8,128)(2,1)S(1)} %collective-permute-done.61.refs_3_, ...), custom_call_target="tpu_custom_call" | custom-call | bytes 42240000 | tf_op jit(solution)/shard_map/pallas_call | solution.py:346
  570.9 12.5 %collective-permute-done.64 = bf16[96,2048]{1,0:T(8,128)(2,1)} collective-permute-done((bf16[96,2048]{1,0:T(8,128)(2,1)}, bf16[96,2048]{1,0:T(8,128)(2,1)}, u32[]{:S(2)}, u32[]{:S(2)}) %collective-permute-start.64) | collective-permute-done | bytes 393248 | tf_op jit(solution)/shard_map/ppermute | solution.py:23
  586.3 10.0 %collective-permute-done.65 = bf16[96,2048]{1,0:T(8,128)(2,1)S(1)} collective-permute-done((bf16[96,2048]{1,0:T(8,128)(2,1)S(1)}, bf16[96,2048]{1,0:T(8,128)(2,1)S(1)}, u32[]{:S(2)}, u32[]{:S(2)}) %collective-permute-start.65) | collective-permute-done | bytes 393248 | tf_op jit(solution)/shard_map/ppermute | solution.py:23
  611.4 13.5 %collective-permute-done.67 = bf16[96,2048]{1,0:T(8,128)(2,1)S(1)} collective-permute-done((bf16[96,2048]{1,0:T(8,128)(2,1)S(1)}, bf16[96,2048]{1,0:T(8,128)(2,1)S(1)}, u32[]{:S(2)}, u32[]{:S(2)}) %collective-permute-start.67) | collective-permute-done | bytes 393248 | tf_op jit(solution)/shard_map/ppermute | solution.py:23
  665.1 11.9 %collective-permute-done.73 = bf16[96,2048]{1,0:T(8,128)(2,1)S(1)} collective-permute-done((bf16[96,2048]{1,0:T(8,128)(2,1)S(1)}, bf16[96,2048]{1,0:T(8,128)(2,1)S(1)}, u32[]{:S(2)}, u32[]{:S(2)}) %collective-permute-start.73) | collective-permute-done | bytes 393248 | tf_op jit(solution)/shard_map/ppermute | solution.py:23
  (555 shorter events, 431.5 us)
Async XLA Ops:
  7.2 52.5 %all-gather.5.cloned.1.call-start = ((), (), s32[]{:S(2)}) async-start(), calls=%async_computation.5 | async-start | bytes 5898240 | tf_op jit(solution)/shard_map/all_gather | solution.py:471
  12.5 143.8 %all-gather.7.cloned.1.call-start = ((), (), s32[]{:S(2)}) async-start(), calls=%async_computation.6 | async-start | bytes 19464192 | tf_op jit(solution)/shard_map/all_gather | solution.py:471
  12.5 14.5 %collective-permute-start = (bf16[96,2048]{1,0:T(8,128)(2,1)S(1)}, bf16[96,2048]{1,0:T(8,128)(2,1)}, u32[]{:S(2)}, u32[]{:S(2)}) collective-permute-start(bf16[96,2048]{1,0:T(8,128)(2,1)S(1)} %select_bitcast_fusion.5), channel_id=1, source_target_pairs={{0,1},{1,2},{2,3},{3,0},{4,5},{5,6},{6,7},{7,4},{8,9},{9,10},{10,1... | collective-permute-start | bytes 1179656 | tf_op jit(solution)/shard_map/ppermute | solution.py:23
  29.3 13.5 %collective-permute-start.1 = (bf16[96,2048]{1,0:T(8,128)(2,1)}, bf16[96,2048]{1,0:T(8,128)(2,1)S(1)}, u32[]{:S(2)}, u32[]{:S(2)}) collective-permute-start(bf16[96,2048]{1,0:T(8,128)(2,1)} %collective-permute-done), channel_id=1, source_target_pairs={{0,1},{1,2},{2,3},{3,0},{4,5},{5,6},{6,7},{7,4},{8,9},{9,10},{10,1... | collective-permute-start | bytes 1179656 | tf_op jit(solution)/shard_map/ppermute | solution.py:23
  42.9 173.1 %all-gather.9.cloned.1.call-start = ((), (), s32[]{:S(2)}) async-start(), calls=%async_computation.7 | async-start | bytes 5898240 | tf_op jit(solution)/shard_map/all_gather | solution.py:471
  95.6 232.9 %all-gather.11.cloned.1.call-start = ((), (), s32[]{:S(2)}) async-start(), calls=%async_computation.8 | async-start | bytes 19464192 | tf_op jit(solution)/shard_map/all_gather | solution.py:471
  140.4 15.1 %collective-permute-start.16 = (bf16[384,1024]{1,0:T(8,128)(2,1)S(1)}, bf16[384,1024]{1,0:T(8,128)(2,1)S(1)}, u32[]{:S(2)}, u32[]{:S(2)}) collective-permute-start(bf16[384,1024]{1,0:T(8,128)(2,1)S(1)} %maximum_select_fusion), channel_id=1, source_target_pairs={{0,16},{16,0},{1,17},{17,1},{2,18},{18,2},{3,19},{19,3},{4,20},{20... | collective-permute-start | bytes 2359304 | tf_op jit(solution)/shard_map/ppermute | solution.py:27
  184.3 16.2 %collective-permute-start.21 = (bf16[384,1408]{1,0:T(8,128)(2,1)S(1)}, bf16[384,1408]{1,0:T(8,128)(2,1)S(1)}, u32[]{:S(2)}, u32[]{:S(2)}) collective-permute-start(bf16[384,1408]{1,0:T(8,128)(2,1)S(1)} %fusion.31.refs_6_), channel_id=1, source_target_pairs={{0,16},{16,0},{1,17},{17,1},{2,18},{18,2},{3,19},{19,3},{4,20},{20... | collective-permute-start | bytes 3244040 | tf_op jit(solution)/shard_map/ppermute | solution.py:27
  215.9 278.1 %reduce-scatter.6.cloned.1.call-start = ((), (), s32[]{:S(2)}) async-start(), calls=%async_computation.9 | async-start | bytes 7208960 | tf_op jit(solution)/shard_map/reduce_scatter | solution.py:364
  352.0 20.9 %collective-permute-start.40 = (bf16[384,2816]{1,0:T(8,128)(2,1)S(1)}, bf16[384,2816]{1,0:T(8,128)(2,1)S(1)}, u32[]{:S(2)}, u32[]{:S(2)}) collective-permute-start(bf16[384,2816]{1,0:T(8,128)(2,1)S(1)} %pad_maximum_fusion.1.refs_2_), channel_id=1, source_target_pairs={{0,16},{16,0},{1,17},{17,1},{2,18},{18,2},{3,19},{19,3},{4,20},{20... | collective-permute-start | bytes 6488072 | tf_op jit(solution)/shard_map/ppermute | solution.py:27
  352.1 19.8 %collective-permute-start.41 = (bf16[384,1408]{1,0:T(8,128)(2,1)S(1)}, bf16[384,1408]{1,0:T(8,128)(2,1)S(1)}, u32[]{:S(2)}, u32[]{:S(2)}) collective-permute-start(bf16[384,1408]{1,0:T(8,128)(2,1)S(1)} %get-tuple-element.271.refs_2_), channel_id=1, source_target_pairs={{0,16},{16,0},{1,17},{17,1},{2,18},{18,2},{3,19},{19,3},{4,20},{20... | collective-permute-start | bytes 3244040 | tf_op jit(solution)/shard_map/ppermute | solution.py:27
  354.8 15.3 %collective-permute-start.42 = (bf16[384,1024]{1,0:T(8,128)(2,1)S(1)}, bf16[384,1024]{1,0:T(8,128)(2,1)S(1)}, u32[]{:S(2)}, u32[]{:S(2)}) collective-permute-start(bf16[384,1024]{1,0:T(8,128)(2,1)S(1)} %maximum_select_fusion.2), channel_id=1, source_target_pairs={{0,16},{16,0},{1,17},{17,1},{2,18},{18,2},{3,19},{19,3},{4,20},{20... | collective-permute-start | bytes 2359304 | tf_op jit(solution)/shard_map/ppermute | solution.py:27
  356.7 14.3 %collective-permute-start.43 = (bf16[384,1024]{1,0:T(8,128)(2,1)S(1)}, bf16[384,1024]{1,0:T(8,128)(2,1)S(1)}, u32[]{:S(2)}, u32[]{:S(2)}) collective-permute-start(bf16[384,1024]{1,0:T(8,128)(2,1)S(1)} %maximum_select_fusion.3), channel_id=1, source_target_pairs={{0,16},{16,0},{1,17},{17,1},{2,18},{18,2},{3,19},{19,3},{4,20},{20... | collective-permute-start | bytes 2359304 | tf_op jit(solution)/shard_map/ppermute | solution.py:27
  388.4 120.3 %reduce-scatter.8.cloned.1.call-start = ((), (), s32[]{:S(2)}) async-start(), calls=%async_computation.10 | async-start | bytes 3604480 | tf_op jit(solution)/shard_map/reduce_scatter | solution.py:364
  407.9 163.0 %reduce-scatter.10.cloned.1.call-start = ((), (), s32[]{:S(2)}) async-start(), calls=%async_computation.11 | async-start | bytes 2949120 | tf_op jit(solution)/shard_map/reduce_scatter | solution.py:364
  430.7 21.9 %collective-permute-start.49 = (bf16[384,1024]{1,0:T(8,128)(2,1)S(1)}, bf16[384,1024]{1,0:T(8,128)(2,1)S(1)}, u32[]{:S(2)}, u32[]{:S(2)}) collective-permute-start(bf16[384,1024]{1,0:T(8,128)(2,1)S(1)} %maximum_select_fusion.4), channel_id=1, source_target_pairs={{0,16},{16,0},{1,17},{17,1},{2,18},{18,2},{3,19},{19,3},{4,20},{20... | collective-permute-start | bytes 2359304 | tf_op jit(solution)/shard_map/ppermute | solution.py:27
  508.7 154.6 %reduce-scatter.12.cloned.1.call-start = ((), (), s32[]{:S(2)}) async-start(), calls=%async_computation.12 | async-start | bytes 10813440 | tf_op jit(solution)/shard_map/reduce_scatter | solution.py:364
  539.4 15.7 %collective-permute-start.61 = (bf16[384,2816]{1,0:T(8,128)(2,1)S(1)}, bf16[384,2816]{1,0:T(8,128)(2,1)S(1)}, u32[]{:S(2)}, u32[]{:S(2)}) collective-permute-start(bf16[384,2816]{1,0:T(8,128)(2,1)S(1)} %pad_maximum_fusion.2.refs_2_), channel_id=1, source_target_pairs={{0,16},{16,0},{1,17},{17,1},{2,18},{18,2},{3,19},{19,3},{4,20},{20... | collective-permute-start | bytes 6488072 | tf_op jit(solution)/shard_map/ppermute | solution.py:27
  541.3 13.8 %collective-permute-start.60 = (bf16[96,2048]{1,0:T(8,128)(2,1)}, bf16[96,2048]{1,0:T(8,128)(2,1)}, u32[]{:S(2)}, u32[]{:S(2)}) collective-permute-start(bf16[96,2048]{1,0:T(8,128)(2,1)} %add_convert_fusion.6), channel_id=1, source_target_pairs={{0,1},{1,2},{2,3},{3,0},{4,5},{5,6},{6,7},{7,4},{8,9},{9,10},{10,1... | collective-permute-start | bytes 1179656 | tf_op jit(solution)/shard_map/ppermute | solution.py:23
  568.8 130.5 %reduce-scatter.14.cloned.1.call-start = ((), (), s32[]{:S(2)}) async-start(), calls=%async_computation.13 | async-start | bytes 2949120 | tf_op jit(solution)/shard_map/reduce_scatter | solution.py:364
  611.2 13.8 %collective-permute-start.67 = (bf16[96,2048]{1,0:T(8,128)(2,1)S(1)}, bf16[96,2048]{1,0:T(8,128)(2,1)S(1)}, u32[]{:S(2)}, u32[]{:S(2)}) collective-permute-start(bf16[96,2048]{1,0:T(8,128)(2,1)S(1)} %collective-permute-done.66), channel_id=1, source_target_pairs={{0,1},{1,2},{2,3},{3,0},{4,5},{5,6},{6,7},{7,4},{8,9},{9,10},{10,1... | collective-permute-start | bytes 1179656 | tf_op jit(solution)/shard_map/ppermute | solution.py:23
  611.2 18.0 %collective-permute-start.68 = (bf16[96,2048]{1,0:T(8,128)(2,1)S(1)}, bf16[96,2048]{1,0:T(8,128)(2,1)S(1)}, u32[]{:S(2)}, u32[]{:S(2)}) collective-permute-start(bf16[96,2048]{1,0:T(8,128)(2,1)S(1)} %add_convert_fusion.3), channel_id=1, source_target_pairs={{0,1},{1,2},{2,3},{3,0},{4,5},{5,6},{6,7},{7,4},{8,9},{9,10},{10,1... | collective-permute-start | bytes 1179656 | tf_op jit(solution)/shard_map/ppermute | solution.py:23
  630.8 18.9 %collective-permute-start.81 = (bf16[96,2048]{1,0:T(8,128)(2,1)S(1)}, bf16[96,2048]{1,0:T(8,128)(2,1)S(1)}, u32[]{:S(2)}, u32[]{:S(2)}) collective-permute-start(bf16[96,2048]{1,0:T(8,128)(2,1)S(1)} %get-tuple-element.430), channel_id=1, source_target_pairs={{0,16},{16,0},{1,17},{17,1},{2,18},{18,2},{3,19},{19,3},{4,20},{20... | collective-permute-start | bytes 1179656 | tf_op jit(solution)/shard_map/ppermute | solution.py:27
  649.5 13.7 %collective-permute-start.72 = (bf16[96,2048]{1,0:T(8,128)(2,1)}, bf16[96,2048]{1,0:T(8,128)(2,1)}, u32[]{:S(2)}, u32[]{:S(2)}) collective-permute-start(bf16[96,2048]{1,0:T(8,128)(2,1)} %slice.591), channel_id=1, source_target_pairs={{0,1},{1,2},{2,3},{3,0},{4,5},{5,6},{6,7},{7,4},{8,9},{9,10},{10,1... | collective-permute-start | bytes 1179656 | tf_op jit(solution)/shard_map/ppermute | solution.py:23
  (164 other events, 1416.8 us)
Sparse Core Ops, SparseCore 0:
  12.6 44.6 all-gather.4
  59.8 92.0 all-gather.6
  154.3 42.0 all-gather.8
  216.0 90.4 all-gather.10
  388.6 67.4 reduce-scatter.5
  459.6 41.7 reduce-scatter.7
  508.8 38.4 reduce-scatter.9
  568.9 89.2 reduce-scatter.11
  663.4 35.8 reduce-scatter.13

commit v5 on v4

--- a/solution.py
+++ b/solution.py
@@ -406,9 +406,8 @@
             normed_two,
             grad_all,
         )
-        grads_jobs = (Job(grads), Job(grads))
+        grads_jobs = (Job(grads),)
         grads_jobs[0].inputs = lambda: (normed_two, swap_job[2], d_gate_up, swap_job[0])
-        grads_jobs[1].inputs = lambda: (grad_all, swap_job[3], hidden, swap_job[1])
         d_norm_two = collect(d_norm_two_all, (swap_job, *grads_jobs))
     reduced = [scatter(job[0]) for job in grads_jobs if job.results]
     d_middle = grad.astype(F32) + norm_back(middle, normalizer(middle), ffn_gain, d_norm_two)
@@ -425,7 +424,9 @@
         aside.accept(aside_job[0])
         aside.taken += 1
     else:
-        grad_attn = spread(d_middle.astype(BF16), (ffn_gain_job, down_job))
+        down_grad = Job(grads, grad_all, swap_job[3], hidden, swap_job[1])
+        grad_attn = spread(d_middle.astype(BF16), (down_grad, down_job, ffn_gain_job))
+        reduced.append(scatter(down_grad[0]))
         aside = CollectRing(down_job[0])
     d_qkv, other_qkv, other_attn, d_norm_one_all = attend_back(
         grad_attn, geo, w_attn, at_first, rotated, log_total
@@ -545,17 +546,19 @@
             normed_one = (tokens_all * normalizer(tokens_all) * norm_gain).astype(BF16)
         attention = (lambda normed, w: attend(normed, geo, w, q_cols, kv_cols), normed_one, w_attn)
         out_term, rotated, log_total, mixed = upstream_ring.run(*attention)
-        middle = layer_in + collect(out_term)
+        others = {}
+        attn_jobs = ()
+        if layer == 0:
+            ring_job = Job(lambda value: (turn(value, "tensor", 1),), upstream_ring.value)
+            attn_jobs = (None, ring_job)
+        middle = layer_in + collect(out_term, attn_jobs)
         normed_two = spread((middle * normalizer(middle) * ffn_gain).astype(BF16), parts=2)
-        others = {}
         if layer == 0:
-            normed_two, upstream_ring.value = barrier(normed_two, upstream_ring.value)
-            others.update(
-                attn=upstream_ring.run(
-                    lambda one, heads: exchange(at_first, (one,), heads), normed_one, mixed
-                )
-            )
-            normed_two, upstream_ring.value = barrier(normed_two, upstream_ring.value)
+            upstream_ring.accept(ring_job[0])
+            upstream_ring.taken += 1
+            swapped = exchange(at_first, barrier(normed_one, normed_two)[:1], mixed)
+            normed_two, *swapped = barrier(normed_two, *swapped)
+            others.update(attn=tuple(swapped))
         gate_up, hidden = feed(normed_two, w_ffn, units)
         down_job = Job(
             lambda hidden, w: (contract(hidden, w[:, 2 * units :], 1, 1).astype(BF16),),

time: 727 us -> 725 us (level)
  transfers between devices with their start and end apart: 95 -> 95, of which waited for: 63 -> 64; matrix products, arithmetic and copies ran while one was open for 21% -> 21% of each run, Pallas kernels for 8% -> 8%
where the time goes in v5:
time: 725 us; the launch traced here: 716 us
  waiting for transfers between devices  415 us (57%)
  matrix products  78.1 us (11%)
  other arithmetic  74.2 us (10%)
  Pallas kernels  58.2 us (8%)
  local copies, waits for them, and re-layouts  52.5 us (7%)
  starting transfers between devices  21.3 us (3%)
  between operations  16.5 us (2%)
    ppermute x63, waiting for transfers between devices, turn(): lax.ppermute(value, axis, [(i, (i + steps) % count) for i in range(count)])  405 us
    dot_general x8, matrix products, contract(): lax.dot_general(left, right, (((left_dim,), (right_dim,)), ((), ())), pre...  37.9 us
    pallas_call x5, Pallas kernels, weight_grads(): pl.pallas_call(weight_grads_kernel, grid_spec=pltpu.PrefetchScalarGridSpe...  37.9 us
    unnamed x215, local copies, waits for them, and re-layouts  35.9 us
    dot_general x2, matrix products, feed(): jnp.dot(normed_two, w_ffn[:, :2 * units], preferred_element_type=F32)  16.7 us
    ppermute x63, starting transfers between devices, turn(): lax.ppermute(value, axis, [(i, (i + steps) % count) for i in range(count)])  15.7 us
  transfers between devices with their start and end apart: 95, of which 64 were waited for; matrix products, arithmetic and copies ran while one was open for 21% of the time, Pallas kernels for 8%

profile of v5, /device:TPU:0, one launch (start us, length us, event | category | flops | bytes accessed | tf_op | source)
XLA Modules:
  0.0 715.7 jit_solution(9523511508811038626)
XLA Ops:
  16.3 10.7 %collective-permute-done = bf16[96,2048]{1,0:T(8,128)(2,1)} collective-permute-done((bf16[96,2048]{1,0:T(8,128)(2,1)S(1)}, bf16[96,2048]{1,0:T(8,128)(2,1)}, u32[]{:S(2)}, u32[]{:S(2)}) %collective-permute-start) | collective-permute-done | bytes 393248 | tf_op jit(solution)/shard_map/ppermute | solution.py:23
  46.7 11.4 %collective-permute-done.3 = bf16[96,2048]{1,0:T(8,128)(2,1)S(1)} collective-permute-done((bf16[96,2048]{1,0:T(8,128)(2,1)S(1)}, bf16[96,2048]{1,0:T(8,128)(2,1)S(1)}, u32[]{:S(2)}, u32[]{:S(2)}) %collective-permute-start.3) | collective-permute-done | bytes 393248 | tf_op jit(solution)/shard_map/ppermute | solution.py:23
  74.2 10.6 %collective-permute-done.6 = bf16[96,2048]{1,0:T(8,128)(2,1)S(1)} collective-permute-done((bf16[96,2048]{1,0:T(8,128)(2,1)S(1)}, bf16[96,2048]{1,0:T(8,128)(2,1)S(1)}, u32[]{:S(2)}, u32[]{:S(2)}) %collective-permute-start.6) | collective-permute-done | bytes 393248 | tf_op jit(solution)/shard_map/ppermute | solution.py:23
  86.0 12.8 %collective-permute-done.7 = bf16[96,2048]{1,0:T(8,128)(2,1)S(1)} collective-permute-done((bf16[96,2048]{1,0:T(8,128)(2,1)S(1)}, bf16[96,2048]{1,0:T(8,128)(2,1)S(1)}, u32[]{:S(2)}, u32[]{:S(2)}) %collective-permute-start.7) | collective-permute-done | bytes 393248 | tf_op jit(solution)/shard_map/ppermute | solution.py:23
  104.1 9.8 %collective-permute-done.9 = bf16[96,2048]{1,0:T(8,128)(2,1)} collective-permute-done((bf16[96,2048]{1,0:T(8,128)(2,1)}, bf16[96,2048]{1,0:T(8,128)(2,1)}, u32[]{:S(2)}, u32[]{:S(2)}) %collective-permute-start.9) | collective-permute-done | bytes 393248 | tf_op jit(solution)/shard_map/ppermute | solution.py:23
  170.8 12.9 %collective-permute-done.18 = bf16[96,2048]{1,0:T(8,128)(2,1)S(1)} collective-permute-done((bf16[96,2048]{1,0:T(8,128)(2,1)S(1)}, bf16[96,2048]{1,0:T(8,128)(2,1)S(1)}, u32[]{:S(2)}, u32[]{:S(2)}) %collective-permute-start.18) | collective-permute-done | bytes 393248 | tf_op jit(solution)/shard_map/ppermute | solution.py:23
  186.3 12.9 %collective-permute-done.19 = bf16[96,2048]{1,0:T(8,128)(2,1)S(1)} collective-permute-done((bf16[96,2048]{1,0:T(8,128)(2,1)S(1)}, bf16[96,2048]{1,0:T(8,128)(2,1)S(1)}, u32[]{:S(2)}, u32[]{:S(2)}) %collective-permute-start.19) | collective-permute-done | bytes 393248 | tf_op jit(solution)/shard_map/ppermute | solution.py:23
  201.3 12.0 %collective-permute-done.22 = bf16[96,2048]{1,0:T(8,128)(2,1)S(1)} collective-permute-done((bf16[96,2048]{1,0:T(8,128)(2,1)S(1)}, bf16[96,2048]{1,0:T(8,128)(2,1)S(1)}, u32[]{:S(2)}, u32[]{:S(2)}) %collective-permute-start.22) | collective-permute-done | bytes 393248 | tf_op jit(solution)/shard_map/ppermute | solution.py:23
  218.9 8.9 %collective-permute-done.23 = bf16[48,2048]{1,0:T(8,128)(2,1)S(1)} collective-permute-done((bf16[48,2048]{1,0:T(8,128)(2,1)S(1)}, bf16[48,2048]{1,0:T(8,128)(2,1)S(1)}, u32[]{:S(2)}, u32[]{:S(2)}) %collective-permute-start.23) | collective-permute-done | bytes 196640 | tf_op jit(solution)/shard_map/ppermute | solution.py:23
  260.9 11.4 %collective-permute-done.30 = bf16[96,2048]{1,0:T(8,128)(2,1)S(1)} collective-permute-done((bf16[96,2048]{1,0:T(8,128)(2,1)S(1)}, bf16[96,2048]{1,0:T(8,128)(2,1)S(1)}, u32[]{:S(2)}, u32[]{:S(2)}) %collective-permute-start.30) | collective-permute-done | bytes 393248 | tf_op jit(solution)/shard_map/ppermute | solution.py:23
  273.3 11.8 %collective-permute-done.31 = bf16[96,2048]{1,0:T(8,128)(2,1)S(1)} collective-permute-done((bf16[96,2048]{1,0:T(8,128)(2,1)S(1)}, bf16[96,2048]{1,0:T(8,128)(2,1)S(1)}, u32[]{:S(2)}, u32[]{:S(2)}) %collective-permute-start.31) | collective-permute-done | bytes 393248 | tf_op jit(solution)/shard_map/ppermute | solution.py:23
  286.8 10.9 %collective-permute-done.32 = bf16[96,2048]{1,0:T(8,128)(2,1)S(1)} collective-permute-done((bf16[96,2048]{1,0:T(8,128)(2,1)S(1)}, bf16[96,2048]{1,0:T(8,128)(2,1)S(1)}, u32[]{:S(2)}, u32[]{:S(2)}) %collective-permute-start.32) | collective-permute-done | bytes 393248 | tf_op jit(solution)/shard_map/ppermute | solution.py:23
  356.8 12.9 %collective-permute-done.39 = bf16[96,2048]{1,0:T(8,128)(2,1)S(1)} collective-permute-done((bf16[96,2048]{1,0:T(8,128)(2,1)S(1)}, bf16[96,2048]{1,0:T(8,128)(2,1)S(1)}, u32[]{:S(2)}, u32[]{:S(2)}) %collective-permute-start.39) | collective-permute-done | bytes 393248 | tf_op jit(solution)/shard_map/ppermute | solution.py:23
  379.0 9.0 %shard_map.205 = bf16[1024,2816]{1,0:T(8,128)(2,1)} custom-call(s32[1]{0:T(128)} %bitcast.26._, bf16[384,2048]{1,0:T(8,128)(2,1)} %constant_dynamic-update-slice_fusion.20.refs_0_, bf16[384,1024]{1,0:T(8,128)(2,1)S(1)} %copy-done.20, bf16[384,2816]{1,0:T(8,128)(2,1)S(1)} %copy-done.4, bf16[384,2816]{1,0:T(8,128)(2,1)S(1)} %copy-done.8), custom_call_target="tpu_custom_call" | custom-call | bytes 28160000 | tf_op jit(solution)/shard_map/pallas_call | solution.py:346
  389.5 12.0 %collective-permute-done.45 = bf16[96,2048]{1,0:T(8,128)(2,1)S(1)} collective-permute-done((bf16[96,2048]{1,0:T(8,128)(2,1)S(1)}, bf16[96,2048]{1,0:T(8,128)(2,1)S(1)}, u32[]{:S(2)}, u32[]{:S(2)}) %collective-permute-start.45) | collective-permute-done | bytes 393248 | tf_op jit(solution)/shard_map/ppermute | solution.py:23
  469.4 9.9 %collective-permute-done.54 = bf16[96,2048]{1,0:T(8,128)(2,1)S(1)} collective-permute-done((bf16[96,2048]{1,0:T(8,128)(2,1)S(1)}, bf16[96,2048]{1,0:T(8,128)(2,1)S(1)}, u32[]{:S(2)}, u32[]{:S(2)}) %collective-permute-start.54) | collective-permute-done | bytes 393248 | tf_op jit(solution)/shard_map/ppermute | solution.py:23
  480.5 11.6 %collective-permute-done.55 = bf16[96,2048]{1,0:T(8,128)(2,1)} collective-permute-done((bf16[96,2048]{1,0:T(8,128)(2,1)S(1)}, bf16[96,2048]{1,0:T(8,128)(2,1)}, u32[]{:S(2)}, u32[]{:S(2)}) %collective-permute-start.55) | collective-permute-done | bytes 393248 | tf_op jit(solution)/shard_map/ppermute | solution.py:23
  496.1 10.6 %collective-permute-done.56 = bf16[96,2048]{1,0:T(8,128)(2,1)} collective-permute-done((bf16[96,2048]{1,0:T(8,128)(2,1)S(1)}, bf16[96,2048]{1,0:T(8,128)(2,1)}, u32[]{:S(2)}, u32[]{:S(2)}) %collective-permute-start.56) | collective-permute-done | bytes 393248 | tf_op jit(solution)/shard_map/ppermute | solution.py:23
  506.8 9.8 %collective-permute-done.57 = bf16[96,2048]{1,0:T(8,128)(2,1)} collective-permute-done((bf16[96,2048]{1,0:T(8,128)(2,1)}, bf16[96,2048]{1,0:T(8,128)(2,1)}, u32[]{:S(2)}, u32[]{:S(2)}) %collective-permute-start.57) | collective-permute-done | bytes 393248 | tf_op jit(solution)/shard_map/ppermute | solution.py:23
  554.0 12.5 %shard_map.209 = bf16[1024,4224]{1,0:T(8,128)(2,1)} custom-call(s32[1]{0:T(128)} %bitcast.26._, bf16[384,2048]{1,0:T(8,128)(2,1)} %constant_dynamic-update-slice_fusion.2.refs_0_, bf16[384,1024]{1,0:T(8,128)(2,1)S(1)} %copy-done.16, bf16[384,2816]{1,0:T(8,128)(2,1)S(1)} %pad_maximum_fusion.2.refs_2_, bf16[384,2816]{1,0:T(8,128)(2,1)S(1)} %collective-permute-done.61.refs_3_, ...), custom_call_target="tpu_custom_call" | custom-call | bytes 42240000 | tf_op jit(solution)/shard_map/pallas_call | solution.py:346
  569.0 12.5 %collective-permute-done.64 = bf16[96,2048]{1,0:T(8,128)(2,1)} collective-permute-done((bf16[96,2048]{1,0:T(8,128)(2,1)}, bf16[96,2048]{1,0:T(8,128)(2,1)}, u32[]{:S(2)}, u32[]{:S(2)}) %collective-permute-start.64) | collective-permute-done | bytes 393248 | tf_op jit(solution)/shard_map/ppermute | solution.py:23
  584.3 9.9 %collective-permute-done.65 = bf16[96,2048]{1,0:T(8,128)(2,1)S(1)} collective-permute-done((bf16[96,2048]{1,0:T(8,128)(2,1)S(1)}, bf16[96,2048]{1,0:T(8,128)(2,1)S(1)}, u32[]{:S(2)}, u32[]{:S(2)}) %collective-permute-start.65) | collective-permute-done | bytes 393248 | tf_op jit(solution)/shard_map/ppermute | solution.py:23
  609.3 13.5 %collective-permute-done.67 = bf16[96,2048]{1,0:T(8,128)(2,1)S(1)} collective-permute-done((bf16[96,2048]{1,0:T(8,128)(2,1)S(1)}, bf16[96,2048]{1,0:T(8,128)(2,1)S(1)}, u32[]{:S(2)}, u32[]{:S(2)}) %collective-permute-start.67) | collective-permute-done | bytes 393248 | tf_op jit(solution)/shard_map/ppermute | solution.py:23
  662.9 11.9 %collective-permute-done.73 = bf16[96,2048]{1,0:T(8,128)(2,1)S(1)} collective-permute-done((bf16[96,2048]{1,0:T(8,128)(2,1)S(1)}, bf16[96,2048]{1,0:T(8,128)(2,1)S(1)}, u32[]{:S(2)}, u32[]{:S(2)}) %collective-permute-start.73) | collective-permute-done | bytes 393248 | tf_op jit(solution)/shard_map/ppermute | solution.py:23
  (555 shorter events, 426.7 us)
Async XLA Ops:
  7.2 52.5 %all-gather.5.cloned.1.call-start = ((), (), s32[]{:S(2)}) async-start(), calls=%async_computation.5 | async-start | bytes 5898240 | tf_op jit(solution)/shard_map/all_gather | solution.py:472
  12.5 142.2 %all-gather.7.cloned.1.call-start = ((), (), s32[]{:S(2)}) async-start(), calls=%async_computation.6 | async-start | bytes 19464192 | tf_op jit(solution)/shard_map/all_gather | solution.py:472
  12.5 14.5 %collective-permute-start = (bf16[96,2048]{1,0:T(8,128)(2,1)S(1)}, bf16[96,2048]{1,0:T(8,128)(2,1)}, u32[]{:S(2)}, u32[]{:S(2)}) collective-permute-start(bf16[96,2048]{1,0:T(8,128)(2,1)S(1)} %select_bitcast_fusion.5), channel_id=1, source_target_pairs={{0,1},{1,2},{2,3},{3,0},{4,5},{5,6},{6,7},{7,4},{8,9},{9,10},{10,1... | collective-permute-start | bytes 1179656 | tf_op jit(solution)/shard_map/ppermute | solution.py:23
  42.9 172.7 %all-gather.9.cloned.1.call-start = ((), (), s32[]{:S(2)}) async-start(), calls=%async_computation.7 | async-start | bytes 5898240 | tf_op jit(solution)/shard_map/all_gather | solution.py:472
  84.9 13.9 %collective-permute-start.7 = (bf16[96,2048]{1,0:T(8,128)(2,1)S(1)}, bf16[96,2048]{1,0:T(8,128)(2,1)S(1)}, u32[]{:S(2)}, u32[]{:S(2)}) collective-permute-start(bf16[96,2048]{1,0:T(8,128)(2,1)S(1)} %add_convert_fusion.15), channel_id=1, source_target_pairs={{0,1},{1,2},{2,3},{3,0},{4,5},{5,6},{6,7},{7,4},{8,9},{9,10},{10,1... | collective-permute-start | bytes 1179656 | tf_op jit(solution)/shard_map/ppermute | solution.py:23
  85.0 18.2 %collective-permute-start.8 = (bf16[96,2048]{1,0:T(8,128)(2,1)S(1)}, bf16[96,2048]{1,0:T(8,128)(2,1)S(1)}, u32[]{:S(2)}, u32[]{:S(2)}) collective-permute-start(bf16[96,2048]{1,0:T(8,128)(2,1)S(1)} %collective-permute-done.5), channel_id=1, source_target_pairs={{0,1},{1,2},{2,3},{3,0},{4,5},{5,6},{6,7},{7,4},{8,9},{9,10},{10,1... | collective-permute-start | bytes 1179656 | tf_op jit(solution)/shard_map/ppermute | solution.py:23
  104.1 224.0 %all-gather.11.cloned.1.call-start = ((), (), s32[]{:S(2)}) async-start(), calls=%async_computation.8 | async-start | bytes 19464192 | tf_op jit(solution)/shard_map/all_gather | solution.py:472
  117.8 13.5 %collective-permute-start.11 = (bf16[48,2048]{1,0:T(8,128)(2,1)S(1)}, bf16[48,2048]{1,0:T(8,128)(2,1)S(1)}, u32[]{:S(2)}, u32[]{:S(2)}) collective-permute-start(bf16[48,2048]{1,0:T(8,128)(2,1)S(1)} %get-tuple-element.526), channel_id=1, source_target_pairs={{0,1},{1,2},{2,3},{3,0},{4,5},{5,6},{6,7},{7,4},{8,9},{9,10},{10,1... | collective-permute-start | bytes 589832 | tf_op jit(solution)/shard_map/ppermute | solution.py:23
  183.8 16.3 %collective-permute-start.21 = (bf16[384,1408]{1,0:T(8,128)(2,1)S(1)}, bf16[384,1408]{1,0:T(8,128)(2,1)S(1)}, u32[]{:S(2)}, u32[]{:S(2)}) collective-permute-start(bf16[384,1408]{1,0:T(8,128)(2,1)S(1)} %fusion.31.refs_6_), channel_id=1, source_target_pairs={{0,16},{16,0},{1,17},{17,1},{2,18},{18,2},{3,19},{19,3},{4,20},{20... | collective-permute-start | bytes 3244040 | tf_op jit(solution)/shard_map/ppermute | solution.py:27
  215.5 276.6 %reduce-scatter.6.cloned.1.call-start = ((), (), s32[]{:S(2)}) async-start(), calls=%async_computation.9 | async-start | bytes 7208960 | tf_op jit(solution)/shard_map/reduce_scatter | solution.py:364
  351.5 20.9 %collective-permute-start.40 = (bf16[384,2816]{1,0:T(8,128)(2,1)S(1)}, bf16[384,2816]{1,0:T(8,128)(2,1)S(1)}, u32[]{:S(2)}, u32[]{:S(2)}) collective-permute-start(bf16[384,2816]{1,0:T(8,128)(2,1)S(1)} %pad_maximum_fusion.1.refs_2_), channel_id=1, source_target_pairs={{0,16},{16,0},{1,17},{17,1},{2,18},{18,2},{3,19},{19,3},{4,20},{20... | collective-permute-start | bytes 6488072 | tf_op jit(solution)/shard_map/ppermute | solution.py:27
  351.6 19.8 %collective-permute-start.41 = (bf16[384,1408]{1,0:T(8,128)(2,1)S(1)}, bf16[384,1408]{1,0:T(8,128)(2,1)S(1)}, u32[]{:S(2)}, u32[]{:S(2)}) collective-permute-start(bf16[384,1408]{1,0:T(8,128)(2,1)S(1)} %get-tuple-element.263.refs_2_), channel_id=1, source_target_pairs={{0,16},{16,0},{1,17},{17,1},{2,18},{18,2},{3,19},{19,3},{4,20},{20... | collective-permute-start | bytes 3244040 | tf_op jit(solution)/shard_map/ppermute | solution.py:27
  354.3 15.3 %collective-permute-start.42 = (bf16[384,1024]{1,0:T(8,128)(2,1)S(1)}, bf16[384,1024]{1,0:T(8,128)(2,1)S(1)}, u32[]{:S(2)}, u32[]{:S(2)}) collective-permute-start(bf16[384,1024]{1,0:T(8,128)(2,1)S(1)} %maximum_select_fusion.2), channel_id=1, source_target_pairs={{0,16},{16,0},{1,17},{17,1},{2,18},{18,2},{3,19},{19,3},{4,20},{20... | collective-permute-start | bytes 2359304 | tf_op jit(solution)/shard_map/ppermute | solution.py:27
  356.2 14.3 %collective-permute-start.43 = (bf16[384,1024]{1,0:T(8,128)(2,1)S(1)}, bf16[384,1024]{1,0:T(8,128)(2,1)S(1)}, u32[]{:S(2)}, u32[]{:S(2)}) collective-permute-start(bf16[384,1024]{1,0:T(8,128)(2,1)S(1)} %maximum_select_fusion.3), channel_id=1, source_target_pairs={{0,16},{16,0},{1,17},{17,1},{2,18},{18,2},{3,19},{19,3},{4,20},{20... | collective-permute-start | bytes 2359304 | tf_op jit(solution)/shard_map/ppermute | solution.py:27
  388.0 118.8 %reduce-scatter.8.cloned.1.call-start = ((), (), s32[]{:S(2)}) async-start(), calls=%async_computation.10 | async-start | bytes 3604480 | tf_op jit(solution)/shard_map/reduce_scatter | solution.py:364
  407.4 43.3 %collective-permute-start.49 = (bf16[384,1024]{1,0:T(8,128)(2,1)}, bf16[384,1024]{1,0:T(8,128)(2,1)}, u32[]{:S(2)}, u32[]{:S(2)}) collective-permute-start(bf16[384,1024]{1,0:T(8,128)(2,1)} %maximum_select_fusion.4), channel_id=1, source_target_pairs={{0,16},{16,0},{1,17},{17,1},{2,18},{18,2},{3,19},{19,3},{4,20},{20... | collective-permute-start | bytes 2359304 | tf_op jit(solution)/shard_map/ppermute | solution.py:27
  417.5 151.4 %reduce-scatter.10.cloned.1.call-start = ((), (), s32[]{:S(2)}) async-start(), calls=%async_computation.11 | async-start | bytes 2949120 | tf_op jit(solution)/shard_map/reduce_scatter | solution.py:364
  506.8 154.3 %reduce-scatter.12.cloned.1.call-start = ((), (), s32[]{:S(2)}) async-start(), calls=%async_computation.12 | async-start | bytes 10813440 | tf_op jit(solution)/shard_map/reduce_scatter | solution.py:364
  537.7 15.5 %collective-permute-start.61 = (bf16[384,2816]{1,0:T(8,128)(2,1)S(1)}, bf16[384,2816]{1,0:T(8,128)(2,1)S(1)}, u32[]{:S(2)}, u32[]{:S(2)}) collective-permute-start(bf16[384,2816]{1,0:T(8,128)(2,1)S(1)} %pad_maximum_fusion.2.refs_2_), channel_id=1, source_target_pairs={{0,16},{16,0},{1,17},{17,1},{2,18},{18,2},{3,19},{19,3},{4,20},{20... | collective-permute-start | bytes 6488072 | tf_op jit(solution)/shard_map/ppermute | solution.py:27
  539.5 13.6 %collective-permute-start.60 = (bf16[96,2048]{1,0:T(8,128)(2,1)}, bf16[96,2048]{1,0:T(8,128)(2,1)}, u32[]{:S(2)}, u32[]{:S(2)}) collective-permute-start(bf16[96,2048]{1,0:T(8,128)(2,1)} %add_convert_fusion.6), channel_id=1, source_target_pairs={{0,1},{1,2},{2,3},{3,0},{4,5},{5,6},{6,7},{7,4},{8,9},{9,10},{10,1... | collective-permute-start | bytes 1179656 | tf_op jit(solution)/shard_map/ppermute | solution.py:23
  566.9 131.2 %reduce-scatter.14.cloned.1.call-start = ((), (), s32[]{:S(2)}) async-start(), calls=%async_computation.13 | async-start | bytes 2949120 | tf_op jit(solution)/shard_map/reduce_scatter | solution.py:364
  609.0 13.8 %collective-permute-start.67 = (bf16[96,2048]{1,0:T(8,128)(2,1)S(1)}, bf16[96,2048]{1,0:T(8,128)(2,1)S(1)}, u32[]{:S(2)}, u32[]{:S(2)}) collective-permute-start(bf16[96,2048]{1,0:T(8,128)(2,1)S(1)} %collective-permute-done.66), channel_id=1, source_target_pairs={{0,1},{1,2},{2,3},{3,0},{4,5},{5,6},{6,7},{7,4},{8,9},{9,10},{10,1... | collective-permute-start | bytes 1179656 | tf_op jit(solution)/shard_map/ppermute | solution.py:23
  609.0 18.0 %collective-permute-start.68 = (bf16[96,2048]{1,0:T(8,128)(2,1)S(1)}, bf16[96,2048]{1,0:T(8,128)(2,1)S(1)}, u32[]{:S(2)}, u32[]{:S(2)}) collective-permute-start(bf16[96,2048]{1,0:T(8,128)(2,1)S(1)} %add_convert_fusion.3), channel_id=1, source_target_pairs={{0,1},{1,2},{2,3},{3,0},{4,5},{5,6},{6,7},{7,4},{8,9},{9,10},{10,1... | collective-permute-start | bytes 1179656 | tf_op jit(solution)/shard_map/ppermute | solution.py:23
  628.9 18.7 %collective-permute-start.81 = (bf16[96,2048]{1,0:T(8,128)(2,1)S(1)}, bf16[96,2048]{1,0:T(8,128)(2,1)S(1)}, u32[]{:S(2)}, u32[]{:S(2)}) collective-permute-start(bf16[96,2048]{1,0:T(8,128)(2,1)S(1)} %get-tuple-element.426), channel_id=1, source_target_pairs={{0,16},{16,0},{1,17},{17,1},{2,18},{18,2},{3,19},{19,3},{4,20},{20... | collective-permute-start | bytes 1179656 | tf_op jit(solution)/shard_map/ppermute | solution.py:27
  (164 other events, 1433.9 us)
Sparse Core Ops, SparseCore 0:
  12.6 44.6 all-gather.4
  59.8 93.3 all-gather.6
  155.7 40.7 all-gather.8
  215.7 89.8 all-gather.10
  388.1 66.8 reduce-scatter.5
  458.4 41.7 reduce-scatter.7
  506.9 39.0 reduce-scatter.9
  567.0 89.9 reduce-scatter.11
  661.2 36.7 reduce-scatter.13

commit v6 on v5

--- a/solution.py
+++ b/solution.py
@@ -437,7 +437,13 @@
         *(grad_attn, other_attn, mixed, other_mixed),
     )
     d_norm_one_all, *pairs = barrier(d_norm_one_all, *pairs)
-    attn_job = Job(grads, *pairs, held=reduced[:1] if last else ())
+    matrices = []
+
+    def last_grads(*given):
+        matrices.extend(grads(*given))
+        return ()
+
+    attn_job = Job(last_grads if last else grads, *pairs, held=reduced[:1] if last else ())
     attn_gain_job = Job(
         lambda d_all, normed: (
             jnp.sum(d_all.astype(F32) * (normed.astype(F32) / norm_gain), axis=0),
@@ -448,10 +454,10 @@
     last_job = Job(lambda: (), held=() if last else reduced[:1])
     d_norm_one = collect(d_norm_one_all, (attn_job, attn_gain_job, last_job))
     reduced[:1] = attn_job.held or last_job.held
-    g_attn = attn_job[0]
+    r_attn = scatter(matrices[0] if last else attn_job[0])
     d_input = d_middle + norm_back(layer_in, normalizer(layer_in), norm_gain, d_norm_one)
     gain_grads = jnp.stack([attn_gain_job[0], ffn_gain_job[0]])
-    return (d_input.astype(BF16), (scatter(g_attn), *reduced), gain_grads, early, aside)
+    return (d_input.astype(BF16), (r_attn, *reduced), gain_grads, early, aside)
 
 
 def both_layers(own, at_first):

time: 725 us -> 725 us (level)
  no operation moved by 1% of the time
where the time goes in v6:
time: 725 us; the launch traced here: 716 us
  waiting for transfers between devices  415 us (57%)
  matrix products  78.1 us (11%)
  other arithmetic  74.2 us (10%)
  Pallas kernels  58.2 us (8%)
  local copies, waits for them, and re-layouts  52.5 us (7%)
  starting transfers between devices  21.2 us (3%)
  between operations  16.5 us (2%)
    ppermute x63, waiting for transfers between devices, turn(): lax.ppermute(value, axis, [(i, (i + steps) % count) for i in range(count)])  405 us
    dot_general x8, matrix products, contract(): lax.dot_general(left, right, (((left_dim,), (right_dim,)), ((), ())), pre...  37.9 us
    pallas_call x5, Pallas kernels, weight_grads(): pl.pallas_call(weight_grads_kernel, grid_spec=pltpu.PrefetchScalarGridSpe...  37.9 us
    unnamed x215, local copies, waits for them, and re-layouts  35.9 us
    dot_general x2, matrix products, feed(): jnp.dot(normed_two, w_ffn[:, :2 * units], preferred_element_type=F32)  16.7 us
    ppermute x63, starting transfers between devices, turn(): lax.ppermute(value, axis, [(i, (i + steps) % count) for i in range(count)])  15.7 us
  transfers between devices with their start and end apart: 95, of which 64 were waited for; matrix products, arithmetic and copies ran while one was open for 21% of the time, Pallas kernels for 8%

profile of v6, /device:TPU:0, one launch (start us, length us, event | category | flops | bytes accessed | tf_op | source)
XLA Modules:
  0.0 715.7 jit_solution(10413371736330463456)
XLA Ops:
  16.3 10.7 %collective-permute-done = bf16[96,2048]{1,0:T(8,128)(2,1)} collective-permute-done((bf16[96,2048]{1,0:T(8,128)(2,1)S(1)}, bf16[96,2048]{1,0:T(8,128)(2,1)}, u32[]{:S(2)}, u32[]{:S(2)}) %collective-permute-start) | collective-permute-done | bytes 393248 | tf_op jit(solution)/shard_map/ppermute | solution.py:23
  46.7 11.4 %collective-permute-done.3 = bf16[96,2048]{1,0:T(8,128)(2,1)S(1)} collective-permute-done((bf16[96,2048]{1,0:T(8,128)(2,1)S(1)}, bf16[96,2048]{1,0:T(8,128)(2,1)S(1)}, u32[]{:S(2)}, u32[]{:S(2)}) %collective-permute-start.3) | collective-permute-done | bytes 393248 | tf_op jit(solution)/shard_map/ppermute | solution.py:23
  74.2 10.6 %collective-permute-done.6 = bf16[96,2048]{1,0:T(8,128)(2,1)S(1)} collective-permute-done((bf16[96,2048]{1,0:T(8,128)(2,1)S(1)}, bf16[96,2048]{1,0:T(8,128)(2,1)S(1)}, u32[]{:S(2)}, u32[]{:S(2)}) %collective-permute-start.6) | collective-permute-done | bytes 393248 | tf_op jit(solution)/shard_map/ppermute | solution.py:23
  86.0 12.8 %collective-permute-done.7 = bf16[96,2048]{1,0:T(8,128)(2,1)S(1)} collective-permute-done((bf16[96,2048]{1,0:T(8,128)(2,1)S(1)}, bf16[96,2048]{1,0:T(8,128)(2,1)S(1)}, u32[]{:S(2)}, u32[]{:S(2)}) %collective-permute-start.7) | collective-permute-done | bytes 393248 | tf_op jit(solution)/shard_map/ppermute | solution.py:23
  104.1 9.8 %collective-permute-done.9 = bf16[96,2048]{1,0:T(8,128)(2,1)} collective-permute-done((bf16[96,2048]{1,0:T(8,128)(2,1)}, bf16[96,2048]{1,0:T(8,128)(2,1)}, u32[]{:S(2)}, u32[]{:S(2)}) %collective-permute-start.9) | collective-permute-done | bytes 393248 | tf_op jit(solution)/shard_map/ppermute | solution.py:23
  170.8 12.9 %collective-permute-done.18 = bf16[96,2048]{1,0:T(8,128)(2,1)S(1)} collective-permute-done((bf16[96,2048]{1,0:T(8,128)(2,1)S(1)}, bf16[96,2048]{1,0:T(8,128)(2,1)S(1)}, u32[]{:S(2)}, u32[]{:S(2)}) %collective-permute-start.18) | collective-permute-done | bytes 393248 | tf_op jit(solution)/shard_map/ppermute | solution.py:23
  186.3 12.9 %collective-permute-done.19 = bf16[96,2048]{1,0:T(8,128)(2,1)S(1)} collective-permute-done((bf16[96,2048]{1,0:T(8,128)(2,1)S(1)}, bf16[96,2048]{1,0:T(8,128)(2,1)S(1)}, u32[]{:S(2)}, u32[]{:S(2)}) %collective-permute-start.19) | collective-permute-done | bytes 393248 | tf_op jit(solution)/shard_map/ppermute | solution.py:23
  201.3 12.0 %collective-permute-done.22 = bf16[96,2048]{1,0:T(8,128)(2,1)S(1)} collective-permute-done((bf16[96,2048]{1,0:T(8,128)(2,1)S(1)}, bf16[96,2048]{1,0:T(8,128)(2,1)S(1)}, u32[]{:S(2)}, u32[]{:S(2)}) %collective-permute-start.22) | collective-permute-done | bytes 393248 | tf_op jit(solution)/shard_map/ppermute | solution.py:23
  218.9 8.9 %collective-permute-done.23 = bf16[48,2048]{1,0:T(8,128)(2,1)S(1)} collective-permute-done((bf16[48,2048]{1,0:T(8,128)(2,1)S(1)}, bf16[48,2048]{1,0:T(8,128)(2,1)S(1)}, u32[]{:S(2)}, u32[]{:S(2)}) %collective-permute-start.23) | collective-permute-done | bytes 196640 | tf_op jit(solution)/shard_map/ppermute | solution.py:23
  260.9 11.4 %collective-permute-done.30 = bf16[96,2048]{1,0:T(8,128)(2,1)S(1)} collective-permute-done((bf16[96,2048]{1,0:T(8,128)(2,1)S(1)}, bf16[96,2048]{1,0:T(8,128)(2,1)S(1)}, u32[]{:S(2)}, u32[]{:S(2)}) %collective-permute-start.30) | collective-permute-done | bytes 393248 | tf_op jit(solution)/shard_map/ppermute | solution.py:23
  273.3 11.8 %collective-permute-done.31 = bf16[96,2048]{1,0:T(8,128)(2,1)S(1)} collective-permute-done((bf16[96,2048]{1,0:T(8,128)(2,1)S(1)}, bf16[96,2048]{1,0:T(8,128)(2,1)S(1)}, u32[]{:S(2)}, u32[]{:S(2)}) %collective-permute-start.31) | collective-permute-done | bytes 393248 | tf_op jit(solution)/shard_map/ppermute | solution.py:23
  286.8 10.9 %collective-permute-done.32 = bf16[96,2048]{1,0:T(8,128)(2,1)S(1)} collective-permute-done((bf16[96,2048]{1,0:T(8,128)(2,1)S(1)}, bf16[96,2048]{1,0:T(8,128)(2,1)S(1)}, u32[]{:S(2)}, u32[]{:S(2)}) %collective-permute-start.32) | collective-permute-done | bytes 393248 | tf_op jit(solution)/shard_map/ppermute | solution.py:23
  356.8 12.9 %collective-permute-done.39 = bf16[96,2048]{1,0:T(8,128)(2,1)S(1)} collective-permute-done((bf16[96,2048]{1,0:T(8,128)(2,1)S(1)}, bf16[96,2048]{1,0:T(8,128)(2,1)S(1)}, u32[]{:S(2)}, u32[]{:S(2)}) %collective-permute-start.39) | collective-permute-done | bytes 393248 | tf_op jit(solution)/shard_map/ppermute | solution.py:23
  379.0 9.0 %shard_map.205 = bf16[1024,2816]{1,0:T(8,128)(2,1)} custom-call(s32[1]{0:T(128)} %bitcast._, bf16[384,2048]{1,0:T(8,128)(2,1)} %constant_dynamic-update-slice_fusion.20.refs_0_, bf16[384,1024]{1,0:T(8,128)(2,1)S(1)} %copy-done.20, bf16[384,2816]{1,0:T(8,128)(2,1)S(1)} %copy-done.4, bf16[384,2816]{1,0:T(8,128)(2,1)S(1)} %copy-done.8), custom_call_target="tpu_custom_call" | custom-call | bytes 28160000 | tf_op jit(solution)/shard_map/pallas_call | solution.py:346
  389.5 12.0 %collective-permute-done.45 = bf16[96,2048]{1,0:T(8,128)(2,1)S(1)} collective-permute-done((bf16[96,2048]{1,0:T(8,128)(2,1)S(1)}, bf16[96,2048]{1,0:T(8,128)(2,1)S(1)}, u32[]{:S(2)}, u32[]{:S(2)}) %collective-permute-start.45) | collective-permute-done | bytes 393248 | tf_op jit(solution)/shard_map/ppermute | solution.py:23
  469.4 9.9 %collective-permute-done.54 = bf16[96,2048]{1,0:T(8,128)(2,1)S(1)} collective-permute-done((bf16[96,2048]{1,0:T(8,128)(2,1)S(1)}, bf16[96,2048]{1,0:T(8,128)(2,1)S(1)}, u32[]{:S(2)}, u32[]{:S(2)}) %collective-permute-start.54) | collective-permute-done | bytes 393248 | tf_op jit(solution)/shard_map/ppermute | solution.py:23
  480.5 11.6 %collective-permute-done.55 = bf16[96,2048]{1,0:T(8,128)(2,1)} collective-permute-done((bf16[96,2048]{1,0:T(8,128)(2,1)S(1)}, bf16[96,2048]{1,0:T(8,128)(2,1)}, u32[]{:S(2)}, u32[]{:S(2)}) %collective-permute-start.55) | collective-permute-done | bytes 393248 | tf_op jit(solution)/shard_map/ppermute | solution.py:23
  496.1 10.6 %collective-permute-done.56 = bf16[96,2048]{1,0:T(8,128)(2,1)} collective-permute-done((bf16[96,2048]{1,0:T(8,128)(2,1)S(1)}, bf16[96,2048]{1,0:T(8,128)(2,1)}, u32[]{:S(2)}, u32[]{:S(2)}) %collective-permute-start.56) | collective-permute-done | bytes 393248 | tf_op jit(solution)/shard_map/ppermute | solution.py:23
  506.8 9.8 %collective-permute-done.57 = bf16[96,2048]{1,0:T(8,128)(2,1)} collective-permute-done((bf16[96,2048]{1,0:T(8,128)(2,1)}, bf16[96,2048]{1,0:T(8,128)(2,1)}, u32[]{:S(2)}, u32[]{:S(2)}) %collective-permute-start.57) | collective-permute-done | bytes 393248 | tf_op jit(solution)/shard_map/ppermute | solution.py:23
  554.0 12.5 %shard_map.209 = bf16[1024,4224]{1,0:T(8,128)(2,1)} custom-call(s32[1]{0:T(128)} %bitcast._, bf16[384,2048]{1,0:T(8,128)(2,1)} %constant_dynamic-update-slice_fusion.2.refs_0_, bf16[384,1024]{1,0:T(8,128)(2,1)S(1)} %copy-done.16, bf16[384,2816]{1,0:T(8,128)(2,1)S(1)} %pad_maximum_fusion.2.refs_2_, bf16[384,2816]{1,0:T(8,128)(2,1)S(1)} %collective-permute-done.61.refs_3_, ...), custom_call_target="tpu_custom_call" | custom-call | bytes 42240000 | tf_op jit(solution)/shard_map/pallas_call | solution.py:346
  569.0 12.5 %collective-permute-done.64 = bf16[96,2048]{1,0:T(8,128)(2,1)} collective-permute-done((bf16[96,2048]{1,0:T(8,128)(2,1)}, bf16[96,2048]{1,0:T(8,128)(2,1)}, u32[]{:S(2)}, u32[]{:S(2)}) %collective-permute-start.64) | collective-permute-done | bytes 393248 | tf_op jit(solution)/shard_map/ppermute | solution.py:23
  584.3 9.9 %collective-permute-done.65 = bf16[96,2048]{1,0:T(8,128)(2,1)S(1)} collective-permute-done((bf16[96,2048]{1,0:T(8,128)(2,1)S(1)}, bf16[96,2048]{1,0:T(8,128)(2,1)S(1)}, u32[]{:S(2)}, u32[]{:S(2)}) %collective-permute-start.65) | collective-permute-done | bytes 393248 | tf_op jit(solution)/shard_map/ppermute | solution.py:23
  609.3 13.5 %collective-permute-done.67 = bf16[96,2048]{1,0:T(8,128)(2,1)S(1)} collective-permute-done((bf16[96,2048]{1,0:T(8,128)(2,1)S(1)}, bf16[96,2048]{1,0:T(8,128)(2,1)S(1)}, u32[]{:S(2)}, u32[]{:S(2)}) %collective-permute-start.67) | collective-permute-done | bytes 393248 | tf_op jit(solution)/shard_map/ppermute | solution.py:23
  662.9 11.9 %collective-permute-done.73 = bf16[96,2048]{1,0:T(8,128)(2,1)S(1)} collective-permute-done((bf16[96,2048]{1,0:T(8,128)(2,1)S(1)}, bf16[96,2048]{1,0:T(8,128)(2,1)S(1)}, u32[]{:S(2)}, u32[]{:S(2)}) %collective-permute-start.73) | collective-permute-done | bytes 393248 | tf_op jit(solution)/shard_map/ppermute | solution.py:23
  (555 shorter events, 426.7 us)
Async XLA Ops:
  7.2 52.5 %all-gather.5.cloned.1.call-start = ((), (), s32[]{:S(2)}) async-start(), calls=%async_computation.5 | async-start | bytes 5898240 | tf_op jit(solution)/shard_map/all_gather | solution.py:478
  12.5 142.2 %all-gather.7.cloned.1.call-start = ((), (), s32[]{:S(2)}) async-start(), calls=%async_computation.6 | async-start | bytes 19464192 | tf_op jit(solution)/shard_map/all_gather | solution.py:478
  12.5 14.5 %collective-permute-start = (bf16[96,2048]{1,0:T(8,128)(2,1)S(1)}, bf16[96,2048]{1,0:T(8,128)(2,1)}, u32[]{:S(2)}, u32[]{:S(2)}) collective-permute-start(bf16[96,2048]{1,0:T(8,128)(2,1)S(1)} %select_bitcast_fusion.5), channel_id=1, source_target_pairs={{0,1},{1,2},{2,3},{3,0},{4,5},{5,6},{6,7},{7,4},{8,9},{9,10},{10,1... | collective-permute-start | bytes 1179656 | tf_op jit(solution)/shard_map/ppermute | solution.py:23
  42.9 172.7 %all-gather.9.cloned.1.call-start = ((), (), s32[]{:S(2)}) async-start(), calls=%async_computation.7 | async-start | bytes 5898240 | tf_op jit(solution)/shard_map/all_gather | solution.py:478
  84.9 13.9 %collective-permute-start.7 = (bf16[96,2048]{1,0:T(8,128)(2,1)S(1)}, bf16[96,2048]{1,0:T(8,128)(2,1)S(1)}, u32[]{:S(2)}, u32[]{:S(2)}) collective-permute-start(bf16[96,2048]{1,0:T(8,128)(2,1)S(1)} %add_convert_fusion.15), channel_id=1, source_target_pairs={{0,1},{1,2},{2,3},{3,0},{4,5},{5,6},{6,7},{7,4},{8,9},{9,10},{10,1... | collective-permute-start | bytes 1179656 | tf_op jit(solution)/shard_map/ppermute | solution.py:23
  85.0 18.2 %collective-permute-start.8 = (bf16[96,2048]{1,0:T(8,128)(2,1)S(1)}, bf16[96,2048]{1,0:T(8,128)(2,1)S(1)}, u32[]{:S(2)}, u32[]{:S(2)}) collective-permute-start(bf16[96,2048]{1,0:T(8,128)(2,1)S(1)} %collective-permute-done.5), channel_id=1, source_target_pairs={{0,1},{1,2},{2,3},{3,0},{4,5},{5,6},{6,7},{7,4},{8,9},{9,10},{10,1... | collective-permute-start | bytes 1179656 | tf_op jit(solution)/shard_map/ppermute | solution.py:23
  104.1 224.0 %all-gather.11.cloned.1.call-start = ((), (), s32[]{:S(2)}) async-start(), calls=%async_computation.8 | async-start | bytes 19464192 | tf_op jit(solution)/shard_map/all_gather | solution.py:478
  117.8 13.5 %collective-permute-start.11 = (bf16[48,2048]{1,0:T(8,128)(2,1)S(1)}, bf16[48,2048]{1,0:T(8,128)(2,1)S(1)}, u32[]{:S(2)}, u32[]{:S(2)}) collective-permute-start(bf16[48,2048]{1,0:T(8,128)(2,1)S(1)} %get-tuple-element.524), channel_id=1, source_target_pairs={{0,1},{1,2},{2,3},{3,0},{4,5},{5,6},{6,7},{7,4},{8,9},{9,10},{10,1... | collective-permute-start | bytes 589832 | tf_op jit(solution)/shard_map/ppermute | solution.py:23
  183.8 16.3 %collective-permute-start.21 = (bf16[384,1408]{1,0:T(8,128)(2,1)S(1)}, bf16[384,1408]{1,0:T(8,128)(2,1)S(1)}, u32[]{:S(2)}, u32[]{:S(2)}) collective-permute-start(bf16[384,1408]{1,0:T(8,128)(2,1)S(1)} %fusion.31.refs_6_), channel_id=1, source_target_pairs={{0,16},{16,0},{1,17},{17,1},{2,18},{18,2},{3,19},{19,3},{4,20},{20... | collective-permute-start | bytes 3244040 | tf_op jit(solution)/shard_map/ppermute | solution.py:27
  215.5 276.6 %reduce-scatter.6.cloned.1.call-start = ((), (), s32[]{:S(2)}) async-start(), calls=%async_computation.9 | async-start | bytes 7208960 | tf_op jit(solution)/shard_map/reduce_scatter | solution.py:364
  351.5 20.9 %collective-permute-start.40 = (bf16[384,2816]{1,0:T(8,128)(2,1)S(1)}, bf16[384,2816]{1,0:T(8,128)(2,1)S(1)}, u32[]{:S(2)}, u32[]{:S(2)}) collective-permute-start(bf16[384,2816]{1,0:T(8,128)(2,1)S(1)} %pad_maximum_fusion.1.refs_2_), channel_id=1, source_target_pairs={{0,16},{16,0},{1,17},{17,1},{2,18},{18,2},{3,19},{19,3},{4,20},{20... | collective-permute-start | bytes 6488072 | tf_op jit(solution)/shard_map/ppermute | solution.py:27
  351.6 19.8 %collective-permute-start.41 = (bf16[384,1408]{1,0:T(8,128)(2,1)S(1)}, bf16[384,1408]{1,0:T(8,128)(2,1)S(1)}, u32[]{:S(2)}, u32[]{:S(2)}) collective-permute-start(bf16[384,1408]{1,0:T(8,128)(2,1)S(1)} %get-tuple-element.262.refs_2_), channel_id=1, source_target_pairs={{0,16},{16,0},{1,17},{17,1},{2,18},{18,2},{3,19},{19,3},{4,20},{20... | collective-permute-start | bytes 3244040 | tf_op jit(solution)/shard_map/ppermute | solution.py:27
  354.3 15.3 %collective-permute-start.42 = (bf16[384,1024]{1,0:T(8,128)(2,1)S(1)}, bf16[384,1024]{1,0:T(8,128)(2,1)S(1)}, u32[]{:S(2)}, u32[]{:S(2)}) collective-permute-start(bf16[384,1024]{1,0:T(8,128)(2,1)S(1)} %maximum_select_fusion.2), channel_id=1, source_target_pairs={{0,16},{16,0},{1,17},{17,1},{2,18},{18,2},{3,19},{19,3},{4,20},{20... | collective-permute-start | bytes 2359304 | tf_op jit(solution)/shard_map/ppermute | solution.py:27
  356.2 14.3 %collective-permute-start.43 = (bf16[384,1024]{1,0:T(8,128)(2,1)S(1)}, bf16[384,1024]{1,0:T(8,128)(2,1)S(1)}, u32[]{:S(2)}, u32[]{:S(2)}) collective-permute-start(bf16[384,1024]{1,0:T(8,128)(2,1)S(1)} %maximum_select_fusion.3), channel_id=1, source_target_pairs={{0,16},{16,0},{1,17},{17,1},{2,18},{18,2},{3,19},{19,3},{4,20},{20... | collective-permute-start | bytes 2359304 | tf_op jit(solution)/shard_map/ppermute | solution.py:27
  388.0 118.8 %reduce-scatter.8.cloned.1.call-start = ((), (), s32[]{:S(2)}) async-start(), calls=%async_computation.10 | async-start | bytes 3604480 | tf_op jit(solution)/shard_map/reduce_scatter | solution.py:364
  407.4 43.3 %collective-permute-start.49 = (bf16[384,1024]{1,0:T(8,128)(2,1)}, bf16[384,1024]{1,0:T(8,128)(2,1)}, u32[]{:S(2)}, u32[]{:S(2)}) collective-permute-start(bf16[384,1024]{1,0:T(8,128)(2,1)} %maximum_select_fusion.4), channel_id=1, source_target_pairs={{0,16},{16,0},{1,17},{17,1},{2,18},{18,2},{3,19},{19,3},{4,20},{20... | collective-permute-start | bytes 2359304 | tf_op jit(solution)/shard_map/ppermute | solution.py:27
  417.5 151.4 %reduce-scatter.10.cloned.1.call-start = ((), (), s32[]{:S(2)}) async-start(), calls=%async_computation.11 | async-start | bytes 2949120 | tf_op jit(solution)/shard_map/reduce_scatter | solution.py:364
  506.8 154.3 %reduce-scatter.14.cloned.1.call-start = ((), (), s32[]{:S(2)}) async-start(), calls=%async_computation.13 | async-start | bytes 10813440 | tf_op jit(solution)/shard_map/reduce_scatter | solution.py:364
  537.7 15.5 %collective-permute-start.61 = (bf16[384,2816]{1,0:T(8,128)(2,1)S(1)}, bf16[384,2816]{1,0:T(8,128)(2,1)S(1)}, u32[]{:S(2)}, u32[]{:S(2)}) collective-permute-start(bf16[384,2816]{1,0:T(8,128)(2,1)S(1)} %pad_maximum_fusion.2.refs_2_), channel_id=1, source_target_pairs={{0,16},{16,0},{1,17},{17,1},{2,18},{18,2},{3,19},{19,3},{4,20},{20... | collective-permute-start | bytes 6488072 | tf_op jit(solution)/shard_map/ppermute | solution.py:27
  539.5 13.6 %collective-permute-start.60 = (bf16[96,2048]{1,0:T(8,128)(2,1)}, bf16[96,2048]{1,0:T(8,128)(2,1)}, u32[]{:S(2)}, u32[]{:S(2)}) collective-permute-start(bf16[96,2048]{1,0:T(8,128)(2,1)} %add_convert_fusion.6), channel_id=1, source_target_pairs={{0,1},{1,2},{2,3},{3,0},{4,5},{5,6},{6,7},{7,4},{8,9},{9,10},{10,1... | collective-permute-start | bytes 1179656 | tf_op jit(solution)/shard_map/ppermute | solution.py:23
  566.9 131.2 %reduce-scatter.12.cloned.1.call-start = ((), (), s32[]{:S(2)}) async-start(), calls=%async_computation.12 | async-start | bytes 2949120 | tf_op jit(solution)/shard_map/reduce_scatter | solution.py:364
  609.0 13.8 %collective-permute-start.67 = (bf16[96,2048]{1,0:T(8,128)(2,1)S(1)}, bf16[96,2048]{1,0:T(8,128)(2,1)S(1)}, u32[]{:S(2)}, u32[]{:S(2)}) collective-permute-start(bf16[96,2048]{1,0:T(8,128)(2,1)S(1)} %collective-permute-done.66), channel_id=1, source_target_pairs={{0,1},{1,2},{2,3},{3,0},{4,5},{5,6},{6,7},{7,4},{8,9},{9,10},{10,1... | collective-permute-start | bytes 1179656 | tf_op jit(solution)/shard_map/ppermute | solution.py:23
  609.0 18.0 %collective-permute-start.68 = (bf16[96,2048]{1,0:T(8,128)(2,1)S(1)}, bf16[96,2048]{1,0:T(8,128)(2,1)S(1)}, u32[]{:S(2)}, u32[]{:S(2)}) collective-permute-start(bf16[96,2048]{1,0:T(8,128)(2,1)S(1)} %add_convert_fusion.3), channel_id=1, source_target_pairs={{0,1},{1,2},{2,3},{3,0},{4,5},{5,6},{6,7},{7,4},{8,9},{9,10},{10,1... | collective-permute-start | bytes 1179656 | tf_op jit(solution)/shard_map/ppermute | solution.py:23
  628.9 18.7 %collective-permute-start.81 = (bf16[96,2048]{1,0:T(8,128)(2,1)S(1)}, bf16[96,2048]{1,0:T(8,128)(2,1)S(1)}, u32[]{:S(2)}, u32[]{:S(2)}) collective-permute-start(bf16[96,2048]{1,0:T(8,128)(2,1)S(1)} %get-tuple-element.424), channel_id=1, source_target_pairs={{0,16},{16,0},{1,17},{17,1},{2,18},{18,2},{3,19},{19,3},{4,20},{20... | collective-permute-start | bytes 1179656 | tf_op jit(solution)/shard_map/ppermute | solution.py:27
  (164 other events, 1433.9 us)
Sparse Core Ops, SparseCore 0:
  12.6 44.6 all-gather.4
  59.8 93.3 all-gather.6
  155.7 40.7 all-gather.8
  215.7 89.8 all-gather.10
  388.1 66.8 reduce-scatter.5
  458.4 41.7 reduce-scatter.7
  506.9 39.0 reduce-scatter.9
  567.0 89.9 reduce-scatter.13
  660.6 37.4 reduce-scatter.11
